TPU v7x, 32 devices: a whole 2x2x4 slice. The times are simulated.
32 devices in a mesh: seq: 16 (over z, y, x), ffn: 2 (over core).
Axes of the slice: x: 2, y: 2, z: 4, core: 2. Of those that a mesh axis runs over, the one named last changes fastest.
Arguments:
- x_long: bfloat16 [2, 4096, 768], P(None, ('seq', 'ffn')), may hold values from -6 to 6
- x_glob: bfloat16 [2, 64, 768], P(None, ('seq', 'ffn')), may hold values from -6 to 6
- sentence: int32 [2, 16, 256], P(None, 'seq'), may hold values from 0 to 3, never falling along the last dimension, each value on 1 to 96 neighbouring positions
- dy_long: bfloat16 [2, 4096, 768], P(None, ('seq', 'ffn')), may hold values from -6 to 6
- dy_glob: bfloat16 [2, 64, 768], P(None, ('seq', 'ffn')), may hold values from -6 to 6
- owner_list: int32 [224], replicated, may hold values from 0 to 223, as said below
- w_master: float32 [448, 128, 128], P(('seq', 'ffn')), may hold values from -0.57735027 to 0.57735027
- m_old: float32 [448, 128, 128], P(('seq', 'ffn')), may hold values from -20.249516 to 20.249516
- v_old: float32 [448, 128, 128], P(('seq', 'ffn')), may hold values from 4.37632 to 437.632, as said below
- left_basis: float32 [448, 128, 128], P(('seq', 'ffn')), may hold values from -1 to 1, as said below
- right_basis: float32 [448, 128, 128], P(('seq', 'ffn')), may hold values from -1 to 1, as said below
- left_stats: float32 [448, 128, 128], P(('seq', 'ffn')), may hold values from 0 to 1064960, as said below
- right_stats: float32 [448, 128, 128], P(('seq', 'ffn')), may hold values from 0 to 1064960, as said below
- rel_table: float32 [169, 768], P(None, 'ffn'), may hold values from -6 to 6
- rel_m: float32 [169, 768], P(None, 'ffn'), may hold values from -3 to 3
- rel_v: float32 [169, 768], P(None, 'ffn'), may hold values from 0.17472 to 0.69888
- norm_params: float32 [4, 768], replicated, may hold values from -0.8 to 1.3
- norm_m: float32 [4, 768], replicated, may hold values from -64 to 64
- norm_v: float32 [4, 768], replicated, may hold values from 437.632 to 1747.2
Outputs:
- y_long: bfloat16 [2, 4096, 768], P(None, ('seq', 'ffn'))
- y_glob: bfloat16 [2, 64, 768], P(None, ('seq', 'ffn'))
- dx_long: float32 [2, 4096, 768], P(None, ('seq', 'ffn'))
- dx_glob: float32 [2, 64, 768], P(None, ('seq', 'ffn'))
- w_new: float32 [448, 128, 128], P(('seq', 'ffn'))
- m_new: float32 [448, 128, 128], P(('seq', 'ffn'))
- v_new: float32 [448, 128, 128], P(('seq', 'ffn'))
- left_basis_new: float32 [448, 128, 128], P(('seq', 'ffn'))
- right_basis_new: float32 [448, 128, 128], P(('seq', 'ffn'))
- left_stats_new: float32 [448, 128, 128], P(('seq', 'ffn'))
- right_stats_new: float32 [448, 128, 128], P(('seq', 'ffn'))
- rel_new: float32 [169, 768], P(None, 'ffn')
- rel_m_new: float32 [169, 768], P(None, 'ffn')
- rel_v_new: float32 [169, 768], P(None, 'ffn')
- norm_new: float32 [4, 768], replicated
- norm_m_new: float32 [4, 768], replicated
- norm_v_new: float32 [4, 768], replicated
Inputs may be any that keep to these rules, and one draw needn't show every extreme that they name: For each sequence s and block b, sentence[s, b, t] never falls along t, every value is used, and no value covers more than 96 tokens. `owner_list`: all entries differ. `v_old`: positive. `left_basis`: each slot's matrix is orthogonal. `right_basis`: each slot's matrix is orthogonal. `left_stats`: each slot's matrix is diagonal with a positive diagonal. `right_stats`: each slot's matrix is diagonal with a positive diagonal.
All inputs are finite; a program needn't handle non-finite values.
Results may differ from a plain program's by a relative error of at most 0.015.
The roundings to bfloat16 on the way count: a program that leaves them out, or rounds other values in their place, can miss the bound.
Values may be sent and summed in bfloat16 or wider, within the bound.
No kernel may reach another device: no remote copies, remote signals or barrier semaphores. Data moves between devices by JAX's collectives and lax.ppermute only.
A program may use at most 192 MiB of HBM per device.

v0:
```python
import functools
import math

import jax
import jax.numpy as jnp
from jax import lax
from jax.experimental import pallas as pl
from jax.experimental.pallas import tpu as pltpu
from jax.sharding import PartitionSpec as P

HEADS = 12
FF = 3072
RADIUS = 84
STEP = 10

BETA_ONE = 0.9
BETA_TWO = 0.95
LEARN_RATE = 0.02
ADAM_RATE = 0.6
WEIGHT_DECAY = 0.01
ADAM_EPS = 1e-08
NORM_EPS = 1e-12
NEG_FILL = -1e30
BF = jnp.bfloat16
F32 = jnp.float32


def seq_bits(count):
    return [1 << at for at in range(count.bit_length() - 1)]


def swap_with(values, bit):
    count = lax.axis_size("seq")
    return lax.ppermute(values, "seq", [(i, i ^ bit) for i in range(count)])


def slot_parts(slots, count):
    bits = seq_bits(count)
    low, high = bits[:3], bits[3:]
    cuts = [slots * at // 14 for at in (0, 5, 10, 14)]
    orders = [low[at:] + low[:at] + high for at in range(3)]
    return [(a, b, order) for a, b, order in zip(cuts, cuts[1:], orders) if b > a]


def part_rows(parts, side, extra):
    rows = [(last - first) * side for first, last, _ in parts]
    return rows[:-1] + [rows[-1] + extra]


def slot_places(owners, slots, rows, side):
    count = lax.axis_size("seq")
    apart = (owners // slots) ^ lax.axis_index("seq")
    inner = owners % slots
    place, row, base = jnp.zeros_like(owners), jnp.zeros_like(owners), 0
    for (first, last, order), many in zip(slot_parts(slots, count), rows):
        index = jnp.zeros_like(owners)
        for at, bit in enumerate(order):
            index = index + jnp.where((apart & bit) != 0, count >> (at + 1), 0)
        here = (inner >= first) & (inner < last)
        place = jnp.where(here, first * count + index * (last - first) + inner - first, place)
        row = jnp.where(here, base + index * many + (inner - first) * side, row)
        base += many * count
    return place, row


FAR_SIZE = 3 * 2**20


def move_kernel(plan, arrays, *refs):
    ins, outs, held, sems = refs[:arrays], refs[arrays : arrays + len(plan)], refs[arrays + len(plan) : -1], refs[-1]
    copies, sums, sem = [], [], 0
    for out, runs in zip(outs, plan):
        base = 0
        for rows, *terms in runs:
            here = out.at[pl.ds(base, rows)]
            targets = [here] if len(terms) == 1 else [held[len(sums) * 2 + k] for k in range(2)]
            waits = []
            for (at, start), target in zip(terms, targets):
                waits.append(pltpu.make_async_copy(ins[at].at[pl.ds(start, rows)], target, sems.at[sem]))
                waits[-1].start()
                sem += 1
            if len(terms) == 1:
                copies += waits
            else:
                sums.append((waits, targets, out, base, rows))
            base += rows
    for waits, (one, two), out, base, rows in sums:
        for wait in waits:
            wait.wait()
        step = next(s for s in (128, 64, 48, 32, 16) if rows % s == 0)

        def add(i, carry):
            at = pl.multiple_of(i * step, 16)
            total = one[pl.ds(at, step), :].astype(F32) + two[pl.ds(at, step), :].astype(F32)
            out[pl.ds(base + at, step), :] = total.astype(BF)
            return carry

        lax.fori_loop(0, rows // step, add, 0)
    for copy in copies:
        copy.wait()


def move_rows(outputs):
    arrays, plan, scratch, count = [], [], [], 0
    for runs in outputs:
        plan.append([])
        for rows, *terms in runs:
            places = []
            for array, start in terms:
                found = [i for i, other in enumerate(arrays) if other is array]
                if not found:
                    arrays.append(array)
                places.append((found[0] if found else len(arrays) - 1, start))
                count += 1
            plan[-1].append((rows, *places))
            if len(terms) == 2:
                scratch += [pltpu.VMEM((rows, terms[0][0].shape[1]), BF)] * 2
    shapes = [(sum(run[0] for run in runs), runs[0][1][0].shape[1]) for runs in outputs]
    return pl.pallas_call(
        functools.partial(move_kernel, plan, len(arrays)),
        grid=(1,),
        out_shape=tuple(jax.ShapeDtypeStruct(shape, BF) for shape in shapes),
        in_specs=[
            pl.BlockSpec(memory_space=pltpu.HBM if array.size > FAR_SIZE else pl.ANY) for array in arrays
        ],
        out_specs=tuple(whole(shape) for shape in shapes),
        scratch_shapes=scratch + [pltpu.SemaphoreType.DMA((count,))],
        cost_estimate=pl.CostEstimate(
            flops=0, bytes_accessed=sum(6 * math.prod(s) for s in shapes), transcendentals=0
        ),
        compiler_params=pltpu.CompilerParams(vmem_limit_bytes=16 * 2**20),
        name="add_rows" if scratch else "join_rows",
    )(*arrays)


def run_sum(rows, one, one_at, two, two_at):
    return (rows, (one, one_at), (two, two_at))


def gather_rows(cells, extra, rows, orders):
    own = sum(rows)
    shared = orders[0][3:][::-1]
    got = [swap_with(values, shared[0]) for values in (cells, extra)]
    devices = [[(cells, 0), (extra, -cells.shape[0])], [(got[0], 0), (got[1], -cells.shape[0])]]
    if len(shared) > 1:
        (cells,) = move_rows([[(array.shape[0], (array, 0)) for runs in devices for array, _ in runs]])
        for bit in shared[1:-1]:
            got = swap_with(cells, bit)
            (cells,) = move_rows([[(cells.shape[0], (cells, 0)), (cells.shape[0], (got, 0))]])
        got = swap_with(cells, shared[-1])
        devices = [[(run, i * own)] for run in (cells, got) for i in range(cells.shape[0] // own)]
    starts = [sum(rows[:at]) for at in range(len(rows))]

    def runs_of(start, many):
        runs = []
        for pieces in devices:
            left, at = many, start
            for array, shift in pieces:
                here = min(left, array.shape[0] - (at + shift))
                if here > 0:
                    runs.append((here, (array, at + shift)))
                    left, at = left - here, at + here
        return runs

    parts = move_rows([runs_of(start, many) for start, many in zip(starts, rows)])
    for step in (2, 1):
        got = [swap_with(part, order[step]) for part, order in zip(parts, orders)]
        parts = move_rows([[(p.shape[0], (p, 0)), (p.shape[0], (g, 0))] for p, g in zip(parts, got)])
    got = [swap_with(part, order[0]) for part, order in zip(parts, orders)]
    return list(zip(parts, got))


def scatter_rows(cells, rows, orders, everywhere, order_everywhere, carried):
    count = lax.axis_size("seq")
    spans = [count * many for many in rows]
    starts = [sum(spans[:at]) for at in range(len(spans))]
    sends = [cells[a + r // 2 : a + r] for a, r in zip(starts, spans)]
    kept = [(cells, a, r // 2) for a, r in zip(starts, spans)]

    def all_sum():
        return [run_sum(everywhere.shape[0], everywhere, 0, all_got, 0)]

    for step in range(3):
        got = [swap_with(send, order[step]) for send, order in zip(sends, orders)]
        all_got = swap_with(everywhere, order_everywhere[step])
        halves = [r // 2 for _, _, r in kept]
        if step < 2:
            *sends, everywhere = move_rows(
                [[run_sum(h, k, a + h, g, h)] for h, (k, a, _), g in zip(halves, kept, got)] + [all_sum()]
            )
            keeps = move_rows([[run_sum(h, k, a, g, 0)] for h, (k, a, _), g in zip(halves, kept, got)])
            kept = [(keep, 0, h) for keep, h in zip(keeps, halves)]
    devices = count // 8

    def merged(at, many):
        return [
            run_sum(r, k, i * r, g, i * r)
            for i in range(at, at + many)
            for r, (k, _, _), g in zip(rows, kept, got)
        ]

    half = devices // 2
    send, everywhere, *carried = move_rows([merged(half, half), all_sum()] + carried)
    (keep,) = move_rows([merged(0, half)])
    for step, bit in enumerate(orders[0][3:]):
        got_all = swap_with(send, bit)
        all_got = swap_with(everywhere, order_everywhere[3 + step])
        if bit == orders[0][-1]:
            return (keep, got_all), (everywhere, all_got), carried
        half = keep.shape[0] // 2
        send, everywhere = move_rows([[run_sum(half, keep, half, got_all, half)], all_sum()])
        (keep,) = move_rows([[run_sum(half, keep, 0, got_all, 0)]])
    return None


def split_two(x):
    hi = x.astype(BF)
    return hi, (x - hi.astype(F32)).astype(BF)


def split_three(x):
    hi = x.astype(BF)
    rest = x - hi.astype(F32)
    mid = rest.astype(BF)
    return hi, mid, (rest - mid.astype(F32)).astype(BF)


def left_six(parts, axis):
    h, m, l = parts
    return jnp.concatenate([h, h, m, m, h, l], axis=axis)


def right_six(parts, axis):
    h, m, l = parts
    return jnp.concatenate([h, m, h, m, l, h], axis=axis)


def left_three(parts, axis):
    h, l = parts
    return jnp.concatenate([h, h, l], axis=axis)


def right_three(parts, axis):
    h, l = parts
    return jnp.concatenate([h, l, h], axis=axis)


def dot_on(a, b, ca, cb):
    return lax.dot_general(a, b, (((ca,), (cb,)), ((), ())), preferred_element_type=F32)


def dot_six(a, b, ca, cb):
    return dot_on(left_six(split_three(a), ca), right_six(split_three(b), cb), ca, cb)


def dot_three(a, b, ca, cb):
    return dot_on(left_three(split_two(a), ca), right_three(split_two(b), cb), ca, cb)


PANEL = 32


def panel_inverse(a_ref, t_ref, npad, side, at):
    groups = PANEL // 8
    iota = lax.broadcasted_iota(jnp.int32, (8, npad), 0)
    a = []
    for i in range(PANEL):
        rows = a_ref[pl.ds(at + i, npad, stride=side), :]
        cols = rows.T[at : at + PANEL]
        a.append([cols[8 * g : 8 * g + 8] for g in range(groups)])
    z = [[None] * groups for _ in range(PANEL)]
    for j in range(PANEL):
        gj, sj = divmod(j, 8)
        r = lax.rsqrt(a[j][gj][sj : sj + 1])
        u = [None if g < gj else a[j][g] * r for g in range(groups)]
        below = list(u)
        below[gj] = jnp.where(iota > sj, u[gj], 0.0)
        for k in range(j + 1, PANEL):
            gk, sk = divmod(k, 8)
            row = u[gk][sk : sk + 1]
            for g in range(gk, groups):
                a[k][g] = a[k][g] - u[g] * row
        for c in range(j):
            row = z[c][gj][sj : sj + 1] * r
            z[c][gj] = jnp.where(iota == sj, row, z[c][gj]) - below[gj] * row
            for g in range(gj + 1, groups):
                z[c][g] = z[c][g] - u[g] * row
        z[j] = [
            jnp.zeros((8, npad), F32)
            if g < gj
            else (jnp.where(iota == sj, r, 0.0) - below[g] * r if g == gj else -u[g] * r)
            for g in range(groups)
        ]
    fill = jnp.zeros((side - PANEL, npad), F32)
    for c in range(PANEL):
        t_ref[pl.ds(c, npad, stride=PANEL), :] = jnp.concatenate(z[c] + [fill], axis=0).T


def adam_step(grad, refs, outs, where, decay_rate):
    param, first_mom, second_mom = [ref[where] for ref in refs]
    first_mom = BETA_ONE * first_mom + (1.0 - BETA_ONE) * grad
    second_mom = BETA_TWO * second_mom + (1.0 - BETA_TWO) * grad * grad
    direction = (
        first_mom
        / (1.0 - BETA_ONE**STEP)
        / (jnp.sqrt(second_mom / (1.0 - BETA_TWO**STEP)) + ADAM_EPS)
    )
    outs[0][where] = param - ADAM_RATE * (direction + decay_rate * param)
    outs[1][where] = first_mom
    outs[2][where] = second_mom


def small_updates(small_refs, refs, outs):
    total = small_refs[0][...].astype(F32) + small_refs[1][...].astype(F32)
    labels, cols = refs[0].shape
    rel = pltpu.roll(total, total.shape[0] - (RIM - RADIUS), 0)[:labels]
    adam_step(rel, refs[:3], outs[:3], (slice(None), slice(None)), WEIGHT_DECAY)
    halves = refs[3].shape[1] // cols
    for row in range(refs[3].shape[0]):
        for half in range(halves):
            at = SMALL_ROWS - 8 + row * halves + half
            where = (slice(row, row + 1), slice(half * cols, (half + 1) * cols))
            adam_step(total[at : at + 1], refs[3:], outs[3:], where, 0.0)


def soap_kernel(npad, kept_ref, got_ref, small_ref, small_got_ref, *refs):
    w_ref, m_ref, v_ref, ql_ref, qr_ref, sl_ref, sr_ref = refs[:7]
    w_out, m_out, v_out, ql_out, qr_out, sl_out, sr_out = refs[13:20]
    a_ref, y_ref, mat_ref, t_ref = refs[26:]
    small_updates((small_ref, small_got_ref), refs[7:13], refs[20:26])
    n = w_ref.shape[0]
    many = next(k for k in (2, 1) if n % k == 0)
    batch = next(b for b in (14, 7, 4, 2) if 2 * n % b == 0)
    side = w_ref.shape[-1]
    eye = (
        lax.broadcasted_iota(jnp.int32, (side, side), 0)
        == lax.broadcasted_iota(jnp.int32, (side, side), 1)
    ).astype(F32)

    def first(at, carry):
        slots = [at * many + k for k in range(many)]
        tiles = [pl.ds(pl.multiple_of(i * side, side), side) for i in slots]
        grads = [kept_ref[rows, :].astype(F32) + got_ref[rows, :].astype(F32) for rows in tiles]
        lefts = [ql_ref[i] for i in slots]
        rights = [qr_ref[i] for i in slots]
        halves = [split_two(x) for x in grads]
        new_l = [
            BETA_TWO * sl_ref[i] + (1.0 - BETA_TWO) * dot_on(left_three(p, 1), right_three(p, 1), 1, 1)
            for i, p in zip(slots, halves)
        ]
        new_r = [
            BETA_TWO * sr_ref[i] + (1.0 - BETA_TWO) * dot_on(left_three(p, 0), right_three(p, 0), 0, 0)
            for i, p in zip(slots, halves)
        ]
        mats = [dot_six(x, y, 1, 0) for x, y in zip(new_l + new_r, lefts + rights)]
        thirds = [split_three(x) for x in mats]
        grams = [dot_on(left_six(p, 0), right_six(p, 0), 0, 0) for p in thirds]
        turned = [dot_three(x, y, 0, 0) for x, y in zip(lefts, grads)]
        rotated = [dot_three(x, y, 1, 0) for x, y in zip(turned, rights)]
        moms = [BETA_ONE * m_ref[i] + (1.0 - BETA_ONE) * x for i, x in zip(slots, rotated)]
        secs = [BETA_TWO * v_ref[i] + (1.0 - BETA_TWO) * x * x for i, x in zip(slots, rotated)]
        steps = [
            x / (1.0 - BETA_ONE**STEP) / (jnp.sqrt(y / (1.0 - BETA_TWO**STEP)) + ADAM_EPS)
            for x, y in zip(moms, secs)
        ]
        turned = [dot_three(x, y, 1, 0) for x, y in zip(lefts, steps)]
        backs = [dot_three(x, y, 1, 1) for x, y in zip(turned, rights)]
        weights = [w_ref[i] for i in slots]
        for k, i in enumerate(slots):
            m_out[i] = moms[k]
            v_out[i] = secs[k]
            w_out[i] = weights[k] - LEARN_RATE * (backs[k] + WEIGHT_DECAY * weights[k])
            sl_out[i] = new_l[k]
            sr_out[i] = new_r[k]
            for kind in range(2):
                mat_ref[2 * i + kind] = mats[kind * many + k]
                rows = pl.ds(pl.multiple_of((2 * i + kind) * side, side), side)
                a_ref[rows, :] = grams[kind * many + k]
                y_ref[rows, :] = eye
        return carry

    lax.fori_loop(0, n // many, first, 0)
    if npad > 2 * n:
        a_ref[2 * n * side :, :] = jnp.concatenate([eye] * (npad - 2 * n), axis=0)
    for at in range(0, side, PANEL):
        panel_inverse(a_ref, t_ref, npad, side, at)

        def update(i, carry):
            bases = [pl.multiple_of((i * batch + b) * side, side) for b in range(batch)]
            rows = [pl.ds(base + at, PANEL) for base in bases]
            both = [jnp.concatenate([a_ref[r, :], y_ref[r, :]], axis=1) for r in rows]
            turns = [
                t_ref[pl.ds(pl.multiple_of((i * batch + b) * PANEL, PANEL), PANEL), :][:, :PANEL]
                for b in range(batch)
            ]
            if at + PANEL < side:
                rest = [pl.ds(base + at + PANEL, side - at - PANEL) for base in bases]
                old = [(a_ref[r, :], y_ref[r, :]) for r in rest]
            fresh = [dot_six(t, x, 0, 0) for t, x in zip(turns, both)]
            if at + PANEL < side:
                changes = []
                for x in fresh:
                    parts = split_three(x)
                    cut = tuple(p[:, at + PANEL : side] for p in parts)
                    changes.append(dot_on(left_six(cut, 0), right_six(parts, 0), 0, 0))
                for r, (old_a, old_y), change in zip(rest, old, changes):
                    a_ref[r, :] = old_a - change[:, :side]
                    y_ref[r, :] = old_y - change[:, side:]
            for r, x in zip(rows, fresh):
                y_ref[r, :] = x[:, side:]
            return carry

        lax.fori_loop(0, 2 * n // batch, update, 0)

    def last(i, carry):
        mats = [mat_ref[2 * i], mat_ref[2 * i + 1]]
        rows = [pl.ds(pl.multiple_of((2 * i + k) * side, side), side) for k in range(2)]
        turns = [y_ref[r, :] for r in rows]
        left, right = [dot_three(x, y, 1, 1) for x, y in zip(mats, turns)]
        ql_out[i] = left
        qr_out[i] = right
        return carry

    lax.fori_loop(0, n, last, 0)


def soap_update(grads, small, state, others):
    n, side = state[0].shape[:2]
    npad = -(-2 * n // 8) * 8
    ins = [*grads, *small, *state, *others]
    outs = [*state, *others]
    return pl.pallas_call(
        functools.partial(soap_kernel, npad),
        grid=(1,),
        out_shape=tuple(jax.ShapeDtypeStruct(s.shape, F32) for s in outs),
        in_specs=[whole(array.shape) for array in ins],
        out_specs=tuple(whole(array.shape) for array in outs),
        scratch_shapes=[
            pltpu.VMEM((npad * side, side), F32),
            pltpu.VMEM((npad * side, side), F32),
            pltpu.VMEM((2 * n, side, side), F32),
            pltpu.VMEM((npad * PANEL, side), F32),
        ],
        cost_estimate=pl.CostEstimate(
            flops=n * 40 * side**3, bytes_accessed=n * 60 * side * side, transcendentals=0
        ),
        compiler_params=pltpu.CompilerParams(vmem_limit_bytes=32 * 2**20),
        name="soap",
    )(*ins)


LANES = 128
LABEL_PAD = 256
RIM = 96
SMALL_ROWS = 192


def up_to(value, unit):
    return -(-value // unit) * unit


def block_at(shape, *index):
    return pl.BlockSpec(shape, lambda i: index, pipeline_mode=pl.Buffered(1))


def whole(shape):
    return block_at(shape, *[0] * len(shape))


def any_space():
    return pl.BlockSpec(memory_space=pl.ANY)


def far_space():
    return pl.BlockSpec(memory_space=pltpu.HBM)


def scalars():
    return pl.BlockSpec(memory_space=pltpu.SMEM)


def kernel_call(body, name, mib, out_shape, in_specs, out_specs, scratch=(), aliases=None, flops=0, bytes_moved=0):
    return pl.pallas_call(
        body,
        name=name,
        grid=(1,),
        out_shape=out_shape,
        in_specs=in_specs,
        out_specs=out_specs,
        scratch_shapes=list(scratch),
        input_output_aliases=aliases or {},
        cost_estimate=pl.CostEstimate(flops=flops, bytes_accessed=bytes_moved, transcendentals=0),
        compiler_params=pltpu.CompilerParams(vmem_limit_bytes=mib * 2**20),
    )


def start_tiles(row_ref, col_ref, kind_ref, sources, tiles, wall_ref, sems):
    base = 0
    for source, many in zip(sources, tiles):

        def start(i, carry):
            for k in range(many):
                place = base + i * many + k
                kind = kind_ref[place]

                @pl.when(kind < 2)
                def _():
                    row = pl.multiple_of(row_ref[place], LANES)
                    col = pl.multiple_of(col_ref[place], LANES)
                    pltpu.make_async_copy(
                        source.at[i, pl.ds(k * LANES, LANES)],
                        wall_ref.at[pl.ds(row, LANES), pl.ds(col, LANES)],
                        sems.at[kind],
                    ).start()

            return carry

        lax.fori_loop(0, source.shape[0], start, 0)
        base += source.shape[0] * many


def wait_rows(wall_ref, rows, sem):
    part = wall_ref.at[pl.ds(0, rows)]
    pltpu.make_async_copy(part, part, sem).wait()


def low_lanes(rows):
    return lax.broadcasted_iota(jnp.int32, (rows, LANES), 1) < LANES // 2


def stack_heads(pair):
    low = low_lanes(pair.shape[0])
    zero = jnp.zeros_like(pair)
    return jnp.concatenate([jnp.where(low, pair, zero), jnp.where(low, zero, pair)], axis=0)


def merge_stack(stacked):
    rows = stacked.shape[0] // 2
    return jnp.where(low_lanes(rows), stacked[:rows], stacked[rows:])


def skew(table, width):
    rows = table.shape[0] // 2
    padded = jnp.concatenate(
        [table, jnp.zeros((table.shape[0], width - table.shape[1]), F32)], axis=1
    )
    halves = [
        pltpu.roll(padded[at : at + rows], 0, 1, stride=1, stride_axis=0) for at in (0, rows)
    ]
    return jnp.concatenate(halves, axis=0)


def unskew(grid, width):
    rows = grid.shape[0] // 2
    lanes = grid.shape[1]
    parts = []
    for at in range(0, 2 * rows, 8):
        shift = (at % rows) % lanes
        part = grid[at : at + 8]
        parts.append(part if shift == 0 else pltpu.roll(part, lanes - shift, 1))
    moved = jnp.concatenate(parts, axis=0)
    index = lax.broadcasted_iota(jnp.int32, moved.shape, 0)
    for bit in (1, 2, 4):
        moved = jnp.where((index & bit) != 0, pltpu.roll(moved, lanes - bit, 1), moved)
    return moved[:, :width]


def softmax_rows(scores):
    top = jnp.max(scores, axis=-1, keepdims=True)
    raised = jnp.exp(scores - top)
    return raised * (1.0 / jnp.sum(raised, axis=-1, keepdims=True))


def window_keys(ref, base, at, width, ext, globs, cols):
    return jnp.concatenate(
        [ref[pl.ds(base + at, width), cols], ref[pl.ds(base + ext, globs), cols]], axis=0
    )


def glob_row_mask(shape, seq, glob_block):
    row = lax.broadcasted_iota(jnp.int32, shape, 0) % (shape[0] // 2)
    return (row >= seq * glob_block) & (row < (seq + 1) * glob_block)


def window_bias(block, blocks, chunk, dims):
    _, block_len, _, _, width, globs, _ = dims
    shape = (2 * LANES, width + globs)
    key = lax.broadcasted_iota(jnp.int32, shape, 1)
    query = lax.broadcasted_iota(jnp.int32, shape, 0) % LANES
    offset = key - query - (RIM - RADIUS)
    token = block * block_len - RIM + chunk * LANES + key
    near = (offset >= 0) & (offset <= 2 * RADIUS) & (token >= 0) & (token < blocks * block_len)
    return jnp.where(near | (key >= width), 0.0, NEG_FILL)


def attend_kernel(dims, wall_at, blocks, row_ref, col_ref, kind_ref, block_ref, xr_ref, rel_ref, gbias_ref,
                  left_ref, right_ref, *refs):
    q_ref, k_ref, v_ref, o_ref, part_ref, xe_ref, wall_out, wall_ref, glob_low, glob_cells, sems = refs[-11:]
    sources = refs[:-11]
    seqs, block_len, glob_block, ext, width, globs, scale = dims
    feed_rows, attn_rows, qk_at, v_at, out_at, tiles = wall_at
    model_dim = xr_ref.shape[1]
    head_cols = q_ref.shape[1]
    start_tiles(row_ref, col_ref, kind_ref, sources, tiles, wall_ref, sems)
    span = ext + globs
    cells = glob_low.shape[0] // blocks
    copies, base = [], 0
    for source in sources[-2:]:
        rows = source.shape[1] - cells
        for i in range(source.shape[0]):
            copies.append((source.at[i, pl.ds(rows, cells)], glob_low.at[pl.ds(base, cells)]))
            base += cells
    for source, target in copies:
        pltpu.make_async_copy(source, target, sems.at[3]).start()
    for seq in range(seqs):
        at = seq * span
        rim = pl.ds(seq * RIM, RIM)
        pltpu.make_async_copy(left_ref.at[rim], xe_ref.at[pl.ds(at, RIM)], sems.at[4]).start()
        pltpu.make_async_copy(
            right_ref.at[rim], xe_ref.at[pl.ds(at + RIM + block_len, RIM)], sems.at[4]
        ).start()
        at += RIM
        xe_ref[at : at + block_len] = xr_ref[seq * block_len : (seq + 1) * block_len]
        at += block_len + RIM
        if ext > block_len + 2 * RIM:
            xe_ref[at : seq * span + ext] = jnp.zeros((ext - block_len - 2 * RIM, model_dim), BF)
    pltpu.make_async_copy(glob_low, glob_low, sems.at[3]).wait()
    glob_cells[...] = glob_low[...].astype(F32)
    cols = model_dim // LANES
    for seq in range(seqs):
        for r in range(glob_block):
            at = seq * span + ext + r * blocks
            for c in range(cols):
                source = pl.ds((seq * glob_block + r) * cols + c, blocks, stride=cells)
                xe_ref[at : at + blocks, c * LANES : (c + 1) * LANES] = glob_cells[source, :].astype(BF)
    rims = xe_ref.at[pl.ds(0, 2 * seqs * RIM)]
    pltpu.make_async_copy(rims, rims, sems.at[4]).wait()
    wait_rows(wall_ref, attn_rows, sems.at[0])
    wq_ref = wall_ref.at[pl.ds(qk_at, model_dim), pl.ds(0, head_cols)]
    wk_ref = wall_ref.at[pl.ds(qk_at, model_dim), pl.ds(head_cols, head_cols)]
    wv_ref = wall_ref.at[pl.ds(v_at, model_dim), pl.ds(0, head_cols)]
    wo_ref = wall_ref.at[pl.ds(out_at, head_cols)]
    pairs = head_cols // LANES
    glob_at = seqs * block_len
    glob_rows = q_ref.shape[0] - glob_at
    span = ext + globs
    chunks = block_len // LANES
    q_ref[...] = dot_on(xr_ref[...], wq_ref[...], 1, 0).astype(BF)

    def project(i, carry):
        rows = pl.ds(pl.multiple_of(i * 256, 256), 256)
        k_ref[rows, :] = dot_on(xe_ref[rows, :], wk_ref[...], 1, 0).astype(BF)
        v_ref[rows, :] = dot_on(xe_ref[rows, :], wv_ref[...], 1, 0).astype(BF)
        return carry

    lax.fori_loop(0, seqs * span // 256, project, 0)
    wait_rows(wall_ref, feed_rows, sems.at[1])
    keep = pltpu.make_async_copy(wall_ref, wall_out, sems.at[2])
    keep.start()

    def window(i, carry):
        seq, chunk = i // chunks, i % chunks
        rows = pl.ds(pl.multiple_of(i * LANES, LANES), LANES)
        base = pl.multiple_of(seq * span, LANES)
        at = pl.multiple_of(chunk * LANES, LANES)
        bias = window_bias(block_ref[0], blocks, chunk, dims)
        for pair in range(pairs):
            cols = slice(pair * LANES, (pair + 1) * LANES)
            query = stack_heads(q_ref[rows, cols] * scale)
            keys = window_keys(k_ref, base, at, width, ext, globs, cols)
            values = window_keys(v_ref, base, at, width, ext, globs, cols)
            scores = dot_on(query, keys, 1, 1)
            scores = scores + skew(dot_on(query, rel_ref[:, cols], 1, 1), width + globs) + bias
            weights = softmax_rows(scores).astype(BF)
            o_ref[rows, cols] = merge_stack(dot_on(weights, values, 1, 0)).astype(BF)
        return carry

    lax.fori_loop(0, seqs * chunks, window, 0)
    rows = slice(glob_at, glob_at + glob_rows)
    for pair in range(pairs):
        cols = slice(pair * LANES, (pair + 1) * LANES)
        query = stack_heads(q_ref[rows, cols] * scale)
        total = jnp.zeros((2 * glob_rows, LANES), F32)
        for seq in range(seqs):
            span_rows = slice(seq * span, (seq + 1) * span)
            bias = gbias_ref[seq]
            scores = dot_on(query, k_ref[span_rows, cols], 1, 1) + jnp.concatenate([bias, bias], axis=0)
            weights = softmax_rows(scores).astype(BF)
            out = dot_on(weights, v_ref[span_rows, cols], 1, 0)
            total = jnp.where(glob_row_mask(total.shape, seq, glob_block), out, total)
        o_ref[rows, cols] = merge_stack(total).astype(BF)
    part_ref[...] = dot_on(o_ref[...], wo_ref[...], 1, 0).astype(BF)
    keep.wait()


def norm_parts(values):
    center = values - jnp.mean(values, axis=-1, keepdims=True)
    spread = jnp.mean(center * center, axis=-1, keepdims=True)
    rate = lax.rsqrt(spread + NORM_EPS)
    return center * rate, rate


def norm_back(grad, normed, rate, gain):
    scaled = grad * gain
    return (
        scaled
        - jnp.mean(scaled, axis=-1, keepdims=True)
        - normed * jnp.mean(scaled * normed, axis=-1, keepdims=True)
    ) * rate


def row_loop(total, body):
    step = 176 if total % 176 == 0 else 16

    def run(i, carry):
        body(pl.ds(pl.multiple_of(i * step, 16), step))
        return carry

    lax.fori_loop(0, total // step, run, 0)


def col_loop(total, body, step=256):
    def run(i, carry):
        body(i)
        return carry

    lax.fori_loop(0, total // step, run, 0)


GELU_RATE = 0.7978845608028654
GELU_CUBE = 0.044715


def gelu_parts(u):
    square = u * u
    curve = jnp.tanh(GELU_RATE * u * (1.0 + GELU_CUBE * square))
    return square, curve


def feed_kernel(xr_ref, part_ref, got_ref, norm_ref, wu_ref, wd_ref, h_ref, hb_ref, u_ref, a_ref, down_ref):
    model_dim = xr_ref.shape[1]
    gain, offset = norm_ref[0:1], norm_ref[1:2]

    def norm(rows):
        mid = xr_ref[rows, :].astype(F32) + (part_ref[rows, :].astype(F32) + got_ref[rows, :].astype(F32))
        normed, _ = norm_parts(mid)
        out = normed * gain + offset
        h_ref[rows, :] = out
        hb_ref[rows, :] = out.astype(BF)

    row_loop(xr_ref.shape[0], norm)
    per_half = model_dim // 256

    def up(j):
        rows = pl.ds(pl.multiple_of((j // per_half) * model_dim, 256), model_dim)
        cols = pl.ds(pl.multiple_of((j % per_half) * 256, 256), 256)
        here = pl.ds(pl.multiple_of(j * 256, 256), 256)
        u = dot_on(hb_ref[...], wu_ref[rows, cols], 1, 0)
        u_ref[:, here] = u
        _, curve = gelu_parts(u)
        a_ref[:, here] = (0.5 * u * (1.0 + curve)).astype(BF)

    col_loop(u_ref.shape[1], up)

    def down(j):
        cols = pl.ds(pl.multiple_of(j * 256, 256), 256)
        down_ref[:, cols] = dot_on(a_ref[...], wd_ref[:, cols], 1, 0).astype(BF)

    col_loop(model_dim, down)


def own_rows(ref, half, seqs, block_len, glob_block):
    per = block_len // 2
    long_part = [
        ref[pl.ds(pl.multiple_of(seq * block_len + half * per, per), per), :] for seq in range(seqs)
    ]
    base, few = seqs * block_len, glob_block // 2
    globs = ref[base:, :]
    glob_part = [
        jnp.where(
            half == 0,
            globs[seq * glob_block : seq * glob_block + few],
            globs[seq * glob_block + few : (seq + 1) * glob_block],
        )
        for seq in range(seqs)
    ]
    return long_part, glob_part


def feed_back_kernel(dims, half_ref, h_ref, down_ref, got_ref, u_ref, dy_ref, norm_ref, wu_ref, wd_ref,
                     y_long_ref, y_glob_ref, dx_ref, dxb_ref, du_ref, dh_ref, gn_ref, y_ref):
    model_dim = h_ref.shape[1]
    gain, offset = norm_ref[2:3], norm_ref[3:4]
    gn_ref[...] = jnp.zeros_like(gn_ref)

    def norm(rows):
        out = h_ref[rows, :] + (down_ref[rows, :].astype(F32) + got_ref[rows, :].astype(F32))
        normed, rate = norm_parts(out)
        y_ref[rows, :] = normed * gain + offset
        grad = dy_ref[rows, :].astype(F32)
        gn_ref[0:1] += jnp.sum(grad * normed, axis=0, keepdims=True)
        gn_ref[1:2] += jnp.sum(grad, axis=0, keepdims=True)
        dx = norm_back(grad, normed, rate, gain)
        dx_ref[rows, :] = dx
        dxb_ref[rows, :] = dx.astype(BF)

    row_loop(h_ref.shape[0], norm)
    long_part, glob_part = own_rows(y_ref, half_ref[0], *dims[:3])
    for seq in range(dims[0]):
        y_long_ref[seq] = long_part[seq].astype(BF)
        y_glob_ref[seq] = glob_part[seq].astype(BF)

    def act(j):
        here = pl.ds(pl.multiple_of(j * 256, 256), 256)
        da = dot_on(dxb_ref[...], wd_ref[here, :], 1, 1)
        u = u_ref[:, here]
        square, curve = gelu_parts(u)
        slope = 0.5 * (1.0 + curve) + 0.5 * u * (1.0 - curve * curve) * (
            GELU_RATE * (1.0 + 3.0 * GELU_CUBE * square)
        )
        du_ref[:, here] = (da * slope).astype(BF)

    col_loop(u_ref.shape[1], act)
    halves = u_ref.shape[1] // model_dim

    def lower(j):
        cols = pl.ds(pl.multiple_of(j * 256, 256), 256)
        total = 0.0
        for half in range(halves):
            rows = pl.ds(pl.multiple_of(half * model_dim + j * 256, 256), 256)
            total = total + dot_on(
                du_ref[:, half * model_dim : (half + 1) * model_dim], wu_ref[rows, :], 1, 1
            )
        dh_ref[:, cols] = total.astype(BF)

    col_loop(model_dim, lower)


def send_tiles(stage_ref, row, rows, first, place_ref, out_ref, sem):
    cols = stage_ref.shape[1] // LANES
    for r in range(rows):
        for c in range(cols):
            pltpu.make_async_copy(
                stage_ref.at[pl.ds(row + r * LANES, LANES), pl.ds(c * LANES, LANES)],
                out_ref.at[pl.ds(pl.multiple_of(place_ref[first + r * cols + c], 16), LANES)],
                sem,
            ).start()


def feed_grads_kernel(tiles_at, place_ref, a_ref, dxb_ref, hb_ref, du_ref, out_ref, down_stage, up_stage, sems):
    up_at, down_at = tiles_at
    model_dim = dxb_ref.shape[1]

    def down(j):
        row = pl.multiple_of(j * 256, 256)
        rows = pl.ds(row, 256)
        down_stage[rows, :] = dot_on(a_ref[:, rows], dxb_ref[...], 0, 0).astype(BF)
        send_tiles(down_stage, row, 2, down_at + j * 2 * (model_dim // LANES), place_ref, out_ref, sems.at[0])

    col_loop(a_ref.shape[1], down)

    def up(j):
        row = pl.multiple_of(j * 256, 256)
        rows = pl.ds(row, 256)
        up_stage[rows, :] = dot_on(hb_ref[:, rows], du_ref[...], 0, 0).astype(BF)
        send_tiles(
            up_stage, row, 2, up_at + j * 2 * (du_ref.shape[1] // LANES), place_ref, out_ref, sems.at[1]
        )

    col_loop(model_dim, up)
    pltpu.make_async_copy(down_stage, down_stage, sems.at[0]).wait()
    pltpu.make_async_copy(up_stage, up_stage, sems.at[1]).wait()


def attend_back_kernel(dims, blocks, attn_tiles, tile_counts, glob_at_rows, block_ref, place_ref, norm_two_ref, xr_ref, part_ref, got_ref, dh_ref, dh_got_ref, dx_ref, o_ref,
                       q_ref, k_ref, v_ref, xe_ref, wo_ref, rel_ref, gbias_ref, norm_ref, grads_in,
                       grads_ref, dq_ref, dkv_ref, mid_ref, small_ref,
                       do_ref, midb_ref, dkv_acc, out_stage, q_stage, k_stage, v_stage, none_ref,
                       drel_ref, norms_ref, gn_ref, glob_stage, glob_low, sems):
    seqs, block_len, glob_block, ext, width, globs, scale = dims
    head_cols = q_ref.shape[1]
    pairs = head_cols // LANES
    glob_at = seqs * block_len
    glob_rows = q_ref.shape[0] - glob_at
    span = ext + globs
    chunks = block_len // LANES
    gain = norm_ref[0:1]
    gn_ref[...] = jnp.zeros_like(gn_ref)

    def norm(rows):
        mid = xr_ref[rows, :].astype(F32) + (part_ref[rows, :].astype(F32) + got_ref[rows, :].astype(F32))
        normed, rate = norm_parts(mid)
        grad = dh_ref[rows, :].astype(F32) + dh_got_ref[rows, :].astype(F32) + dx_ref[rows, :]
        gn_ref[0:1] += jnp.sum(grad * normed, axis=0, keepdims=True)
        gn_ref[1:2] += jnp.sum(grad, axis=0, keepdims=True)
        out = norm_back(grad, normed, rate, gain)
        mid_ref[rows, :] = out
        midb_ref[rows, :] = out.astype(BF)

    row_loop(xr_ref.shape[0], norm)
    do_ref[...] = dot_on(midb_ref[...], wo_ref[...], 1, 1).astype(BF)
    out_stage[...] = dot_on(o_ref[...], midb_ref[...], 0, 0).astype(BF)
    send_tiles(out_stage, 0, out_stage.shape[0] // LANES, 3 * attn_tiles, place_ref, grads_ref, sems.at[0])
    none_ref[...] = jnp.zeros_like(none_ref)
    spare = []
    for tile in range(*tile_counts):
        target = grads_ref.at[pl.ds(pl.multiple_of(place_ref[tile], 16), LANES)]
        spare.append(pltpu.make_async_copy(none_ref, target, sems.at[4]))
        spare[-1].start()
    dkv_acc[...] = jnp.zeros_like(dkv_acc)
    drel_ref[...] = jnp.zeros_like(drel_ref)

    def grads_of(scores, grad_out, values):
        weights = softmax_rows(scores)
        dp = dot_on(grad_out, values, 1, 1)
        delta = jnp.sum(weights * dp, axis=-1, keepdims=True)
        return weights.astype(BF), weights * (dp - delta)

    def window(i, carry):
        seq, chunk = i // chunks, i % chunks
        rows = pl.ds(pl.multiple_of(i * LANES, LANES), LANES)
        base = pl.multiple_of(seq * span, LANES)
        at = pl.multiple_of(chunk * LANES, LANES)
        near_rows = pl.ds(base + at, width)
        far_rows = pl.ds(base + ext, globs)
        bias = window_bias(block_ref[0], blocks, chunk, dims)
        near = lax.broadcasted_iota(jnp.int32, bias.shape, 1) < width
        for pair in range(pairs):
            cols = slice(pair * LANES, (pair + 1) * LANES)
            query = stack_heads(q_ref[rows, cols] * scale)
            grad_out = stack_heads(do_ref[rows, cols])
            keys = window_keys(k_ref, base, at, width, ext, globs, cols)
            values = window_keys(v_ref, base, at, width, ext, globs, cols)
            labels = rel_ref[:, cols]
            scores = dot_on(query, keys, 1, 1)
            scores = scores + skew(dot_on(query, labels, 1, 1), width + globs) + bias
            weights, ds = grads_of(scores, grad_out, values)
            dsb = ds.astype(BF)
            by_label = unskew(jnp.where(near, dsb.astype(F32), 0.0), LABEL_PAD).astype(BF)
            dv = dot_on(weights, grad_out, 0, 0)
            dk = dot_on(dsb, query, 0, 0)
            dq = dot_on(dsb, keys, 1, 0) + dot_on(by_label, labels, 1, 0)
            dq_ref[rows, cols] = (merge_stack(dq) * scale).astype(BF)
            drel_ref[:, cols] += dot_on(by_label, query, 0, 0)
            dkv_acc[pair, near_rows] += dk[:width]
            dkv_acc[pair, far_rows] += dk[width:]
            dkv_acc[pairs + pair, near_rows] += dv[:width]
            dkv_acc[pairs + pair, far_rows] += dv[width:]
        return carry

    lax.fori_loop(0, seqs * chunks, window, 0)
    rows = slice(glob_at, glob_at + glob_rows)
    for pair in range(pairs):
        cols = slice(pair * LANES, (pair + 1) * LANES)
        query = stack_heads(q_ref[rows, cols] * scale)
        grad_out = stack_heads(do_ref[rows, cols])
        total = jnp.zeros((2 * glob_rows, LANES), F32)
        for seq in range(seqs):
            span_rows = slice(seq * span, (seq + 1) * span)
            bias = gbias_ref[seq]
            keys = k_ref[span_rows, cols]
            scores = dot_on(query, keys, 1, 1) + jnp.concatenate([bias, bias], axis=0)
            weights, ds = grads_of(scores, grad_out, v_ref[span_rows, cols])
            own = glob_row_mask(ds.shape, seq, glob_block)
            weights = jnp.where(own, weights.astype(F32), 0.0).astype(BF)
            dsb = jnp.where(own, ds, 0.0).astype(BF)
            dkv_acc[pair, span_rows] += dot_on(dsb, query, 0, 0)
            dkv_acc[pairs + pair, span_rows] += dot_on(weights, grad_out, 0, 0)
            total = total + dot_on(dsb, keys, 1, 0)
        dq_ref[rows, cols] = (merge_stack(total) * scale).astype(BF)
    first_row, row_step, cells, per_block = glob_at_rows
    for seq in range(seqs):
        for r in range(per_block):
            source = pl.ds(seq * span + ext + r * blocks, blocks)
            for c in range(2 * pairs):
                rows = pl.ds((seq * per_block + r) * 2 * pairs + c, blocks, stride=cells)
                glob_stage[rows, :] = dkv_acc[c, source, :]
    glob_low[...] = glob_stage[...].astype(BF)
    for i in range(blocks):
        pltpu.make_async_copy(
            glob_low.at[pl.ds(i * cells, cells)],
            grads_ref.at[pl.ds(first_row + (i + 1) * row_step - cells, cells)],
            sems.at[5],
        ).start()
    norms_ref[...] = jnp.zeros_like(norms_ref)
    for row, source in enumerate((gn_ref, gn_ref, norm_two_ref, norm_two_ref)):
        for half in range(source.shape[1] // head_cols):
            at = row * (source.shape[1] // head_cols) + half
            norms_ref[at : at + 1] = source[row % 2 : row % 2 + 1, half * head_cols : (half + 1) * head_cols]
    small_ref[...] = jnp.concatenate([drel_ref[: SMALL_ROWS - 8], norms_ref[...]], axis=0).astype(BF)
    for c in range(2 * pairs):
        dkv_ref[:, c * LANES : (c + 1) * LANES] = dkv_acc[c].astype(BF)
    for at, stage in ((0, q_stage), (1, k_stage), (2, v_stage)):
        rows_ref = xr_ref if at == 0 else xe_ref
        grad = dq_ref[...] if at == 0 else dkv_ref[:, (at - 1) * head_cols : at * head_cols]

        def cut(j):
            row = pl.multiple_of(j * 256, 256)
            stage[pl.ds(row, 256), :] = dot_on(rows_ref[:, pl.ds(row, 256)], grad, 0, 0).astype(BF)
            send_tiles(
                stage, row, 2, at * attn_tiles + j * 2 * (head_cols // LANES), place_ref, grads_ref, sems.at[1 + at]
            )

        col_loop(stage.shape[0], cut)
    for at, stage in enumerate((out_stage, q_stage, k_stage, v_stage)):
        pltpu.make_async_copy(stage, stage, sems.at[at]).wait()
    for copy in spare:
        copy.wait()
    pltpu.make_async_copy(glob_low, glob_low, sems.at[5]).wait()


def start_weights(wall_ref, at, head_cols, wqk_ref, wv_ref, sems):
    model_dim = wqk_ref.shape[0]
    copies = [
        pltpu.make_async_copy(wall_ref.at[pl.ds(at[0], model_dim)], wqk_ref, sems.at[0]),
        pltpu.make_async_copy(
            wall_ref.at[pl.ds(at[1], model_dim), pl.ds(0, head_cols)], wv_ref, sems.at[1]
        ),
    ]
    for copy in copies:
        copy.start()
    return copies


def back_rows(proj, wqk_ref, wv_ref):
    both = wqk_ref.shape[1]
    return dot_on(proj[:, :both], wqk_ref[...], 1, 1) + dot_on(proj[:, both:], wv_ref[...], 1, 1)


def dx_kernel(dims, at, half_ref, dq_ref, dkv_ref, next_ref, last_ref, mid_ref, wall_ref,
              keep_ref, send_ref, proj_ref, wqk_ref, wv_ref, sems):
    seqs, block_len, _, ext, _, globs, _ = dims
    head_cols = dq_ref.shape[1]
    copies = start_weights(wall_ref, at, head_cols, wqk_ref, wv_ref, sems)
    proj_ref[:, :head_cols] = dq_ref[: seqs * block_len]
    for seq in range(seqs):
        base, row = seq * (ext + globs) + RIM, seq * block_len
        middle = block_len - 2 * RIM
        own = dkv_ref[base : base + block_len].astype(F32)
        sums = [
            own[:RIM] + last_ref[seq * RIM : (seq + 1) * RIM].astype(F32),
            own[RIM : RIM + middle],
            own[RIM + middle :] + next_ref[seq * RIM : (seq + 1) * RIM].astype(F32),
        ]
        proj_ref[row : row + block_len, head_cols:] = jnp.concatenate(sums, axis=0).astype(BF)
    for copy in copies:
        copy.wait()
    per = block_len // 2
    for out_ref, half in ((keep_ref, half_ref[0]), (send_ref, 1 - half_ref[0])):
        for seq in range(seqs):
            rows = pl.ds(pl.multiple_of(seq * block_len + half * per, per), per)
            total = back_rows(proj_ref[rows, :], wqk_ref, wv_ref)
            if out_ref is keep_ref:
                total = total + mid_ref[rows, :]
            out_ref[seq] = total.astype(out_ref.dtype)


def dx_glob_kernel(dims, at, half_ref, dq_ref, kept_ref, got_ref, mid_ref, wall_ref,
                   keep_ref, send_ref, cells_ref, wqk_ref, wv_ref, sems):
    seqs, block_len, glob_block = dims[:3]
    head_cols = dq_ref.shape[1]
    base = seqs * block_len
    used, cols = seqs * glob_block, 2 * head_cols // LANES
    copies = start_weights(wall_ref, at, head_cols, wqk_ref, wv_ref, sems)
    first = kept_ref.shape[0] - used * cols
    cells_ref[...] = kept_ref[first:].astype(F32) + got_ref[first:].astype(F32)
    wide = [cells_ref[pl.ds(c, used, stride=cols), :] for c in range(cols)]
    dkv = jnp.concatenate(wide, axis=1)
    dkv = jnp.concatenate([dkv, jnp.zeros((dq_ref.shape[0] - base - used, 2 * head_cols), F32)], axis=0)
    proj = jnp.concatenate([dq_ref[base:], dkv.astype(BF)], axis=1)
    for copy in copies:
        copy.wait()
    total = back_rows(proj, wqk_ref, wv_ref)
    few = glob_block // 2
    here = half_ref[0] == 0
    for seq in range(seqs):
        start = seq * glob_block
        halves = [total[start : start + few], total[start + few : start + glob_block]]
        mids = [
            mid_ref[base + start : base + start + few, :],
            mid_ref[base + start + few : base + start + glob_block, :],
        ]
        keep_ref[seq] = jnp.where(here, halves[0] + mids[0], halves[1] + mids[1])
        send_ref[seq] = jnp.where(here, halves[1], halves[0]).astype(BF)


def swap_cores(values):
    count = lax.axis_size("ffn")
    return lax.ppermute(values, "ffn", [(i, i ^ 1) for i in range(count)])


def on_device(
    x_long,
    x_glob,
    sentence,
    dy_long,
    dy_glob,
    owner_list,
    w_master,
    m_old,
    v_old,
    left_basis,
    right_basis,
    left_stats,
    right_stats,
    rel_table,
    rel_m,
    rel_v,
    norm_params,
    norm_m,
    norm_v,
):
    ffn_count = lax.axis_size("ffn")
    seq_count = lax.axis_size("seq")
    seqs, tok_half, model_dim = x_long.shape
    glob_half = x_glob.shape[1]
    block_len = tok_half * ffn_count
    glob_block = glob_half * ffn_count
    globs = glob_block * seq_count
    head_cols = model_dim // ffn_count
    hidden = FF // ffn_count
    scale = (model_dim // HEADS) ** (-0.5)
    slots, side = w_master.shape[:2]
    attn_tiles = model_dim * head_cols // (side * side)
    ffn_tiles = model_dim * hidden // (side * side)
    tile_count = 4 * attn_tiles + 2 * ffn_tiles
    slot_count = owner_list.shape[0]
    labels = rel_table.shape[0]
    half_index = lax.axis_index("ffn")
    first_half = half_index == 0
    parts = slot_parts(slots, seq_count)

    glob_cells = seqs * glob_block * model_dim // LANES
    rows_per = part_rows(parts, side, glob_cells)
    places, place_rows = slot_places(owner_list, slots, rows_per, side)
    held = jnp.sum(
        jnp.where(
            places[None, :] == jnp.arange(slot_count, dtype=jnp.int32)[:, None],
            jnp.arange(slot_count, dtype=jnp.int32)[None, :],
            0,
        ),
        axis=1,
    )
    per_row = model_dim // side
    up_rows = hidden // model_dim * model_dim
    qk_at = up_rows + hidden
    v_at = qk_at + model_dim
    out_at = v_at + model_dim
    head_tiles = head_cols // side
    up_tiles = hidden // side

    def tile_row_col(tile):
        kind_qkv = tile // attn_tiles
        inner = tile % attn_tiles
        qkv_row = jnp.where(kind_qkv == 2, v_at, qk_at) + inner // head_tiles * side
        qkv_col = jnp.where(kind_qkv == 1, head_cols, 0) + inner % head_tiles * side
        out_row = out_at + inner // per_row * side
        up = tile - 4 * attn_tiles
        up_col = up % up_tiles * side
        up_row = up_col // model_dim * model_dim + up // up_tiles * side
        down = up - ffn_tiles
        down_row = up_rows + down // per_row * side
        row = jnp.where(
            tile < 3 * attn_tiles,
            qkv_row,
            jnp.where(
                tile < 4 * attn_tiles,
                out_row,
                jnp.where(up < ffn_tiles, up_row, down_row),
            ),
        )
        col = jnp.where(
            tile < 3 * attn_tiles,
            qkv_col,
            jnp.where(
                tile < 4 * attn_tiles,
                inner % per_row * side,
                jnp.where(up < ffn_tiles, up_col % model_dim, down % per_row * side),
            ),
        )
        return row, col

    wall_row, wall_col = tile_row_col(held)
    wall_kind = jnp.where(held < 4 * attn_tiles, 0, jnp.where(held < tile_count, 1, 2))

    mine = jnp.concatenate([x_long, dy_long, x_glob, dy_glob], axis=1)
    other = swap_cores(mine)
    lower = jnp.where(first_half, mine, other)
    upper = jnp.where(first_half, other, mine)

    def block_rows(at, count):
        return jnp.concatenate([lower[:, at : at + count], upper[:, at : at + count]], axis=1)

    long_rows = block_rows(0, tok_half)
    dy_rows = block_rows(tok_half, tok_half)
    glob_rows = block_rows(2 * tok_half, glob_half)
    dy_globs = block_rows(2 * tok_half + glob_half, glob_half)
    used = seqs * (block_len + glob_block)
    row_count = seqs * block_len + up_to(seqs * glob_block, 16)
    pad_rows = jnp.zeros((row_count - used, model_dim), BF)

    def in_rows(long_part, glob_part):
        return jnp.concatenate(
            [long_part.reshape(-1, model_dim), glob_part.reshape(-1, model_dim), pad_rows]
        )

    x_rows = in_rows(long_rows, glob_rows)
    dy_all = in_rows(dy_rows, dy_globs)
    rim = jnp.where(first_half, x_long[:, :RIM], x_long[:, tok_half - RIM :])
    to_next = [(i * ffn_count + 1, (i + 1) * ffn_count + 1) for i in range(seq_count - 1)]
    to_last = [((i + 1) * ffn_count, i * ffn_count) for i in range(seq_count - 1)]
    rim = lax.ppermute(rim, ("seq", "ffn"), to_next + to_last)
    rim_other = swap_cores(rim)
    rim_left = jnp.where(first_half, rim_other, rim).reshape(-1, model_dim)
    rim_right = jnp.where(first_half, rim, rim_other).reshape(-1, model_dim)

    weights_low = w_master.astype(BF)
    glob_other = swap_cores(x_glob)
    glob_own = jnp.concatenate(
        [jnp.where(first_half, x_glob, glob_other), jnp.where(first_half, glob_other, x_glob)], axis=1
    )
    orders = [order for _, _, order in parts]
    gathered = [
        [piece.reshape(-1, many, LANES) for piece in pieces]
        for pieces, many in zip(
            gather_rows(
                weights_low.reshape(-1, LANES), glob_own.reshape(-1, LANES), rows_per, orders
            ),
            rows_per,
        )
    ]
    tiles_per = tuple(last - first for (first, last, _), pieces in zip(parts, gathered) for _ in pieces)
    gathered = [piece for pieces in gathered for piece in pieces]
    reach = 2 * RADIUS
    width = up_to(LANES + 2 * RIM, LANES) if globs % LANES == 0 else up_to(LANES + 2 * RIM + globs, LANES) - globs
    ext = block_len - LANES + width
    span = ext + globs
    rel_low = jnp.pad(
        rel_table.astype(BF), ((RIM - RADIUS, LABEL_PAD - labels - RIM + RADIUS), (0, 0))
    )

    glob_bias_rows = row_count - seqs * block_len
    row_at = jnp.arange(glob_bias_rows, dtype=jnp.int32)[None, :, None]
    seq_at = jnp.arange(seqs, dtype=jnp.int32)[:, None, None]
    spread = jnp.pad(sentence[:, 0], ((0, 0), (RIM, span - RIM - block_len)), constant_values=-1)
    span_at = jnp.arange(span, dtype=jnp.int32)[None, None, :]
    own = (spread[:, None, :] == row_at - seq_at * glob_block) & (spread[:, None, :] >= 0)
    glob_bias = jnp.where(own | (span_at >= ext), 0.0, NEG_FILL).astype(F32)

    spec_up = block_at((up_rows, model_dim), 0, 0)
    spec_down = block_at((hidden, model_dim), 1, 0)
    spec_out = block_at((head_cols, model_dim), out_at // head_cols, 0)

    def rows_of(cols, dtype=BF, rows=row_count):
        return jax.ShapeDtypeStruct((rows, cols), dtype)

    def specs(arrays):
        return [whole(a.shape) for a in arrays]

    dims = (seqs, block_len, glob_block, ext, width, globs, scale)
    fwd_shapes = (
        rows_of(head_cols),
        rows_of(head_cols, rows=seqs * span),
        rows_of(head_cols, rows=seqs * span),
        rows_of(head_cols),
        rows_of(model_dim),
        rows_of(model_dim, rows=seqs * span),
    )
    wall_at = (
        2 * ffn_tiles // per_row * side,
        4 * attn_tiles // per_row * side,
        qk_at,
        v_at,
        out_at,
        tiles_per,
    )
    wall_shape = jax.ShapeDtypeStruct((out_at + head_cols, model_dim), BF)
    block_now = lax.axis_index("seq").astype(jnp.int32).reshape(1)
    ins = [x_rows, rel_low, glob_bias]
    query, keys, values, heads_out, attn_part, x_ext, wall = kernel_call(
        functools.partial(attend_kernel, dims, wall_at, seq_count),
        "attend",
        28,
        fwd_shapes + (wall_shape,),
        [scalars()] * 4 + specs(ins) + [any_space()] * (2 + len(gathered)),
        tuple(specs(fwd_shapes)) + (any_space(),),
        [
            pltpu.VMEM(wall_shape.shape, BF),
            pltpu.VMEM((seq_count * glob_cells, LANES), BF),
            pltpu.VMEM((seq_count * glob_cells, LANES), F32),
            pltpu.SemaphoreType.DMA((5,)),
        ],
        flops=4 * 10**9,
        bytes_moved=10**7,
    )(wall_row, wall_col, wall_kind, block_now, *ins, rim_left, rim_right, *gathered)
    attn_got = swap_cores(attn_part)
    feed_shapes = (
        rows_of(model_dim, F32),
        rows_of(model_dim),
        rows_of(hidden, F32),
        rows_of(hidden),
        rows_of(model_dim),
    )
    norm_one, norm_low, up_pre, act_low, down_part = kernel_call(
        feed_kernel,
        "feed",
        24,
        feed_shapes,
        specs([x_rows, attn_part, attn_got, norm_params]) + [spec_up, spec_down],
        tuple(specs(feed_shapes)),
        flops=3 * 10**9,
        bytes_moved=10**7,
    )(x_rows, attn_part, attn_got, norm_params, wall, wall)
    down_got = swap_cores(down_part)
    norm_shape = jax.ShapeDtypeStruct((8, model_dim), F32)
    half_now = half_index.astype(jnp.int32).reshape(1)
    back_shapes = (
        jax.ShapeDtypeStruct(x_long.shape, BF),
        jax.ShapeDtypeStruct(x_glob.shape, BF),
        rows_of(model_dim, F32),
        rows_of(model_dim),
        rows_of(hidden),
        rows_of(model_dim),
        norm_shape,
    )
    y_long, y_glob, d_pre, d_pre_low, d_up, d_norm_part, norm_two_grad = kernel_call(
        functools.partial(feed_back_kernel, dims),
        "feed_back",
        30,
        back_shapes,
        [scalars()]
        + specs([norm_one, down_part, down_got, up_pre, dy_all, norm_params])
        + [spec_up, spec_down],
        tuple(specs(back_shapes)),
        [pltpu.VMEM((row_count, model_dim), F32)],
        flops=3 * 10**9,
        bytes_moved=10**7,
    )(half_now, norm_one, down_part, down_got, up_pre, dy_all, norm_params, wall, wall)
    d_norm_got = swap_cores(d_norm_part)
    grads_shape = jax.ShapeDtypeStruct((seq_count * sum(rows_per), LANES), BF)
    slot_grads = kernel_call(
        functools.partial(feed_grads_kernel, (4 * attn_tiles, 4 * attn_tiles + ffn_tiles)),
        "feed_grads",
        16,
        grads_shape,
        [scalars()] + specs([act_low, d_pre_low, norm_low, d_up]),
        any_space(),
        [
            pltpu.VMEM((hidden, model_dim), BF),
            pltpu.VMEM((model_dim, hidden), BF),
            pltpu.SemaphoreType.DMA((2,)),
        ],
        flops=3 * 10**9,
        bytes_moved=10**7,
    )(place_rows, act_low, d_pre_low, norm_low, d_up)
    ins = [
        x_rows,
        attn_part,
        attn_got,
        d_norm_part,
        d_norm_got,
        d_pre,
        heads_out,
        query,
        keys,
        values,
        x_ext,
    ]
    last_shapes = (
        grads_shape,
        rows_of(head_cols),
        rows_of(2 * head_cols, rows=seqs * span),
        rows_of(model_dim, F32),
        rows_of(head_cols, rows=SMALL_ROWS),
    )
    slot_grads, d_query, dkv, d_mid, small = kernel_call(
        functools.partial(
            attend_back_kernel,
            dims,
            seq_count,
            attn_tiles,
            (tile_count, slot_count),
            (seq_count * sum(rows_per[:-1]), rows_per[-1], glob_cells, glob_block),
        ),
        "attend_back",
        32,
        last_shapes,
        [scalars(), scalars(), whole(norm_shape.shape)]
        + specs(ins)
        + [spec_out]
        + specs([rel_low, glob_bias, norm_params])
        + [any_space()],
        (any_space(),) + tuple(specs(last_shapes[1:])),
        [
            pltpu.VMEM((row_count, head_cols), BF),
            pltpu.VMEM((row_count, model_dim), BF),
            pltpu.VMEM((2 * head_cols // LANES, seqs * span, LANES), F32),
            pltpu.VMEM((head_cols, model_dim), BF),
            pltpu.VMEM((model_dim, head_cols), BF),
            pltpu.VMEM((model_dim, head_cols), BF),
            pltpu.VMEM((model_dim, head_cols), BF),
            pltpu.VMEM((side, side), BF),
            pltpu.VMEM((LABEL_PAD, head_cols), F32),
            pltpu.VMEM((8, head_cols), F32),
            pltpu.VMEM((8, model_dim), F32),
            pltpu.VMEM((seq_count * glob_cells, LANES), F32),
            pltpu.VMEM((seq_count * glob_cells, LANES), BF),
            pltpu.SemaphoreType.DMA((6,)),
        ],
        {3 + len(ins) + 4: 0},
        flops=8 * 10**9,
        bytes_moved=2 * 10**7,
    )(block_now, place_rows, norm_two_grad, *ins, wall, rel_low, glob_bias, norm_params, slot_grads)

    bits = seq_bits(seq_count)
    carried = [
        [(RIM, (dkv, seq * span + at)) for seq in range(seqs)] for at in (0, RIM + block_len)
    ]
    sums, small, (to_last, to_next) = scatter_rows(
        slot_grads, rows_per, orders, small, bits[3:] + bits[:3], carried
    )
    from_next = lax.ppermute(to_last, "seq", [(i + 1, i) for i in range(seq_count - 1)])
    from_last = lax.ppermute(to_next, "seq", [(i, i + 1) for i in range(seq_count - 1)])

    weights_at = (qk_at, v_at)
    weights_held = [
        pltpu.VMEM((model_dim, model_dim), BF),
        pltpu.VMEM((model_dim, head_cols), BF),
        pltpu.SemaphoreType.DMA((2,)),
    ]
    dx_shapes = (
        jax.ShapeDtypeStruct(x_long.shape, F32),
        jax.ShapeDtypeStruct(x_long.shape, BF),
    )
    ins = [d_query, dkv, from_next, from_last, d_mid]
    dx_kept, dx_sent = kernel_call(
        functools.partial(dx_kernel, dims, weights_at),
        "dx_long",
        20,
        dx_shapes,
        [scalars()] + specs(ins) + [any_space()],
        tuple(specs(dx_shapes)),
        [pltpu.VMEM((seqs * block_len, 3 * head_cols), BF)] + weights_held,
        flops=10**9,
        bytes_moved=10**7,
    )(half_now, *ins, wall)
    dx_long = dx_kept + swap_cores(dx_sent).astype(F32)
    glob_shapes = (
        jax.ShapeDtypeStruct(x_glob.shape, F32),
        jax.ShapeDtypeStruct(x_glob.shape, BF),
    )
    ins = [d_query, sums[0], sums[1], d_mid]
    dx_kept, dx_sent = kernel_call(
        functools.partial(dx_glob_kernel, dims, weights_at),
        "dx_glob",
        12,
        glob_shapes,
        [scalars()] + specs(ins) + [any_space()],
        tuple(specs(glob_shapes)),
        [pltpu.VMEM((glob_cells, LANES), F32)] + weights_held,
        flops=10**8,
        bytes_moved=10**6,
    )(half_now, *ins, wall)
    dx_glob = dx_kept + swap_cores(dx_sent).astype(F32)

    state = (w_master, m_old, v_old, left_basis, right_basis, left_stats, right_stats)
    others = (rel_table, rel_m, rel_v, norm_params, norm_m, norm_v)
    new_state = soap_update(sums, small, state, others)
    w_new, m_new, v_new, left_q, right_q, left_s, right_s = new_state[:7]
    rel_new, rel_m_new, rel_v_new, norm_new, norm_m_new, norm_v_new = new_state[7:]
    return (
        y_long,
        y_glob,
        dx_long,
        dx_glob,
        w_new,
        m_new,
        v_new,
        left_q,
        right_q,
        left_s,
        right_s,
        rel_new,
        rel_m_new,
        rel_v_new,
        norm_new,
        norm_m_new,
        norm_v_new,
    )


def solution(mesh):
    in_specs = (
        P(None, ("seq", "ffn"), None),
        P(None, ("seq", "ffn"), None),
        P(None, "seq", None),
        P(None, ("seq", "ffn"), None),
        P(None, ("seq", "ffn"), None),
        P(),
        P(("seq", "ffn"), None, None),
        P(("seq", "ffn"), None, None),
        P(("seq", "ffn"), None, None),
        P(("seq", "ffn"), None, None),
        P(("seq", "ffn"), None, None),
        P(("seq", "ffn"), None, None),
        P(("seq", "ffn"), None, None),
        P(None, "ffn"),
        P(None, "ffn"),
        P(None, "ffn"),
        P(),
        P(),
        P(),
    )
    out_specs = (
        P(None, ("seq", "ffn"), None),
        P(None, ("seq", "ffn"), None),
        P(None, ("seq", "ffn"), None),
        P(None, ("seq", "ffn"), None),
        P(("seq", "ffn"), None, None),
        P(("seq", "ffn"), None, None),
        P(("seq", "ffn"), None, None),
        P(("seq", "ffn"), None, None),
        P(("seq", "ffn"), None, None),
        P(("seq", "ffn"), None, None),
        P(("seq", "ffn"), None, None),
        P(None, "ffn"),
        P(None, "ffn"),
        P(None, "ffn"),
        P(),
        P(),
        P(),
    )
    return jax.shard_map(
        on_device, mesh=mesh, in_specs=in_specs, out_specs=out_specs, check_vma=False
    )
```

profile of v0, /device:TPU:17, one launch (start us, length us, event | category | flops | bytes accessed | tf_op | source)
XLA Modules:
  0.0 298.6 jit_solution(8489141318425439260)
XLA Ops:
  0.7 0.7 collective-permute-start.4
  1.4 1.1 slice_select_fusion
  2.5 3.1 %collective-permute-start.1 = (bf16[2,96,768]{2,1,0:T(8,128)(2,1)S(1)}, bf16[2,96,768]{2,1,0:T(8,128)(2,1)S(1)}, u32[]{:S(2)}, u32[]{:S(2)}) collective-permute-start(bf16[2,96,768]{2,1,0:T(8,128)(2,1)S(1)} %slice_select_fusion), channel_id=1, source_target_pairs={{1,3},{3,5},{5,7},{7,9},{9,11},{11,13},{13,15},{15,17},{17,19},{19... | collective-permute-start | bytes 884744 | tf_op jit(solution)/shard_map/ppermute | solution.py:1212
  5.7 1.3 convert_element_type.15
  7.2 1.3 collective-permute-start
  8.7 2.7 collective-permute-start.5
  11.4 16.4 %collective-permute-done.5.refs_3_ = bf16[48,128]{1,0:T(8,128)(2,1)S(1)} collective-permute-done((bf16[48,128]{1,0:T(8,128)(2,1)S(1)}, bf16[48,128]{1,0:T(8,128)(2,1)S(1)}, u32[]{:S(2)}, u32[]{:S(2)}) %collective-permute-start.5) | collective-permute-done | bytes 12320 | tf_op jit(solution)/shard_map/ppermute | solution.py:34
  27.8 1.3 join_rows.3
  29.6 4.9 %collective-permute-start.6 = (bf16[1280,128]{1,0:T(8,128)(2,1)S(1)}, bf16[1280,128]{1,0:T(8,128)(2,1)S(1)}, u32[]{:S(2)}, u32[]{:S(2)}) collective-permute-start(bf16[1280,128]{1,0:T(8,128)(2,1)S(1)} %get-tuple-element.85.refs_0_), channel_id=1, source_target_pairs={{0,8},{2,10},{4,12},{6,14},{8,0},{10,2},{12,4},{14,6},{16,24},{18,... | collective-permute-start | bytes 983048 | tf_op jit(solution)/shard_map/ppermute | solution.py:34
  35.2 0.7 pad.21.clone
  35.9 5.9 %collective-permute-done.6.refs_1_ = bf16[1280,128]{1,0:T(8,128)(2,1)S(1)} collective-permute-done((bf16[1280,128]{1,0:T(8,128)(2,1)S(1)}, bf16[1280,128]{1,0:T(8,128)(2,1)S(1)}, u32[]{:S(2)}, u32[]{:S(2)}) %collective-permute-start.6) | collective-permute-done | bytes 327712 | tf_op jit(solution)/shard_map/ppermute | solution.py:34
  41.9 0.8 collective-permute-done.7.refs_3_
  42.7 0.6 join_rows.4
  43.9 2.3 collective-permute-start.2
  46.2 1.2 collective-permute-start.11
  47.6 13.1 %collective-permute-done.11.refs_5_ = bf16[2240,128]{1,0:T(8,128)(2,1)S(1)} collective-permute-done((bf16[2240,128]{1,0:T(8,128)(2,1)S(1)}, bf16[2240,128]{1,0:T(8,128)(2,1)S(1)}, u32[]{:S(2)}, u32[]{:S(2)}) %collective-permute-start.11) | collective-permute-done | bytes 573472 | tf_op jit(solution)/shard_map/ppermute | solution.py:34
  60.7 2.5 join_rows.5
  63.3 1.3 collective-permute-start.12
  64.5 0.6 collective-permute-start.13
  65.1 1.4 broadcast_select_fusion.1
  66.6 1.5 collective-permute-start.14
  68.2 1.3 fusion.14
  69.6 0.6 copy-done.31
  70.5 21.8 %collective-permute-done.14 = bf16[4480,128]{1,0:T(8,128)(2,1)} collective-permute-done((bf16[4480,128]{1,0:T(8,128)(2,1)}, bf16[4480,128]{1,0:T(8,128)(2,1)}, u32[]{:S(2)}, u32[]{:S(2)}) %collective-permute-start.14) | collective-permute-done | bytes 1146912 | tf_op jit(solution)/shard_map/ppermute | solution.py:34
  92.3 0.6 collective-permute-done.12
  92.9 1.1 collective-permute-done.13
  94.0 16.5 %attend.1 = (bf16[528,384]{1,0:T(8,128)(2,1)S(1)}, bf16[1024,384]{1,0:T(8,128)(2,1)S(1)}, bf16[1024,384]{1,0:T(8,128)(2,1)S(1)}, bf16[528,384]{1,0:T(8,128)(2,1)...) custom-call(s32[224]{0:T(256)S(1)} %get-tuple-element.175.row_ref, ...), custom_call_target="tpu_custom_call" | custom-call | flops 4000000000 | bytes 10000000 | tf_op jit(solution)/shard_map/attend/pallas_call | solution.py:1280
  110.5 2.1 collective-permute-start.15
  112.7 1.9 collective-permute-done.15.got_ref
  114.6 5.3 %feed.1 = (f32[528,768]{1,0:T(8,128)S(1)}, bf16[528,768]{1,0:T(8,128)(2,1)S(1)}, f32[528,1536]{1,0:T(8,128)S(1)}, bf16[528,1536]{1,0:T(8,128)(2,1)S(1)}, bf16[528,768]{1,0:T(8,128)(2,1)S(1)}) custom-call(bf16[528,768]{1,0:T(8,128)(2,1)S(1)} %get-tuple-element.172.xr_ref, bf16[528,768]{1,0:T(8,128)(2,1)S(1)} %get-tuple-element.94.part_ref, ...), custom_call_target="tpu_custom_call" | custom-call | flops 3000000000 | bytes 10000000 | tf_op jit(solution)/shard_map/feed/pallas_call | solution.py:1304
  120.4 2.0 collective-permute-done.16.got_ref
  122.4 7.2 %feed_back.1 = (bf16[2,128,768]{2,1,0:T(8,128)(2,1)}, bf16[2,2,768]{2,1,0:T(2,128)(2,1)}, f32[528,768]{1,0:T(8,128)S(1)}, bf16[528,768]{1,0:T(8,128)(2,1)S(1)}, ...) custom-call(s32[1]{0:T(128)} %bitcast.half_ref, ...), custom_call_target="tpu_custom_call" | custom-call | flops 3000000000 | bytes 10000000 | tf_op jit(solution)/shard_map/feed_back/pallas_call | solution.py:1326
  129.6 1.2 copy-done.14
  131.1 7.5 %feed_grads.1.grads_in = bf16[29440,128]{1,0:T(8,128)(2,1)S(1)} custom-call(s32[224]{0:T(256)S(1)} %get-tuple-element.153.place_ref, bf16[528,1536]{1,0:T(8,128)(2,1)S(1)} %get-tuple-element.109.a_ref, bf16[528,768]{1,0:T(8,128)(2,1)S(1)} %get-tuple-element.110.dxb_ref, bf16[528,768]{1,0:T(8,128)(2,1)S(1)} %get-tuple-element.111.hb_ref, ...), custom_call_target="tpu_custom_call" | custom-call | flops 3000000000 | bytes 10000000 | tf_op jit(solution)/shard_map/feed_grads/pallas_call | solution.py:1341
  138.7 27.3 %attend_back.1 = (bf16[29440,128]{1,0:T(8,128)(2,1)S(1)}, bf16[528,384]{1,0:T(8,128)(2,1)S(1)}, bf16[1024,768]{1,0:T(8,128)(2,1)S(1)}, f32[528,768]{1,0:T(8,128)S(1)}, bf16[192,384]{1,0:T(8,128)(2,1)S(1)}) custom-call(s32[1]{0:T(128)} %bitcast.2.block_ref, s32[224]{0:T(256)S(1)} %get-tuple-element.153.place_ref, ...), custom_call_target="tpu_custom_call", output_to_operand_aliasing={{0}: (18, {})} | custom-call | flops 8000000000 | bytes 20000000 | tf_op jit(solution)/shard_map/attend_back/pallas_call | solution.py:1376
  166.2 0.7 collective-permute-start.19
  166.9 1.0 collective-permute-start.18
  167.9 1.5 collective-permute-start.20
  169.4 27.0 %collective-permute-done.21.refs_5_ = bf16[192,384]{1,0:T(8,128)(2,1)S(1)} collective-permute-done((bf16[192,384]{1,0:T(8,128)(2,1)S(1)}, bf16[192,384]{1,0:T(8,128)(2,1)S(1)}, u32[]{:S(2)}, u32[]{:S(2)}) %collective-permute-start.21) | collective-permute-done | bytes 147488 | tf_op jit(solution)/shard_map/ppermute | solution.py:34
  196.8 2.3 add_rows.7
  199.1 1.1 collective-permute-start.22
  200.2 1.3 collective-permute-start.23
  201.5 1.0 collective-permute-start.24
  203.0 1.9 add_rows.6
  204.9 12.3 %collective-permute-done.25.refs_7_ = bf16[192,384]{1,0:T(8,128)(2,1)S(1)} collective-permute-done((bf16[192,384]{1,0:T(8,128)(2,1)S(1)}, bf16[192,384]{1,0:T(8,128)(2,1)S(1)}, u32[]{:S(2)}, u32[]{:S(2)}) %collective-permute-start.25) | collective-permute-done | bytes 147488 | tf_op jit(solution)/shard_map/ppermute | solution.py:34
  217.2 1.5 add_rows.9
  219.0 1.0 collective-permute-start.27
  220.0 0.6 collective-permute-start.28
  220.6 0.9 collective-permute-start.29
  221.5 1.1 add_rows.8
  222.6 5.7 %collective-permute-done.29.refs_7_ = bf16[192,384]{1,0:T(8,128)(2,1)S(1)} collective-permute-done((bf16[192,384]{1,0:T(8,128)(2,1)S(1)}, bf16[192,384]{1,0:T(8,128)(2,1)S(1)}, u32[]{:S(2)}, u32[]{:S(2)}) %collective-permute-start.29) | collective-permute-done | bytes 147488 | tf_op jit(solution)/shard_map/ppermute | solution.py:34
  228.3 2.9 add_rows.10
  231.2 0.7 collective-permute-start.33
  231.8 4.4 %collective-permute-start.30 = (bf16[192,768]{1,0:T(8,128)(2,1)S(1)}, bf16[192,768]{1,0:T(8,128)(2,1)S(1)}, u32[]{:S(2)}, u32[]{:S(2)}) collective-permute-start(bf16[192,768]{1,0:T(8,128)(2,1)S(1)} %get-tuple-element.131), channel_id=1, source_target_pairs={{2,0},{4,2},{6,4},{8,6},{10,8},{12,10},{14,12},{16,14},{18,16},{20... | collective-permute-start | bytes 884744 | tf_op jit(solution)/shard_map/ppermute | solution.py:1422
  236.2 1.9 collective-permute-start.31
  238.2 19.9 %collective-permute-done.30.next_ref = bf16[192,768]{1,0:T(8,128)(2,1)S(1)} collective-permute-done((bf16[192,768]{1,0:T(8,128)(2,1)S(1)}, bf16[192,768]{1,0:T(8,128)(2,1)S(1)}, u32[]{:S(2)}, u32[]{:S(2)}) %collective-permute-start.30) | collective-permute-done | bytes 294944 | tf_op jit(solution)/shard_map/ppermute | solution.py:1422
  258.1 3.6 %collective-permute-done.31.last_ref = bf16[192,768]{1,0:T(8,128)(2,1)S(1)} collective-permute-done((bf16[192,768]{1,0:T(8,128)(2,1)S(1)}, bf16[192,768]{1,0:T(8,128)(2,1)S(1)}, u32[]{:S(2)}, u32[]{:S(2)}) %collective-permute-start.31) | collective-permute-done | bytes 294944 | tf_op jit(solution)/shard_map/ppermute | solution.py:1423
  261.7 2.9 dx_long.1
  264.6 0.9 collective-permute-start.32
  265.5 1.6 add_rows.11.kept_ref
  267.2 0.9 dx_glob.1
  270.1 26.9 %soap.1 = (f32[14,128,128]{2,1,0:T(8,128)}, f32[14,128,128]{2,1,0:T(8,128)}, f32[14,128,128]{2,1,0:T(8,128)}, f32[14,128,128]{2,1,0:T(8,128)}, f32[14,128,128]{2...) custom-call(bf16[1840,128]{1,0:T(8,128)(2,1)S(1)} %add_rows.11.kept_, ...), custom_call_target="tpu_custom_call" | custom-call | flops 1174405120 | bytes 13762560 | tf_op jit(solution)/shard_map/soap/pallas_call | solution.py:432
  297.0 0.6 convert_add_fusion.1
  297.6 0.9 convert_add_fusion
  (134 shorter events, 7.2 us)
Async XLA Ops:
  0.7 6.4 %copy-start.27 = (bf16[2,2,768]{2,1,0:T(2,128)(2,1)S(1)}, bf16[2,2,768]{2,1,0:T(2,128)(2,1)}, u32[]{:S(2)}) copy-start(bf16[2,2,768]{2,1,0:T(2,128)(2,1)} %param.20) | copy-start | bytes 18436
  0.7 6.4 %copy-start.22 = (bf16[2,128,768]{2,1,0:T(8,128)(2,1)S(1)}, bf16[2,128,768]{2,1,0:T(8,128)(2,1)}, u32[]{:S(2)}) copy-start(bf16[2,128,768]{2,1,0:T(8,128)(2,1)} %param.19) | copy-start | bytes 1179652
  0.7 6.4 %copy-start.29 = (bf16[2,2,768]{2,1,0:T(2,128)(2,1)S(1)}, bf16[2,2,768]{2,1,0:T(2,128)(2,1)}, u32[]{:S(2)}) copy-start(bf16[2,2,768]{2,1,0:T(2,128)(2,1)} %param.23) | copy-start | bytes 18436
  0.7 6.4 %copy-start.25 = (bf16[2,128,768]{2,1,0:T(8,128)(2,1)S(1)}, bf16[2,128,768]{2,1,0:T(8,128)(2,1)}, u32[]{:S(2)}) copy-start(bf16[2,128,768]{2,1,0:T(8,128)(2,1)} %param.22) | copy-start | bytes 1179652
  0.7 7.9 %collective-permute-start.4 = (bf16[2,2,768]{2,1,0:T(2,128)(2,1)}, bf16[2,2,768]{2,1,0:T(2,128)(2,1)S(1)}, u32[]{:S(2)}, u32[]{:S(2)}) collective-permute-start(bf16[2,2,768]{2,1,0:T(2,128)(2,1)} %param.20), channel_id=1, source_target_pairs={{0,1},{1,0},{2,3},{3,2},{4,5},{5,4},{6,7},{7,6},{8,9},{9,8},{10,11... | collective-permute-start | bytes 18440 | tf_op jit(solution)/shard_map/ppermute | solution.py:1089
  2.5 5.9 %copy-start.32 = (s32[224]{0:T(256)S(1)}, s32[224]{0:T(256)}, u32[]{:S(2)}) copy-start(s32[224]{0:T(256)} %param.24) | copy-start | bytes 2692
  2.5 41.4 %collective-permute-start.1 = (bf16[2,96,768]{2,1,0:T(8,128)(2,1)S(1)}, bf16[2,96,768]{2,1,0:T(8,128)(2,1)S(1)}, u32[]{:S(2)}, u32[]{:S(2)}) collective-permute-start(bf16[2,96,768]{2,1,0:T(8,128)(2,1)S(1)} %slice_select_fusion), channel_id=1, source_target_pairs={{1,3},{3,5},{5,7},{7,9},{9,11},{11,13},{13,15},{15,17},{17,19},{19... | collective-permute-start | bytes 884744 | tf_op jit(solution)/shard_map/ppermute | solution.py:1212
  6.9 28.2 %copy-start.33 = (s32[2,1,256]{2,1,0:T(1,128)S(1)}, s32[2,1,256]{2,1,0:T(1,128)}, u32[]{:S(2)}) copy-start(s32[2,1,256]{2,1,0:T(1,128)} %param.21) | copy-start | bytes 6148
  6.9 28.2 %copy-start.2 = (f32[169,384]{1,0:T(8,128)S(1)}, f32[169,384]{1,0:T(8,128)}, u32[]{:S(2)}) copy-start(f32[169,384]{1,0:T(8,128)} %refs_7_.1) | copy-start | bytes 778756
  7.0 20.8 %collective-permute-start.3 = (bf16[1792,128]{1,0:T(8,128)(2,1)S(1)}, bf16[1792,128]{1,0:T(8,128)(2,1)S(1)}, u32[]{:S(2)}, u32[]{:S(2)}) collective-permute-start(bf16[1792,128]{1,0:T(8,128)(2,1)S(1)} %bitcast.18), channel_id=1, source_target_pairs={{0,16},{2,18},{4,20},{6,22},{8,24},{10,26},{12,28},{14,30},{16,0},... | collective-permute-start | bytes 1376264 | tf_op jit(solution)/shard_map/ppermute | solution.py:34
  7.2 57.9 %collective-permute-start = (bf16[2,260,768]{2,1,0:T(8,128)(2,1)S(1)}, bf16[2,260,768]{2,1,0:T(8,128)(2,1)}, u32[]{:S(2)}, u32[]{:S(2)}) collective-permute-start(bf16[2,260,768]{2,1,0:T(8,128)(2,1)S(1)} %pad_maximum_fusion), channel_id=1, source_target_pairs={{0,1},{1,0},{2,3},{3,2},{4,5},{5,4},{6,7},{7,6},{8,9},{9,8},{10,11... | collective-permute-start | bytes 2396168 | tf_op jit(solution)/shard_map/ppermute | solution.py:1089
  8.7 19.1 %collective-permute-start.5 = (bf16[48,128]{1,0:T(8,128)(2,1)S(1)}, bf16[48,128]{1,0:T(8,128)(2,1)S(1)}, u32[]{:S(2)}, u32[]{:S(2)}) collective-permute-start(bf16[48,128]{1,0:T(8,128)(2,1)S(1)} %reshape.127.refs_2_), channel_id=1, source_target_pairs={{0,16},{2,18},{4,20},{6,22},{8,24},{10,26},{12,28},{14,30},{16,0},... | collective-permute-start | bytes 36872 | tf_op jit(solution)/shard_map/ppermute | solution.py:34
  29.1 6.8 %collective-permute-start.8 = (bf16[1120,128]{1,0:T(8,128)(2,1)S(1)}, bf16[1120,128]{1,0:T(8,128)(2,1)S(1)}, u32[]{:S(2)}, u32[]{:S(2)}) collective-permute-start(bf16[1120,128]{1,0:T(8,128)(2,1)S(1)} %get-tuple-element.87.refs_4_), channel_id=1, source_target_pairs={{0,4},{2,6},{4,0},{6,2},{8,12},{10,14},{12,8},{14,10},{16,20},{18,... | collective-permute-start | bytes 860168 | tf_op jit(solution)/shard_map/ppermute | solution.py:34
  29.6 12.3 %collective-permute-start.6 = (bf16[1280,128]{1,0:T(8,128)(2,1)S(1)}, bf16[1280,128]{1,0:T(8,128)(2,1)S(1)}, u32[]{:S(2)}, u32[]{:S(2)}) collective-permute-start(bf16[1280,128]{1,0:T(8,128)(2,1)S(1)} %get-tuple-element.85.refs_0_), channel_id=1, source_target_pairs={{0,8},{2,10},{4,12},{6,14},{8,0},{10,2},{12,4},{14,6},{16,24},{18,... | collective-permute-start | bytes 983048 | tf_op jit(solution)/shard_map/ppermute | solution.py:34
  34.5 8.2 %collective-permute-start.7 = (bf16[1280,128]{1,0:T(8,128)(2,1)S(1)}, bf16[1280,128]{1,0:T(8,128)(2,1)S(1)}, u32[]{:S(2)}, u32[]{:S(2)}) collective-permute-start(bf16[1280,128]{1,0:T(8,128)(2,1)S(1)} %get-tuple-element.86.refs_2_), channel_id=1, source_target_pairs={{0,2},{2,0},{4,6},{6,4},{8,10},{10,8},{12,14},{14,12},{16,18},{18,... | collective-permute-start | bytes 983048 | tf_op jit(solution)/shard_map/ppermute | solution.py:34
  43.3 17.5 %collective-permute-start.9 = (bf16[2560,128]{1,0:T(8,128)(2,1)S(1)}, bf16[2560,128]{1,0:T(8,128)(2,1)S(1)}, u32[]{:S(2)}, u32[]{:S(2)}) collective-permute-start(bf16[2560,128]{1,0:T(8,128)(2,1)S(1)} %get-tuple-element.88.refs_0_), channel_id=1, source_target_pairs={{0,4},{2,6},{4,0},{6,2},{8,12},{10,14},{12,8},{14,10},{16,20},{18,... | collective-permute-start | bytes 1966088 | tf_op jit(solution)/shard_map/ppermute | solution.py:34
  43.5 17.2 %collective-permute-start.10 = (bf16[2560,128]{1,0:T(8,128)(2,1)S(1)}, bf16[2560,128]{1,0:T(8,128)(2,1)S(1)}, u32[]{:S(2)}, u32[]{:S(2)}) collective-permute-start(bf16[2560,128]{1,0:T(8,128)(2,1)S(1)} %get-tuple-element.89.refs_2_), channel_id=1, source_target_pairs={{0,8},{2,10},{4,12},{6,14},{8,0},{10,2},{12,4},{14,6},{16,24},{18,... | collective-permute-start | bytes 1966088 | tf_op jit(solution)/shard_map/ppermute | solution.py:34
  43.9 3.6 %collective-permute-start.2 = (bf16[2,96,768]{2,1,0:T(8,128)(2,1)S(1)}, bf16[2,96,768]{2,1,0:T(8,128)(2,1)S(1)}, u32[]{:S(2)}, u32[]{:S(2)}) collective-permute-start(bf16[2,96,768]{2,1,0:T(8,128)(2,1)S(1)} %collective-permute-done.1), channel_id=1, source_target_pairs={{0,1},{1,0},{2,3},{3,2},{4,5},{5,4},{6,7},{7,6},{8,9},{9,8},{10,11... | collective-permute-start | bytes 884744 | tf_op jit(solution)/shard_map/ppermute | solution.py:1089
  46.2 14.6 %collective-permute-start.11 = (bf16[2240,128]{1,0:T(8,128)(2,1)S(1)}, bf16[2240,128]{1,0:T(8,128)(2,1)S(1)}, u32[]{:S(2)}, u32[]{:S(2)}) collective-permute-start(bf16[2240,128]{1,0:T(8,128)(2,1)S(1)} %get-tuple-element.90.refs_4_), channel_id=1, source_target_pairs={{0,2},{2,0},{4,6},{6,4},{8,10},{10,8},{12,14},{14,12},{16,18},{18,... | collective-permute-start | bytes 1720328 | tf_op jit(solution)/shard_map/ppermute | solution.py:34
  47.5 17.6 %copy-start.23 = (bf16[2,128,768]{2,1,0:T(8,128)(2,1)S(1)}, bf16[2,128,768]{2,1,0:T(8,128)(2,1)}, u32[]{:S(2)}) copy-start(bf16[2,128,768]{2,1,0:T(8,128)(2,1)} %param.19) | copy-start | bytes 1179652
  47.6 17.6 %copy-start.26 = (bf16[2,128,768]{2,1,0:T(8,128)(2,1)S(1)}, bf16[2,128,768]{2,1,0:T(8,128)(2,1)}, u32[]{:S(2)}) copy-start(bf16[2,128,768]{2,1,0:T(8,128)(2,1)} %param.22) | copy-start | bytes 1179652
  47.6 17.5 %copy-start.28 = (bf16[2,2,768]{2,1,0:T(2,128)(2,1)S(1)}, bf16[2,2,768]{2,1,0:T(2,128)(2,1)}, u32[]{:S(2)}) copy-start(bf16[2,2,768]{2,1,0:T(2,128)(2,1)} %param.20) | copy-start | bytes 18436
  47.6 17.5 %copy-start.30 = (bf16[2,2,768]{2,1,0:T(2,128)(2,1)S(1)}, bf16[2,2,768]{2,1,0:T(2,128)(2,1)}, u32[]{:S(2)}) copy-start(bf16[2,2,768]{2,1,0:T(2,128)(2,1)} %param.23) | copy-start | bytes 18436
  63.3 29.6 %collective-permute-start.12 = (bf16[5120,128]{1,0:T(8,128)(2,1)S(1)}, bf16[5120,128]{1,0:T(8,128)(2,1)}, u32[]{:S(2)}, u32[]{:S(2)}) collective-permute-start(bf16[5120,128]{1,0:T(8,128)(2,1)S(1)} %get-tuple-element.91), channel_id=1, source_target_pairs={{0,2},{2,0},{4,6},{6,4},{8,10},{10,8},{12,14},{14,12},{16,18},{18,... | collective-permute-start | bytes 3932168 | tf_op jit(solution)/shard_map/ppermute | solution.py:34
  64.5 29.5 %collective-permute-start.13 = (bf16[5120,128]{1,0:T(8,128)(2,1)}, bf16[5120,128]{1,0:T(8,128)(2,1)}, u32[]{:S(2)}, u32[]{:S(2)}) collective-permute-start(bf16[5120,128]{1,0:T(8,128)(2,1)} %get-tuple-element.92), channel_id=1, source_target_pairs={{0,4},{2,6},{4,0},{6,2},{8,12},{10,14},{12,8},{14,10},{16,20},{18,... | collective-permute-start | bytes 3932168 | tf_op jit(solution)/shard_map/ppermute | solution.py:34
  66.6 25.7 %collective-permute-start.14 = (bf16[4480,128]{1,0:T(8,128)(2,1)}, bf16[4480,128]{1,0:T(8,128)(2,1)}, u32[]{:S(2)}, u32[]{:S(2)}) collective-permute-start(bf16[4480,128]{1,0:T(8,128)(2,1)} %get-tuple-element.93), channel_id=1, source_target_pairs={{0,8},{2,10},{4,12},{6,14},{8,0},{10,2},{12,4},{14,6},{16,24},{18,... | collective-permute-start | bytes 3440648 | tf_op jit(solution)/shard_map/ppermute | solution.py:34
  94.0 20.6 %copy-start.11 = (f32[4,768]{1,0:T(4,128)S(1)}, f32[4,768]{1,0:T(4,128)}, u32[]{:S(2)}) copy-start(f32[4,768]{1,0:T(4,128)} %refs_10_.1) | copy-start | bytes 36868
  110.5 9.5 %copy-start.16 = (bf16[1024,768]{1,0:T(8,128)(2,1)}, bf16[1024,768]{1,0:T(8,128)(2,1)S(1)}, u32[]{:S(2)}) copy-start(bf16[1024,768]{1,0:T(8,128)(2,1)S(1)} %get-tuple-element.108.xe_ref) | copy-start | bytes 4718596
  110.5 9.5 %copy-start.18 = (bf16[1024,384]{1,0:T(8,128)(2,1)}, bf16[1024,384]{1,0:T(8,128)(2,1)S(1)}, u32[]{:S(2)}) copy-start(bf16[1024,384]{1,0:T(8,128)(2,1)S(1)} %get-tuple-element.107.v_ref) | copy-start | bytes 2359300
  110.5 9.5 %copy-start.20 = (bf16[528,384]{1,0:T(8,128)(2,1)}, bf16[528,384]{1,0:T(8,128)(2,1)S(1)}, u32[]{:S(2)}) copy-start(bf16[528,384]{1,0:T(8,128)(2,1)S(1)} %get-tuple-element.104.o_ref) | copy-start | bytes 1216516
  110.5 11.8 %copy-start = (bf16[4992,768]{1,0:T(8,128)(2,1)}, bf16[4992,768]{1,0:T(8,128)(2,1)S(1)}, u32[]{:S(2)}) copy-start(bf16[4992,768]{1,0:T(8,128)(2,1)S(1)} %get-tuple-element.95.wu_ref.wd_ref.wo_ref.wall_ref) | copy-start | bytes 23003140
  110.5 4.1 %collective-permute-start.15 = (bf16[528,768]{1,0:T(8,128)(2,1)S(1)}, bf16[528,768]{1,0:T(8,128)(2,1)S(1)}, u32[]{:S(2)}, u32[]{:S(2)}) collective-permute-start(bf16[528,768]{1,0:T(8,128)(2,1)S(1)} %get-tuple-element.94.part_ref), channel_id=1, source_target_pairs={{0,1},{1,0},{2,3},{3,2},{4,5},{5,4},{6,7},{7,6},{8,9},{9,8},{10,11... | collective-permute-start | bytes 2433032 | tf_op jit(solution)/shard_map/ppermute | solution.py:1089
  120.0 2.4 collective-permute-start.16
  130.8 7.9 %collective-permute-start.17 = (bf16[528,768]{1,0:T(8,128)(2,1)S(1)}, bf16[528,768]{1,0:T(8,128)(2,1)S(1)}, u32[]{:S(2)}, u32[]{:S(2)}) collective-permute-start(bf16[528,768]{1,0:T(8,128)(2,1)S(1)} %get-tuple-element.102.dh_ref), channel_id=1, source_target_pairs={{0,1},{1,0},{2,3},{3,2},{4,5},{5,4},{6,7},{7,6},{8,9},{9,8},{10,11... | collective-permute-start | bytes 2433032 | tf_op jit(solution)/shard_map/ppermute | solution.py:1089
  131.1 7.6 %copy-start.15 = (f32[528,768]{1,0:T(8,128)S(1)}, f32[528,768]{1,0:T(8,128)}, u32[]{:S(2)}) copy-start(f32[528,768]{1,0:T(8,128)} %copy-done.14) | copy-start | bytes 4866052
  131.1 7.6 %copy-start.17 = (bf16[1024,768]{1,0:T(8,128)(2,1)S(1)}, bf16[1024,768]{1,0:T(8,128)(2,1)}, u32[]{:S(2)}) copy-start(bf16[1024,768]{1,0:T(8,128)(2,1)} %copy-done.16) | copy-start | bytes 4718596
  131.1 7.6 %copy-start.19 = (bf16[1024,384]{1,0:T(8,128)(2,1)S(1)}, bf16[1024,384]{1,0:T(8,128)(2,1)}, u32[]{:S(2)}) copy-start(bf16[1024,384]{1,0:T(8,128)(2,1)} %copy-done.18) | copy-start | bytes 2359300
  131.1 7.6 %copy-start.21 = (bf16[528,384]{1,0:T(8,128)(2,1)S(1)}, bf16[528,384]{1,0:T(8,128)(2,1)}, u32[]{:S(2)}) copy-start(bf16[528,384]{1,0:T(8,128)(2,1)} %copy-done.20) | copy-start | bytes 1216516
  166.2 30.4 %collective-permute-start.19 = (bf16[5120,128]{1,0:T(8,128)(2,1)S(1)}, bf16[5120,128]{1,0:T(8,128)(2,1)S(1)}, u32[]{:S(2)}, u32[]{:S(2)}) collective-permute-start(bf16[5120,128]{1,0:T(8,128)(2,1)S(1)} %get-tuple-element.155), channel_id=1, source_target_pairs={{0,4},{2,6},{4,0},{6,2},{8,12},{10,14},{12,8},{14,10},{16,20},{18,... | collective-permute-start | bytes 3932168 | tf_op jit(solution)/shard_map/ppermute | solution.py:34
  166.9 29.9 %collective-permute-start.18 = (bf16[5120,128]{1,0:T(8,128)(2,1)S(1)}, bf16[5120,128]{1,0:T(8,128)(2,1)S(1)}, u32[]{:S(2)}, u32[]{:S(2)}) collective-permute-start(bf16[5120,128]{1,0:T(8,128)(2,1)S(1)} %get-tuple-element.156), channel_id=1, source_target_pairs={{0,2},{2,0},{4,6},{6,4},{8,10},{10,8},{12,14},{14,12},{16,18},{18,... | collective-permute-start | bytes 3932168 | tf_op jit(solution)/shard_map/ppermute | solution.py:34
  167.9 28.7 %collective-permute-start.20 = (bf16[4480,128]{1,0:T(8,128)(2,1)S(1)}, bf16[4480,128]{1,0:T(8,128)(2,1)S(1)}, u32[]{:S(2)}, u32[]{:S(2)}) collective-permute-start(bf16[4480,128]{1,0:T(8,128)(2,1)S(1)} %slice.51), channel_id=1, source_target_pairs={{0,8},{2,10},{4,12},{6,14},{8,0},{10,2},{12,4},{14,6},{16,24},{18,... | collective-permute-start | bytes 3440648 | tf_op jit(solution)/shard_map/ppermute | solution.py:34
  169.4 27.0 %collective-permute-start.21 = (bf16[192,384]{1,0:T(8,128)(2,1)S(1)}, bf16[192,384]{1,0:T(8,128)(2,1)S(1)}, u32[]{:S(2)}, u32[]{:S(2)}) collective-permute-start(bf16[192,384]{1,0:T(8,128)(2,1)S(1)} %get-tuple-element.117.refs_4_), channel_id=1, source_target_pairs={{0,16},{2,18},{4,20},{6,22},{8,24},{10,26},{12,28},{14,30},{16,0},... | collective-permute-start | bytes 442376 | tf_op jit(solution)/shard_map/ppermute | solution.py:34
  199.1 18.1 %collective-permute-start.22 = (bf16[2560,128]{1,0:T(8,128)(2,1)S(1)}, bf16[2560,128]{1,0:T(8,128)(2,1)S(1)}, u32[]{:S(2)}, u32[]{:S(2)}) collective-permute-start(bf16[2560,128]{1,0:T(8,128)(2,1)S(1)} %get-tuple-element.118), channel_id=1, source_target_pairs={{0,4},{2,6},{4,0},{6,2},{8,12},{10,14},{12,8},{14,10},{16,20},{18,... | collective-permute-start | bytes 1966088 | tf_op jit(solution)/shard_map/ppermute | solution.py:34
  200.2 17.1 %collective-permute-start.23 = (bf16[2560,128]{1,0:T(8,128)(2,1)S(1)}, bf16[2560,128]{1,0:T(8,128)(2,1)S(1)}, u32[]{:S(2)}, u32[]{:S(2)}) collective-permute-start(bf16[2560,128]{1,0:T(8,128)(2,1)S(1)} %get-tuple-element.120), channel_id=1, source_target_pairs={{0,8},{2,10},{4,12},{6,14},{8,0},{10,2},{12,4},{14,6},{16,24},{18,... | collective-permute-start | bytes 1966088 | tf_op jit(solution)/shard_map/ppermute | solution.py:34
  201.5 15.7 %collective-permute-start.24 = (bf16[2240,128]{1,0:T(8,128)(2,1)S(1)}, bf16[2240,128]{1,0:T(8,128)(2,1)S(1)}, u32[]{:S(2)}, u32[]{:S(2)}) collective-permute-start(bf16[2240,128]{1,0:T(8,128)(2,1)S(1)} %get-tuple-element.122), channel_id=1, source_target_pairs={{0,2},{2,0},{4,6},{6,4},{8,10},{10,8},{12,14},{14,12},{16,18},{18,... | collective-permute-start | bytes 1720328 | tf_op jit(solution)/shard_map/ppermute | solution.py:34
  202.6 14.7 %collective-permute-start.25 = (bf16[192,384]{1,0:T(8,128)(2,1)S(1)}, bf16[192,384]{1,0:T(8,128)(2,1)S(1)}, u32[]{:S(2)}, u32[]{:S(2)}) collective-permute-start(bf16[192,384]{1,0:T(8,128)(2,1)S(1)} %get-tuple-element.124.refs_6_), channel_id=1, source_target_pairs={{0,2},{2,0},{4,6},{6,4},{8,10},{10,8},{12,14},{14,12},{16,18},{18,... | collective-permute-start | bytes 442376 | tf_op jit(solution)/shard_map/ppermute | solution.py:34
  203.0 58.7 %slice-start = ((s8[7667712]{0:T(1024)(128)(4,1)}), s8[4194304]{0:T(1024)(128)(4,1)S(1)}, s32[]{:S(2)}) async-start(s8[7667712]{0:T(1024)(128)(4,1)} %bitcast.16), calls=%async_computation | async-start | bytes 8388608
  217.2 44.4 %slice-start.1 = ((s8[7667712]{0:T(1024)(128)(4,1)}), s8[3473408]{0:T(1024)(128)(4,1)S(1)}, s32[]{:S(2)}) async-start(s8[7667712]{0:T(1024)(128)(4,1)} %bitcast.16), calls=%async_computation.1 | async-start | bytes 6946816
  218.8 9.5 %collective-permute-start.26 = (bf16[1280,128]{1,0:T(8,128)(2,1)S(1)}, bf16[1280,128]{1,0:T(8,128)(2,1)S(1)}, u32[]{:S(2)}, u32[]{:S(2)}) collective-permute-start(bf16[1280,128]{1,0:T(8,128)(2,1)S(1)} %get-tuple-element.125), channel_id=1, source_target_pairs={{0,8},{2,10},{4,12},{6,14},{8,0},{10,2},{12,4},{14,6},{16,24},{18,... | collective-permute-start | bytes 983048 | tf_op jit(solution)/shard_map/ppermute | solution.py:34
  219.0 9.2 %collective-permute-start.27 = (bf16[1280,128]{1,0:T(8,128)(2,1)S(1)}, bf16[1280,128]{1,0:T(8,128)(2,1)S(1)}, u32[]{:S(2)}, u32[]{:S(2)}) collective-permute-start(bf16[1280,128]{1,0:T(8,128)(2,1)S(1)} %get-tuple-element.127), channel_id=1, source_target_pairs={{0,2},{2,0},{4,6},{6,4},{8,10},{10,8},{12,14},{14,12},{16,18},{18,... | collective-permute-start | bytes 983048 | tf_op jit(solution)/shard_map/ppermute | solution.py:34
  220.0 8.2 %collective-permute-start.28 = (bf16[1120,128]{1,0:T(8,128)(2,1)S(1)}, bf16[1120,128]{1,0:T(8,128)(2,1)S(1)}, u32[]{:S(2)}, u32[]{:S(2)}) collective-permute-start(bf16[1120,128]{1,0:T(8,128)(2,1)S(1)} %get-tuple-element.129), channel_id=1, source_target_pairs={{0,4},{2,6},{4,0},{6,2},{8,12},{10,14},{12,8},{14,10},{16,20},{18,... | collective-permute-start | bytes 860168 | tf_op jit(solution)/shard_map/ppermute | solution.py:34
  220.6 7.6 %collective-permute-start.29 = (bf16[192,384]{1,0:T(8,128)(2,1)S(1)}, bf16[192,384]{1,0:T(8,128)(2,1)S(1)}, u32[]{:S(2)}, u32[]{:S(2)}) collective-permute-start(bf16[192,384]{1,0:T(8,128)(2,1)S(1)} %get-tuple-element.130.refs_6_), channel_id=1, source_target_pairs={{0,4},{2,6},{4,0},{6,2},{8,12},{10,14},{12,8},{14,10},{16,20},{18,... | collective-permute-start | bytes 442376 | tf_op jit(solution)/shard_map/ppermute | solution.py:34
  231.2 36.0 %collective-permute-start.33 = (bf16[1840,128]{1,0:T(8,128)(2,1)S(1)}, bf16[1840,128]{1,0:T(8,128)(2,1)S(1)}, u32[]{:S(2)}, u32[]{:S(2)}) collective-permute-start(bf16[1840,128]{1,0:T(8,128)(2,1)S(1)} %get-tuple-element.136), channel_id=1, source_target_pairs={{0,16},{2,18},{4,20},{6,22},{8,24},{10,26},{12,28},{14,30},{16,0},... | collective-permute-start | bytes 1413128 | tf_op jit(solution)/shard_map/ppermute | solution.py:34
  231.8 26.3 %collective-permute-start.30 = (bf16[192,768]{1,0:T(8,128)(2,1)S(1)}, bf16[192,768]{1,0:T(8,128)(2,1)S(1)}, u32[]{:S(2)}, u32[]{:S(2)}) collective-permute-start(bf16[192,768]{1,0:T(8,128)(2,1)S(1)} %get-tuple-element.131), channel_id=1, source_target_pairs={{2,0},{4,2},{6,4},{8,6},{10,8},{12,10},{14,12},{16,14},{18,16},{20... | collective-permute-start | bytes 884744 | tf_op jit(solution)/shard_map/ppermute | solution.py:1422
  236.2 25.4 %collective-permute-start.31 = (bf16[192,768]{1,0:T(8,128)(2,1)S(1)}, bf16[192,768]{1,0:T(8,128)(2,1)S(1)}, u32[]{:S(2)}, u32[]{:S(2)}) collective-permute-start(bf16[192,768]{1,0:T(8,128)(2,1)S(1)} %get-tuple-element.132), channel_id=1, source_target_pairs={{0,2},{2,4},{4,6},{6,8},{8,10},{10,12},{12,14},{14,16},{16,18},{18... | collective-permute-start | bytes 884744 | tf_op jit(solution)/shard_map/ppermute | solution.py:1423
  238.2 30.1 %collective-permute-start.35 = (bf16[192,384]{1,0:T(8,128)(2,1)S(1)}, bf16[192,384]{1,0:T(8,128)(2,1)S(1)}, u32[]{:S(2)}, u32[]{:S(2)}) collective-permute-start(bf16[192,384]{1,0:T(8,128)(2,1)S(1)} %get-tuple-element.139.small_ref), channel_id=1, source_target_pairs={{0,8},{2,10},{4,12},{6,14},{8,0},{10,2},{12,4},{14,6},{16,24},{18,... | collective-permute-start | bytes 442376 | tf_op jit(solution)/shard_map/ppermute | solution.py:34
  264.6 33.0 %collective-permute-start.32 = (bf16[2,128,768]{2,1,0:T(8,128)(2,1)S(1)}, bf16[2,128,768]{2,1,0:T(8,128)(2,1)S(1)}, u32[]{:S(2)}, u32[]{:S(2)}) collective-permute-start(bf16[2,128,768]{2,1,0:T(8,128)(2,1)S(1)} %get-tuple-element.135), channel_id=1, source_target_pairs={{0,1},{1,0},{2,3},{3,2},{4,5},{5,4},{6,7},{7,6},{8,9},{9,8},{10,11... | collective-permute-start | bytes 1179656 | tf_op jit(solution)/shard_map/ppermute | solution.py:1089
  267.1 2.5 copy-start.7
  267.2 2.8 copy-start.8
  267.2 2.8 copy-start.9
  267.2 2.9 copy-start.10
  267.2 2.9 copy-start.12
  267.2 2.8 copy-start.13
  268.2 28.8 %collective-permute-start.34 = (bf16[2,2,768]{2,1,0:T(2,128)(2,1)S(1)}, bf16[2,2,768]{2,1,0:T(2,128)(2,1)S(1)}, u32[]{:S(2)}, u32[]{:S(2)}) collective-permute-start(bf16[2,2,768]{2,1,0:T(2,128)(2,1)S(1)} %get-tuple-element.138), channel_id=1, source_target_pairs={{0,1},{1,0},{2,3},{3,2},{4,5},{5,4},{6,7},{7,6},{8,9},{9,8},{10,11... | collective-permute-start | bytes 18440 | tf_op jit(solution)/shard_map/ppermute | solution.py:1089
  (8 other events, 12.0 us)
where the time goes:
time: 299 us
  waiting for transfers between devices  133 us (44%)
  Pallas kernels  110 us (37%)
  starting transfers between devices  42 us (14%)
  other arithmetic  6.39 us (2%)
  local copies, waits for them, and re-layouts  5.99 us (2%)
    ppermute x25, waiting for transfers between devices, swap_with(): return lax.ppermute(values, 'seq', [(i, i ^ bit) for i in range(count)])  105 us
    pallas_call x1, Pallas kernels, on_device(): kernel_call(functools.partial(attend_back_kernel, dims, seq_count, attn_t...  27.3 us
    pallas_call x1, Pallas kernels, soap_update(): pl.pallas_call(functools.partial(soap_kernel, npad), grid=(1,), out_shape...  26.9 us
    ppermute x25, starting transfers between devices, swap_with(): return lax.ppermute(values, 'seq', [(i, i ^ bit) for i in range(count)])  24.4 us
    ppermute x1, waiting for transfers between devices, on_device(): lax.ppermute(to_last, 'seq', [(i + 1, i) for i in range(seq_count - 1)])  19.9 us
    pallas_call x1, Pallas kernels, on_device(): kernel_call(functools.partial(attend_kernel, dims, wall_at, seq_count), '...  16.5 us
    pallas_call x9, Pallas kernels, move_rows(): pl.pallas_call(functools.partial(move_kernel, plan, len(arrays)), grid=(1...  15.7 us
    ppermute x8, starting transfers between devices, swap_cores(): return lax.ppermute(values, 'ffn', [(i, i ^ 1) for i in range(count)])  8.19 us
  transfers between devices with their start and end apart: 36, of which 16 were waited for; matrix products, arithmetic and copies ran while one was open for 3% of the time, Pallas kernels for 16%

commit v1 on v0

--- a/solution.py
+++ b/solution.py
@@ -175,7 +175,8 @@
     spans = [count * many for many in rows]
     starts = [sum(spans[:at]) for at in range(len(spans))]
     sends = [cells[a + r // 2 : a + r] for a, r in zip(starts, spans)]
-    kept = [(cells, a, r // 2) for a, r in zip(starts, spans)]
+    kept = move_rows([[(r // 2, (cells, a))] for a, r in zip(starts, spans)])
+    kept = [(keep, 0, keep.shape[0]) for keep in kept]
 
     def all_sum():
         return [run_sum(everywhere.shape[0], everywhere, 0, all_got, 0)]
@@ -251,6 +252,10 @@
 
 def dot_six(a, b, ca, cb):
     return dot_on(left_six(split_three(a), ca), right_six(split_three(b), cb), ca, cb)
+
+
+def dot_one(a, b, ca, cb):
+    return dot_on(a.astype(BF), b.astype(BF), ca, cb)
 
 
 def dot_three(a, b, ca, cb):
@@ -324,14 +329,12 @@
 
 
 def soap_kernel(npad, kept_ref, got_ref, small_ref, small_got_ref, *refs):
-    w_ref, m_ref, v_ref, ql_ref, qr_ref, sl_ref, sr_ref = refs[:7]
-    w_out, m_out, v_out, ql_out, qr_out, sl_out, sr_out = refs[13:20]
-    a_ref, y_ref, mat_ref, t_ref = refs[26:]
+    state, done = refs[:7], refs[13:20]
+    given, a_ref, y_ref, mat_ref, t_ref, out_sems = refs[26:]
+    n, side = state[0].shape[:2]
+    many = next(k for k in (7, 2, 1) if n % k == 0)
+    batch = next(b for b in (14, 7, 4, 2) if 2 * n % b == 0)
     small_updates((small_ref, small_got_ref), refs[7:13], refs[20:26])
-    n = w_ref.shape[0]
-    many = next(k for k in (2, 1) if n % k == 0)
-    batch = next(b for b in (14, 7, 4, 2) if 2 * n % b == 0)
-    side = w_ref.shape[-1]
     eye = (
         lax.broadcasted_iota(jnp.int32, (side, side), 0)
         == lax.broadcasted_iota(jnp.int32, (side, side), 1)
@@ -339,39 +342,42 @@
 
     def first(at, carry):
         slots = [at * many + k for k in range(many)]
+
+        def old(kind):
+            return [state[kind][i] for i in slots]
+
+        lefts, rights = old(3), old(4)
         tiles = [pl.ds(pl.multiple_of(i * side, side), side) for i in slots]
         grads = [kept_ref[rows, :].astype(F32) + got_ref[rows, :].astype(F32) for rows in tiles]
-        lefts = [ql_ref[i] for i in slots]
-        rights = [qr_ref[i] for i in slots]
         halves = [split_two(x) for x in grads]
         new_l = [
-            BETA_TWO * sl_ref[i] + (1.0 - BETA_TWO) * dot_on(left_three(p, 1), right_three(p, 1), 1, 1)
-            for i, p in zip(slots, halves)
+            BETA_TWO * x + (1.0 - BETA_TWO) * dot_on(left_three(p, 1), right_three(p, 1), 1, 1)
+            for x, p in zip(old(5), halves)
         ]
         new_r = [
-            BETA_TWO * sr_ref[i] + (1.0 - BETA_TWO) * dot_on(left_three(p, 0), right_three(p, 0), 0, 0)
-            for i, p in zip(slots, halves)
+            BETA_TWO * x + (1.0 - BETA_TWO) * dot_on(left_three(p, 0), right_three(p, 0), 0, 0)
+            for x, p in zip(old(6), halves)
         ]
         mats = [dot_six(x, y, 1, 0) for x, y in zip(new_l + new_r, lefts + rights)]
         thirds = [split_three(x) for x in mats]
         grams = [dot_on(left_six(p, 0), right_six(p, 0), 0, 0) for p in thirds]
-        turned = [dot_three(x, y, 0, 0) for x, y in zip(lefts, grads)]
-        rotated = [dot_three(x, y, 1, 0) for x, y in zip(turned, rights)]
-        moms = [BETA_ONE * m_ref[i] + (1.0 - BETA_ONE) * x for i, x in zip(slots, rotated)]
-        secs = [BETA_TWO * v_ref[i] + (1.0 - BETA_TWO) * x * x for i, x in zip(slots, rotated)]
+        turned = [dot_one(x, y, 0, 0) for x, y in zip(lefts, grads)]
+        rotated = [dot_one(x, y, 1, 0) for x, y in zip(turned, rights)]
+        moms = [BETA_ONE * old_m + (1.0 - BETA_ONE) * x for old_m, x in zip(old(1), rotated)]
+        secs = [BETA_TWO * old_v + (1.0 - BETA_TWO) * x * x for old_v, x in zip(old(2), rotated)]
         steps = [
             x / (1.0 - BETA_ONE**STEP) / (jnp.sqrt(y / (1.0 - BETA_TWO**STEP)) + ADAM_EPS)
             for x, y in zip(moms, secs)
         ]
-        turned = [dot_three(x, y, 1, 0) for x, y in zip(lefts, steps)]
-        backs = [dot_three(x, y, 1, 1) for x, y in zip(turned, rights)]
-        weights = [w_ref[i] for i in slots]
+        turned = [dot_one(x, y, 1, 0) for x, y in zip(lefts, steps)]
+        backs = [dot_one(x, y, 1, 1) for x, y in zip(turned, rights)]
+        weights = old(0)
         for k, i in enumerate(slots):
-            m_out[i] = moms[k]
-            v_out[i] = secs[k]
-            w_out[i] = weights[k] - LEARN_RATE * (backs[k] + WEIGHT_DECAY * weights[k])
-            sl_out[i] = new_l[k]
-            sr_out[i] = new_r[k]
+            given[0, i] = weights[k] - LEARN_RATE * (backs[k] + WEIGHT_DECAY * weights[k])
+            given[1, i] = moms[k]
+            given[2, i] = secs[k]
+            given[5, i] = new_l[k]
+            given[6, i] = new_r[k]
             for kind in range(2):
                 mat_ref[2 * i + kind] = mats[kind * many + k]
                 rows = pl.ds(pl.multiple_of((2 * i + kind) * side, side), side)
@@ -379,7 +385,14 @@
                 y_ref[rows, :] = eye
         return carry
 
+    def send(kinds):
+        copies = [pltpu.make_async_copy(given.at[k], done[k], out_sems.at[k]) for k in kinds]
+        for copy in copies:
+            copy.start()
+        return copies
+
     lax.fori_loop(0, n // many, first, 0)
+    copies = send((0, 1, 2, 5, 6))
     if npad > 2 * n:
         a_ref[2 * n * side :, :] = jnp.concatenate([eye] * (npad - 2 * n), axis=0)
     for at in range(0, side, PANEL):
@@ -417,11 +430,13 @@
         rows = [pl.ds(pl.multiple_of((2 * i + k) * side, side), side) for k in range(2)]
         turns = [y_ref[r, :] for r in rows]
         left, right = [dot_three(x, y, 1, 1) for x, y in zip(mats, turns)]
-        ql_out[i] = left
-        qr_out[i] = right
+        given[3, i] = left
+        given[4, i] = right
         return carry
 
     lax.fori_loop(0, n, last, 0)
+    for copy in copies + send((3, 4)):
+        copy.wait()
 
 
 def soap_update(grads, small, state, others):
@@ -434,12 +449,14 @@
         grid=(1,),
         out_shape=tuple(jax.ShapeDtypeStruct(s.shape, F32) for s in outs),
         in_specs=[whole(array.shape) for array in ins],
-        out_specs=tuple(whole(array.shape) for array in outs),
+        out_specs=(far_space(),) * len(state) + tuple(whole(array.shape) for array in others),
         scratch_shapes=[
+            pltpu.VMEM((7, n, side, side), F32),
             pltpu.VMEM((npad * side, side), F32),
             pltpu.VMEM((npad * side, side), F32),
             pltpu.VMEM((2 * n, side, side), F32),
             pltpu.VMEM((npad * PANEL, side), F32),
+            pltpu.SemaphoreType.DMA((7,)),
         ],
         cost_estimate=pl.CostEstimate(
             flops=n * 40 * side**3, bytes_accessed=n * 60 * side * side, transcendentals=0
@@ -598,7 +615,7 @@
     q_ref, k_ref, v_ref, o_ref, part_ref, xe_ref, wall_out, wall_ref, glob_low, glob_cells, sems = refs[-11:]
     sources = refs[:-11]
     seqs, block_len, glob_block, ext, width, globs, scale = dims
-    feed_rows, attn_rows, qk_at, v_at, out_at, tiles = wall_at
+    feed_rows, attn_rows, kv_at, q_at, out_at, tiles = wall_at
     model_dim = xr_ref.shape[1]
     head_cols = q_ref.shape[1]
     start_tiles(row_ref, col_ref, kind_ref, sources, tiles, wall_ref, sems)
@@ -636,9 +653,8 @@
     rims = xe_ref.at[pl.ds(0, 2 * seqs * RIM)]
     pltpu.make_async_copy(rims, rims, sems.at[4]).wait()
     wait_rows(wall_ref, attn_rows, sems.at[0])
-    wq_ref = wall_ref.at[pl.ds(qk_at, model_dim), pl.ds(0, head_cols)]
-    wk_ref = wall_ref.at[pl.ds(qk_at, model_dim), pl.ds(head_cols, head_cols)]
-    wv_ref = wall_ref.at[pl.ds(v_at, model_dim), pl.ds(0, head_cols)]
+    wq_ref = wall_ref.at[pl.ds(q_at, model_dim), pl.ds(0, head_cols)]
+    wkv_ref = wall_ref.at[pl.ds(kv_at, model_dim)]
     wo_ref = wall_ref.at[pl.ds(out_at, head_cols)]
     pairs = head_cols // LANES
     glob_at = seqs * block_len
@@ -649,8 +665,9 @@
 
     def project(i, carry):
         rows = pl.ds(pl.multiple_of(i * 256, 256), 256)
-        k_ref[rows, :] = dot_on(xe_ref[rows, :], wk_ref[...], 1, 0).astype(BF)
-        v_ref[rows, :] = dot_on(xe_ref[rows, :], wv_ref[...], 1, 0).astype(BF)
+        both = dot_on(xe_ref[rows, :], wkv_ref[...], 1, 0).astype(BF)
+        k_ref[rows, :] = both[:, :head_cols]
+        v_ref[rows, :] = both[:, head_cols:]
         return carry
 
     lax.fori_loop(0, seqs * span // 256, project, 0)
@@ -664,31 +681,35 @@
         base = pl.multiple_of(seq * span, LANES)
         at = pl.multiple_of(chunk * LANES, LANES)
         bias = window_bias(block_ref[0], blocks, chunk, dims)
-        for pair in range(pairs):
-            cols = slice(pair * LANES, (pair + 1) * LANES)
-            query = stack_heads(q_ref[rows, cols] * scale)
-            keys = window_keys(k_ref, base, at, width, ext, globs, cols)
-            values = window_keys(v_ref, base, at, width, ext, globs, cols)
-            scores = dot_on(query, keys, 1, 1)
-            scores = scores + skew(dot_on(query, rel_ref[:, cols], 1, 1), width + globs) + bias
-            weights = softmax_rows(scores).astype(BF)
-            o_ref[rows, cols] = merge_stack(dot_on(weights, values, 1, 0)).astype(BF)
+        cols = [slice(pair * LANES, (pair + 1) * LANES) for pair in range(pairs)]
+        query = [stack_heads(q_ref[rows, c] * scale) for c in cols]
+        keys = [window_keys(k_ref, base, at, width, ext, globs, c) for c in cols]
+        values = [window_keys(v_ref, base, at, width, ext, globs, c) for c in cols]
+        near = [dot_on(q, rel_ref[:, c], 1, 1) for q, c in zip(query, cols)]
+        scores = [dot_on(q, k, 1, 1) for q, k in zip(query, keys)]
+        scores = [x + skew(y, width + globs) + bias for x, y in zip(scores, near)]
+        weights = [softmax_rows(x).astype(BF) for x in scores]
+        outs = [merge_stack(dot_on(w, v, 1, 0)).astype(BF) for w, v in zip(weights, values)]
+        for c, out in zip(cols, outs):
+            o_ref[rows, c] = out
         return carry
 
     lax.fori_loop(0, seqs * chunks, window, 0)
     rows = slice(glob_at, glob_at + glob_rows)
+    both = [(pair, seq) for pair in range(pairs) for seq in range(seqs)]
+    cols = [slice(pair * LANES, (pair + 1) * LANES) for pair in range(pairs)]
+    spans = [slice(seq * span, (seq + 1) * span) for seq in range(seqs)]
+    query = [stack_heads(q_ref[rows, c] * scale) for c in cols]
+    bias = [jnp.concatenate([gbias_ref[seq]] * 2, axis=0) for seq in range(seqs)]
+    scores = [dot_on(query[pair], k_ref[spans[seq], cols[pair]], 1, 1) + bias[seq] for pair, seq in both]
+    weights = [softmax_rows(x).astype(BF) for x in scores]
+    outs = [dot_on(w, v_ref[spans[seq], cols[pair]], 1, 0) for w, (pair, seq) in zip(weights, both)]
     for pair in range(pairs):
-        cols = slice(pair * LANES, (pair + 1) * LANES)
-        query = stack_heads(q_ref[rows, cols] * scale)
-        total = jnp.zeros((2 * glob_rows, LANES), F32)
-        for seq in range(seqs):
-            span_rows = slice(seq * span, (seq + 1) * span)
-            bias = gbias_ref[seq]
-            scores = dot_on(query, k_ref[span_rows, cols], 1, 1) + jnp.concatenate([bias, bias], axis=0)
-            weights = softmax_rows(scores).astype(BF)
-            out = dot_on(weights, v_ref[span_rows, cols], 1, 0)
-            total = jnp.where(glob_row_mask(total.shape, seq, glob_block), out, total)
-        o_ref[rows, cols] = merge_stack(total).astype(BF)
+        total = outs[pair * seqs]
+        for seq in range(1, seqs):
+            total = jnp.where(glob_row_mask(total.shape, seq, glob_block), outs[pair * seqs + seq], total)
+        used = lax.broadcasted_iota(jnp.int32, total.shape, 0) % glob_rows < seqs * glob_block
+        o_ref[rows, cols[pair]] = merge_stack(jnp.where(used, total, 0.0)).astype(BF)
     part_ref[...] = dot_on(o_ref[...], wo_ref[...], 1, 0).astype(BF)
     keep.wait()
 
@@ -925,49 +946,56 @@
         far_rows = pl.ds(base + ext, globs)
         bias = window_bias(block_ref[0], blocks, chunk, dims)
         near = lax.broadcasted_iota(jnp.int32, bias.shape, 1) < width
-        for pair in range(pairs):
-            cols = slice(pair * LANES, (pair + 1) * LANES)
-            query = stack_heads(q_ref[rows, cols] * scale)
-            grad_out = stack_heads(do_ref[rows, cols])
-            keys = window_keys(k_ref, base, at, width, ext, globs, cols)
-            values = window_keys(v_ref, base, at, width, ext, globs, cols)
-            labels = rel_ref[:, cols]
-            scores = dot_on(query, keys, 1, 1)
-            scores = scores + skew(dot_on(query, labels, 1, 1), width + globs) + bias
-            weights, ds = grads_of(scores, grad_out, values)
-            dsb = ds.astype(BF)
-            by_label = unskew(jnp.where(near, dsb.astype(F32), 0.0), LABEL_PAD).astype(BF)
-            dv = dot_on(weights, grad_out, 0, 0)
-            dk = dot_on(dsb, query, 0, 0)
-            dq = dot_on(dsb, keys, 1, 0) + dot_on(by_label, labels, 1, 0)
-            dq_ref[rows, cols] = (merge_stack(dq) * scale).astype(BF)
-            drel_ref[:, cols] += dot_on(by_label, query, 0, 0)
-            dkv_acc[pair, near_rows] += dk[:width]
-            dkv_acc[pair, far_rows] += dk[width:]
-            dkv_acc[pairs + pair, near_rows] += dv[:width]
-            dkv_acc[pairs + pair, far_rows] += dv[width:]
+        cols = [slice(pair * LANES, (pair + 1) * LANES) for pair in range(pairs)]
+        query = [stack_heads(q_ref[rows, c] * scale) for c in cols]
+        grad_out = [stack_heads(do_ref[rows, c]) for c in cols]
+        keys = [window_keys(k_ref, base, at, width, ext, globs, c) for c in cols]
+        values = [window_keys(v_ref, base, at, width, ext, globs, c) for c in cols]
+        labels = [rel_ref[:, c] for c in cols]
+        shifted = [dot_on(q, x, 1, 1) for q, x in zip(query, labels)]
+        scores = [dot_on(q, k, 1, 1) for q, k in zip(query, keys)]
+        scores = [x + skew(y, width + globs) + bias for x, y in zip(scores, shifted)]
+        pairs_of = [grads_of(x, g, v) for x, g, v in zip(scores, grad_out, values)]
+        dsb = [ds.astype(BF) for _, ds in pairs_of]
+        by_label = [unskew(jnp.where(near, x.astype(F32), 0.0), LABEL_PAD).astype(BF) for x in dsb]
+        dv = [dot_on(w, g, 0, 0) for (w, _), g in zip(pairs_of, grad_out)]
+        dk = [dot_on(x, q, 0, 0) for x, q in zip(dsb, query)]
+        dq = [
+            dot_on(x, k, 1, 0) + dot_on(y, l, 1, 0) for x, k, y, l in zip(dsb, keys, by_label, labels)
+        ]
+        drel = [dot_on(y, q, 0, 0) for y, q in zip(by_label, query)]
+        for pair, c in enumerate(cols):
+            dq_ref[rows, c] = (merge_stack(dq[pair]) * scale).astype(BF)
+            drel_ref[:, c] += drel[pair]
+            for at_acc, grad in ((pair, dk[pair]), (pairs + pair, dv[pair])):
+                dkv_acc[at_acc, near_rows] += grad[:width]
+                dkv_acc[at_acc, far_rows] += grad[width:]
         return carry
 
     lax.fori_loop(0, seqs * chunks, window, 0)
     rows = slice(glob_at, glob_at + glob_rows)
+    both = [(pair, seq) for pair in range(pairs) for seq in range(seqs)]
+    cols = [slice(pair * LANES, (pair + 1) * LANES) for pair in range(pairs)]
+    spans = [slice(seq * span, (seq + 1) * span) for seq in range(seqs)]
+    query = [stack_heads(q_ref[rows, c] * scale) for c in cols]
+    grad_out = [stack_heads(do_ref[rows, c]) for c in cols]
+    bias = [jnp.concatenate([gbias_ref[seq]] * 2, axis=0) for seq in range(seqs)]
+    keys = [k_ref[spans[seq], cols[pair]] for pair, seq in both]
+    scores = [dot_on(query[pair], k, 1, 1) + bias[seq] for k, (pair, seq) in zip(keys, both)]
+    grads = [
+        grads_of(x, grad_out[pair], v_ref[spans[seq], cols[pair]]) for x, (pair, seq) in zip(scores, both)
+    ]
+    own = [glob_row_mask(scores[0].shape, seq, glob_block) for seq in range(seqs)]
+    weights = [jnp.where(own[seq], w.astype(F32), 0.0).astype(BF) for (w, _), (_, seq) in zip(grads, both)]
+    dsb = [jnp.where(own[seq], ds, 0.0).astype(BF) for (_, ds), (_, seq) in zip(grads, both)]
+    dk = [dot_on(x, query[pair], 0, 0) for x, (pair, _) in zip(dsb, both)]
+    dv = [dot_on(w, grad_out[pair], 0, 0) for w, (pair, _) in zip(weights, both)]
+    dq = [dot_on(x, k, 1, 0) for x, k in zip(dsb, keys)]
     for pair in range(pairs):
-        cols = slice(pair * LANES, (pair + 1) * LANES)
-        query = stack_heads(q_ref[rows, cols] * scale)
-        grad_out = stack_heads(do_ref[rows, cols])
-        total = jnp.zeros((2 * glob_rows, LANES), F32)
+        dq_ref[rows, cols[pair]] = (merge_stack(sum(dq[pair * seqs : (pair + 1) * seqs])) * scale).astype(BF)
         for seq in range(seqs):
-            span_rows = slice(seq * span, (seq + 1) * span)
-            bias = gbias_ref[seq]
-            keys = k_ref[span_rows, cols]
-            scores = dot_on(query, keys, 1, 1) + jnp.concatenate([bias, bias], axis=0)
-            weights, ds = grads_of(scores, grad_out, v_ref[span_rows, cols])
-            own = glob_row_mask(ds.shape, seq, glob_block)
-            weights = jnp.where(own, weights.astype(F32), 0.0).astype(BF)
-            dsb = jnp.where(own, ds, 0.0).astype(BF)
-            dkv_acc[pair, span_rows] += dot_on(dsb, query, 0, 0)
-            dkv_acc[pairs + pair, span_rows] += dot_on(weights, grad_out, 0, 0)
-            total = total + dot_on(dsb, keys, 1, 0)
-        dq_ref[rows, cols] = (merge_stack(total) * scale).astype(BF)
+            dkv_acc[pair, spans[seq]] += dk[pair * seqs + seq]
+            dkv_acc[pairs + pair, spans[seq]] += dv[pair * seqs + seq]
     first_row, row_step, cells, per_block = glob_at_rows
     for seq in range(seqs):
         for r in range(per_block):
@@ -990,18 +1018,21 @@
     small_ref[...] = jnp.concatenate([drel_ref[: SMALL_ROWS - 8], norms_ref[...]], axis=0).astype(BF)
     for c in range(2 * pairs):
         dkv_ref[:, c * LANES : (c + 1) * LANES] = dkv_acc[c].astype(BF)
-    for at, stage in ((0, q_stage), (1, k_stage), (2, v_stage)):
-        rows_ref = xr_ref if at == 0 else xe_ref
-        grad = dq_ref[...] if at == 0 else dkv_ref[:, (at - 1) * head_cols : at * head_cols]
-
-        def cut(j):
-            row = pl.multiple_of(j * 256, 256)
-            stage[pl.ds(row, 256), :] = dot_on(rows_ref[:, pl.ds(row, 256)], grad, 0, 0).astype(BF)
-            send_tiles(
-                stage, row, 2, at * attn_tiles + j * 2 * (head_cols // LANES), place_ref, grads_ref, sems.at[1 + at]
-            )
-
-        col_loop(stage.shape[0], cut)
+    per = head_cols // LANES
+
+    def cut(j):
+        row = pl.multiple_of(j * 256, 256)
+        rows = pl.ds(row, 256)
+        first = 2 * per * j
+        q_stage[rows, :] = dot_on(xr_ref[:, rows], dq_ref[...], 0, 0).astype(BF)
+        send_tiles(q_stage, row, 2, first, place_ref, grads_ref, sems.at[1])
+        both = dot_on(xe_ref[:, rows], dkv_ref[...], 0, 0).astype(BF)
+        k_stage[rows, :] = both[:, :head_cols]
+        v_stage[rows, :] = both[:, head_cols:]
+        send_tiles(k_stage, row, 2, attn_tiles + first, place_ref, grads_ref, sems.at[2])
+        send_tiles(v_stage, row, 2, 2 * attn_tiles + first, place_ref, grads_ref, sems.at[3])
+
+    col_loop(q_stage.shape[0], cut)
     for at, stage in enumerate((out_stage, q_stage, k_stage, v_stage)):
         pltpu.make_async_copy(stage, stage, sems.at[at]).wait()
     for copy in spare:
@@ -1009,12 +1040,12 @@
     pltpu.make_async_copy(glob_low, glob_low, sems.at[5]).wait()
 
 
-def start_weights(wall_ref, at, head_cols, wqk_ref, wv_ref, sems):
-    model_dim = wqk_ref.shape[0]
+def start_weights(wall_ref, at, head_cols, wkv_ref, wq_ref, sems):
+    model_dim = wkv_ref.shape[0]
     copies = [
-        pltpu.make_async_copy(wall_ref.at[pl.ds(at[0], model_dim)], wqk_ref, sems.at[0]),
+        pltpu.make_async_copy(wall_ref.at[pl.ds(at[0], model_dim)], wkv_ref, sems.at[0]),
         pltpu.make_async_copy(
-            wall_ref.at[pl.ds(at[1], model_dim), pl.ds(0, head_cols)], wv_ref, sems.at[1]
+            wall_ref.at[pl.ds(at[1], model_dim), pl.ds(0, head_cols)], wq_ref, sems.at[1]
         ),
     ]
     for copy in copies:
@@ -1022,16 +1053,16 @@
     return copies
 
 
-def back_rows(proj, wqk_ref, wv_ref):
-    both = wqk_ref.shape[1]
-    return dot_on(proj[:, :both], wqk_ref[...], 1, 1) + dot_on(proj[:, both:], wv_ref[...], 1, 1)
+def back_rows(proj, wkv_ref, wq_ref):
+    cols = wq_ref.shape[1]
+    return dot_on(proj[:, :cols], wq_ref[...], 1, 1) + dot_on(proj[:, cols:], wkv_ref[...], 1, 1)
 
 
 def dx_kernel(dims, at, half_ref, dq_ref, dkv_ref, next_ref, last_ref, mid_ref, wall_ref,
-              keep_ref, send_ref, proj_ref, wqk_ref, wv_ref, sems):
+              keep_ref, send_ref, proj_ref, wkv_ref, wq_ref, sems):
     seqs, block_len, _, ext, _, globs, _ = dims
     head_cols = dq_ref.shape[1]
-    copies = start_weights(wall_ref, at, head_cols, wqk_ref, wv_ref, sems)
+    copies = start_weights(wall_ref, at, head_cols, wkv_ref, wq_ref, sems)
     proj_ref[:, :head_cols] = dq_ref[: seqs * block_len]
     for seq in range(seqs):
         base, row = seq * (ext + globs) + RIM, seq * block_len
@@ -1049,19 +1080,19 @@
     for out_ref, half in ((keep_ref, half_ref[0]), (send_ref, 1 - half_ref[0])):
         for seq in range(seqs):
             rows = pl.ds(pl.multiple_of(seq * block_len + half * per, per), per)
-            total = back_rows(proj_ref[rows, :], wqk_ref, wv_ref)
+            total = back_rows(proj_ref[rows, :], wkv_ref, wq_ref)
             if out_ref is keep_ref:
                 total = total + mid_ref[rows, :]
             out_ref[seq] = total.astype(out_ref.dtype)
 
 
 def dx_glob_kernel(dims, at, half_ref, dq_ref, kept_ref, got_ref, mid_ref, wall_ref,
-                   keep_ref, send_ref, cells_ref, wqk_ref, wv_ref, sems):
+                   keep_ref, send_ref, cells_ref, wkv_ref, wq_ref, sems):
     seqs, block_len, glob_block = dims[:3]
     head_cols = dq_ref.shape[1]
     base = seqs * block_len
     used, cols = seqs * glob_block, 2 * head_cols // LANES
-    copies = start_weights(wall_ref, at, head_cols, wqk_ref, wv_ref, sems)
+    copies = start_weights(wall_ref, at, head_cols, wkv_ref, wq_ref, sems)
     first = kept_ref.shape[0] - used * cols
     cells_ref[...] = kept_ref[first:].astype(F32) + got_ref[first:].astype(F32)
     wide = [cells_ref[pl.ds(c, used, stride=cols), :] for c in range(cols)]
@@ -1070,7 +1101,7 @@
     proj = jnp.concatenate([dq_ref[base:], dkv.astype(BF)], axis=1)
     for copy in copies:
         copy.wait()
-    total = back_rows(proj, wqk_ref, wv_ref)
+    total = back_rows(proj, wkv_ref, wq_ref)
     few = glob_block // 2
     here = half_ref[0] == 0
     for seq in range(seqs):
@@ -1143,17 +1174,17 @@
     )
     per_row = model_dim // side
     up_rows = hidden // model_dim * model_dim
-    qk_at = up_rows + hidden
-    v_at = qk_at + model_dim
-    out_at = v_at + model_dim
+    kv_at = up_rows + hidden
+    q_at = kv_at + model_dim
+    out_at = q_at + model_dim
     head_tiles = head_cols // side
     up_tiles = hidden // side
 
     def tile_row_col(tile):
         kind_qkv = tile // attn_tiles
         inner = tile % attn_tiles
-        qkv_row = jnp.where(kind_qkv == 2, v_at, qk_at) + inner // head_tiles * side
-        qkv_col = jnp.where(kind_qkv == 1, head_cols, 0) + inner % head_tiles * side
+        qkv_row = jnp.where(kind_qkv == 0, q_at, kv_at) + inner // head_tiles * side
+        qkv_col = jnp.where(kind_qkv == 2, head_cols, 0) + inner % head_tiles * side
         out_row = out_at + inner // per_row * side
         up = tile - 4 * attn_tiles
         up_col = up % up_tiles * side
@@ -1183,7 +1214,30 @@
     wall_row, wall_col = tile_row_col(held)
     wall_kind = jnp.where(held < 4 * attn_tiles, 0, jnp.where(held < tile_count, 1, 2))
 
+    weights_low = w_master.astype(BF).reshape(-1, LANES)
+    glob_other = swap_cores(x_glob)
+    glob_own = jnp.concatenate(
+        [jnp.where(first_half, x_glob, glob_other), jnp.where(first_half, glob_other, x_glob)], axis=1
+    )
+    orders = [order for _, _, order in parts]
+    gathered = gather_rows(
+        weights_low, glob_own.reshape(-1, LANES), rows_per, orders
+    )
+    gathered = [
+        [piece.reshape(-1, many, LANES) for piece in pieces] for pieces, many in zip(gathered, rows_per)
+    ]
+    tiles_per = tuple(last - first for (first, last, _), pieces in zip(parts, gathered) for _ in pieces)
+    gathered = [piece for pieces in gathered for piece in pieces]
+
+    rim = jnp.where(first_half, x_long[:, :RIM], x_long[:, tok_half - RIM :])
     mine = jnp.concatenate([x_long, dy_long, x_glob, dy_glob], axis=1)
+    spare = -mine.shape[1] % 8
+    mine = jnp.concatenate([mine, jnp.zeros((seqs, spare, model_dim), BF)], axis=1)
+    first, second = mine.reshape(-1, model_dim), rim.reshape(-1, model_dim)
+    first, second, _ = move_rows(
+        [[(first.shape[0], (first, 0))], [(second.shape[0], (second, 0))], [(16, (weights_low, 0))]]
+    )
+    mine, rim = first.reshape(mine.shape), second
     other = swap_cores(mine)
     lower = jnp.where(first_half, mine, other)
     upper = jnp.where(first_half, other, mine)
@@ -1206,31 +1260,13 @@
 
     x_rows = in_rows(long_rows, glob_rows)
     dy_all = in_rows(dy_rows, dy_globs)
-    rim = jnp.where(first_half, x_long[:, :RIM], x_long[:, tok_half - RIM :])
     to_next = [(i * ffn_count + 1, (i + 1) * ffn_count + 1) for i in range(seq_count - 1)]
     to_last = [((i + 1) * ffn_count, i * ffn_count) for i in range(seq_count - 1)]
     rim = lax.ppermute(rim, ("seq", "ffn"), to_next + to_last)
     rim_other = swap_cores(rim)
-    rim_left = jnp.where(first_half, rim_other, rim).reshape(-1, model_dim)
-    rim_right = jnp.where(first_half, rim, rim_other).reshape(-1, model_dim)
-
-    weights_low = w_master.astype(BF)
-    glob_other = swap_cores(x_glob)
-    glob_own = jnp.concatenate(
-        [jnp.where(first_half, x_glob, glob_other), jnp.where(first_half, glob_other, x_glob)], axis=1
-    )
-    orders = [order for _, _, order in parts]
-    gathered = [
-        [piece.reshape(-1, many, LANES) for piece in pieces]
-        for pieces, many in zip(
-            gather_rows(
-                weights_low.reshape(-1, LANES), glob_own.reshape(-1, LANES), rows_per, orders
-            ),
-            rows_per,
-        )
-    ]
-    tiles_per = tuple(last - first for (first, last, _), pieces in zip(parts, gathered) for _ in pieces)
-    gathered = [piece for pieces in gathered for piece in pieces]
+    rim_left = jnp.where(first_half, rim_other, rim)
+    rim_right = jnp.where(first_half, rim, rim_other)
+
     reach = 2 * RADIUS
     width = up_to(LANES + 2 * RIM, LANES) if globs % LANES == 0 else up_to(LANES + 2 * RIM + globs, LANES) - globs
     ext = block_len - LANES + width
@@ -1269,8 +1305,8 @@
     wall_at = (
         2 * ffn_tiles // per_row * side,
         4 * attn_tiles // per_row * side,
-        qk_at,
-        v_at,
+        kv_at,
+        q_at,
         out_at,
         tiles_per,
     )
@@ -1422,7 +1458,7 @@
     from_next = lax.ppermute(to_last, "seq", [(i + 1, i) for i in range(seq_count - 1)])
     from_last = lax.ppermute(to_next, "seq", [(i, i + 1) for i in range(seq_count - 1)])
 
-    weights_at = (qk_at, v_at)
+    weights_at = (kv_at, q_at)
     weights_held = [
         pltpu.VMEM((model_dim, model_dim), BF),
         pltpu.VMEM((model_dim, head_cols), BF),

time: 299 us -> 288 us (0.963)
  Pallas kernels: 110 us -> 102 us
  waiting for transfers between devices: 133 us -> 128 us
    ppermute x25, waiting for transfers between devices: 105 us -> 101 us  [swap_with(): return lax.ppermute(values, 'seq', [(i, i ^ bit) for i in range(count)])]
    pallas_call x1, Pallas kernels: 26.9 us -> 23.1 us  [soap_update(): pl.pallas_call(functools.partial(soap_kernel, npad), grid=(1,), out_shape...]
    pallas_call x1, Pallas kernels: 27.3 us -> 23.8 us  [on_device(): kernel_call(functools.partial(attend_back_kernel, dims, seq_count, attn_t...]
    pallas_call x9 -> x11, Pallas kernels: 15.7 us -> 17.2 us  [move_rows(): pl.pallas_call(functools.partial(move_kernel, plan, len(arrays)), grid=(1...]
  transfers between devices with their start and end apart: 36 -> 36, of which waited for: 16 -> 17; matrix products, arithmetic and copies ran while one was open for 3% -> 3% of each run, Pallas kernels for 16% -> 16%
where the time goes in v1:
time: 288 us
  waiting for transfers between devices  128 us (44%)
  Pallas kernels  102 us (35%)
  starting transfers between devices  41.9 us (15%)
  other arithmetic  7.27 us (3%)
  local copies, waits for them, and re-layouts  7.26 us (3%)
    ppermute x25, waiting for transfers between devices, swap_with(): return lax.ppermute(values, 'seq', [(i, i ^ bit) for i in range(count)])  101 us
    pallas_call x1, Pallas kernels, on_device(): kernel_call(functools.partial(attend_back_kernel, dims, seq_count, attn_t...  23.8 us
    ppermute x25, starting transfers between devices, swap_with(): return lax.ppermute(values, 'seq', [(i, i ^ bit) for i in range(count)])  23.8 us
    pallas_call x1, Pallas kernels, soap_update(): pl.pallas_call(functools.partial(soap_kernel, npad), grid=(1,), out_shape...  23.1 us
    ppermute x1, waiting for transfers between devices, on_device(): lax.ppermute(to_last, 'seq', [(i + 1, i) for i in range(seq_count - 1)])  20 us
    pallas_call x11, Pallas kernels, move_rows(): pl.pallas_call(functools.partial(move_kernel, plan, len(arrays)), grid=(1...  17.2 us
    pallas_call x1, Pallas kernels, on_device(): kernel_call(functools.partial(attend_kernel, dims, wall_at, seq_count), '...  14.3 us
    ppermute x8, starting transfers between devices, swap_cores(): return lax.ppermute(values, 'ffn', [(i, i ^ 1) for i in range(count)])  9.65 us
  transfers between devices with their start and end apart: 36, of which 17 were waited for; matrix products, arithmetic and copies ran while one was open for 3% of the time, Pallas kernels for 16%

profile of v1, /device:TPU:17, one launch (start us, length us, event | category | flops | bytes accessed | tf_op | source)
XLA Modules:
  0.0 287.7 jit_solution(3526187364776168715)
XLA Ops:
  0.7 0.7 collective-permute-start.4
  1.4 1.3 convert_element_type.14
  3.2 0.8 join_rows.5
  4.0 3.1 %collective-permute-start.1 = (bf16[192,768]{1,0:T(8,128)(2,1)S(1)}, bf16[192,768]{1,0:T(8,128)(2,1)}, u32[]{:S(2)}, u32[]{:S(2)}) collective-permute-start(bf16[192,768]{1,0:T(8,128)(2,1)S(1)} %get-tuple-element.91), channel_id=1, source_target_pairs={{1,3},{3,5},{5,7},{7,9},{9,11},{11,13},{13,15},{15,17},{17,19},{19... | collective-permute-start | bytes 884744 | tf_op jit(solution)/shard_map/ppermute | solution.py:1265
  7.1 3.9 %collective-permute-start = (bf16[2,264,768]{2,1,0:T(8,128)(2,1)S(1)}, bf16[2,264,768]{2,1,0:T(8,128)(2,1)}, u32[]{:S(2)}, u32[]{:S(2)}) collective-permute-start(bf16[2,264,768]{2,1,0:T(8,128)(2,1)S(1)} %bitcast.24), channel_id=1, source_target_pairs={{0,1},{1,0},{2,3},{3,2},{4,5},{5,4},{6,7},{7,6},{8,9},{9,8},{10,11... | collective-permute-start | bytes 2433032 | tf_op jit(solution)/shard_map/ppermute | solution.py:1120
  11.4 11.8 %collective-permute-done.5.refs_3_ = bf16[48,128]{1,0:T(8,128)(2,1)S(1)} collective-permute-done((bf16[48,128]{1,0:T(8,128)(2,1)S(1)}, bf16[48,128]{1,0:T(8,128)(2,1)S(1)}, u32[]{:S(2)}, u32[]{:S(2)}) %collective-permute-start.5) | collective-permute-done | bytes 12320 | tf_op jit(solution)/shard_map/ppermute | solution.py:34
  23.2 1.3 join_rows.6
  24.5 1.1 collective-permute-start.8
  25.6 4.7 %collective-permute-start.6 = (bf16[1280,128]{1,0:T(8,128)(2,1)S(1)}, bf16[1280,128]{1,0:T(8,128)(2,1)S(1)}, u32[]{:S(2)}, u32[]{:S(2)}) collective-permute-start(bf16[1280,128]{1,0:T(8,128)(2,1)S(1)} %get-tuple-element.92.refs_0_), channel_id=1, source_target_pairs={{0,8},{2,10},{4,12},{6,14},{8,0},{10,2},{12,4},{14,6},{16,24},{18,... | collective-permute-start | bytes 983048 | tf_op jit(solution)/shard_map/ppermute | solution.py:34
  30.3 4.1 %collective-permute-start.7 = (bf16[1280,128]{1,0:T(8,128)(2,1)S(1)}, bf16[1280,128]{1,0:T(8,128)(2,1)S(1)}, u32[]{:S(2)}, u32[]{:S(2)}) collective-permute-start(bf16[1280,128]{1,0:T(8,128)(2,1)S(1)} %get-tuple-element.93.refs_2_), channel_id=1, source_target_pairs={{0,2},{2,0},{4,6},{6,4},{8,10},{10,8},{12,14},{14,12},{16,18},{18,... | collective-permute-start | bytes 983048 | tf_op jit(solution)/shard_map/ppermute | solution.py:34
  34.7 0.5 collective-permute-done.8.refs_5_
  35.3 2.4 collective-permute-done.6.refs_1_
  37.6 3.5 %collective-permute-done.7.refs_3_ = bf16[1280,128]{1,0:T(8,128)(2,1)S(1)} collective-permute-done((bf16[1280,128]{1,0:T(8,128)(2,1)S(1)}, bf16[1280,128]{1,0:T(8,128)(2,1)S(1)}, u32[]{:S(2)}, u32[]{:S(2)}) %collective-permute-start.7) | collective-permute-done | bytes 327712 | tf_op jit(solution)/shard_map/ppermute | solution.py:34
  41.2 0.6 join_rows.7
  42.5 0.5 collective-permute-start.2
  43.6 0.9 collective-permute-done.2
  44.4 1.0 broadcast_select_fusion.2
  45.5 12.1 %collective-permute-done.11.refs_5_ = bf16[2240,128]{1,0:T(8,128)(2,1)S(1)} collective-permute-done((bf16[2240,128]{1,0:T(8,128)(2,1)S(1)}, bf16[2240,128]{1,0:T(8,128)(2,1)S(1)}, u32[]{:S(2)}, u32[]{:S(2)}) %collective-permute-start.11) | collective-permute-done | bytes 573472 | tf_op jit(solution)/shard_map/ppermute | solution.py:34
  57.6 0.9 collective-permute-done.9.refs_1_
  58.5 2.9 %join_rows.8 = (bf16[5120,128]{1,0:T(8,128)(2,1)}, bf16[5120,128]{1,0:T(8,128)(2,1)}, bf16[4480,128]{1,0:T(8,128)(2,1)}) custom-call(bf16[2560,128]{1,0:T(8,128)(2,1)S(1)} %get-tuple-element.95.refs_0_, bf16[2560,128]{1,0:T(8,128)(2,1)S(1)} %collective-permute-done.9.refs_1_, bf16[2560,128]{1,0:T(8,128)(2,1)S(1)} %get-tuple-element.96.refs_2_, ...), custom_call_target="tpu_custom_call" | custom-call | bytes 11304960 | tf_op jit(solution)/shard_map/join_rows/pallas_call | solution.py:119
  61.5 1.5 collective-permute-start.12
  62.9 1.3 collective-permute-start.13
  64.3 2.4 broadcast_select_fusion.1
  66.7 0.8 fusion.16
  67.6 1.5 fusion.14
  69.5 23.3 %collective-permute-done.14 = bf16[4480,128]{1,0:T(8,128)(2,1)} collective-permute-done((bf16[4480,128]{1,0:T(8,128)(2,1)}, bf16[4480,128]{1,0:T(8,128)(2,1)}, u32[]{:S(2)}, u32[]{:S(2)}) %collective-permute-start.14) | collective-permute-done | bytes 1146912 | tf_op jit(solution)/shard_map/ppermute | solution.py:34
  92.8 14.3 %attend.1 = (bf16[528,384]{1,0:T(8,128)(2,1)S(1)}, bf16[1024,384]{1,0:T(8,128)(2,1)S(1)}, bf16[1024,384]{1,0:T(8,128)(2,1)S(1)}, bf16[528,384]{1,0:T(8,128)(2,1)...) custom-call(s32[224]{0:T(256)S(1)} %get-tuple-element.185.row_ref, ...), custom_call_target="tpu_custom_call" | custom-call | flops 4000000000 | bytes 10000000 | tf_op jit(solution)/shard_map/attend/pallas_call | solution.py:1316
  107.1 1.9 collective-permute-start.15
  109.1 1.9 collective-permute-done.15.got_ref
  111.0 5.3 %feed.1 = (f32[528,768]{1,0:T(8,128)S(1)}, bf16[528,768]{1,0:T(8,128)(2,1)S(1)}, f32[528,1536]{1,0:T(8,128)S(1)}, bf16[528,1536]{1,0:T(8,128)(2,1)S(1)}, bf16[528,768]{1,0:T(8,128)(2,1)S(1)}) custom-call(bf16[528,768]{1,0:T(8,128)(2,1)S(1)} %get-tuple-element.182.xr_ref, bf16[528,768]{1,0:T(8,128)(2,1)S(1)} %get-tuple-element.101.part_ref, ...), custom_call_target="tpu_custom_call" | custom-call | flops 3000000000 | bytes 10000000 | tf_op jit(solution)/shard_map/feed/pallas_call | solution.py:1340
  116.8 1.9 collective-permute-done.16.got_ref
  118.8 7.3 %feed_back.1 = (bf16[2,128,768]{2,1,0:T(8,128)(2,1)}, bf16[2,2,768]{2,1,0:T(2,128)(2,1)}, f32[528,768]{1,0:T(8,128)S(1)}, bf16[528,768]{1,0:T(8,128)(2,1)S(1)}, ...) custom-call(s32[1]{0:T(128)} %bitcast.half_ref, ...), custom_call_target="tpu_custom_call" | custom-call | flops 3000000000 | bytes 10000000 | tf_op jit(solution)/shard_map/feed_back/pallas_call | solution.py:1362
  126.0 1.2 copy-done.14
  127.6 7.5 %feed_grads.1.grads_in = bf16[29440,128]{1,0:T(8,128)(2,1)S(1)} custom-call(s32[224]{0:T(256)S(1)} %get-tuple-element.163.place_ref, bf16[528,1536]{1,0:T(8,128)(2,1)S(1)} %get-tuple-element.116.a_ref, bf16[528,768]{1,0:T(8,128)(2,1)S(1)} %get-tuple-element.117.dxb_ref, bf16[528,768]{1,0:T(8,128)(2,1)S(1)} %get-tuple-element.118.hb_ref, ...), custom_call_target="tpu_custom_call" | custom-call | flops 3000000000 | bytes 10000000 | tf_op jit(solution)/shard_map/feed_grads/pallas_call | solution.py:1377
  135.2 1.1 copy-done.17
  136.3 23.8 %attend_back.1 = (bf16[29440,128]{1,0:T(8,128)(2,1)S(1)}, bf16[528,384]{1,0:T(8,128)(2,1)S(1)}, bf16[1024,768]{1,0:T(8,128)(2,1)S(1)}, f32[528,768]{1,0:T(8,128)S(1)}, bf16[192,384]{1,0:T(8,128)(2,1)S(1)}) custom-call(s32[1]{0:T(128)} %bitcast.6.block_ref, s32[224]{0:T(256)S(1)} %get-tuple-element.163.place_ref, ...), custom_call_target="tpu_custom_call", output_to_operand_aliasing={{0}: (18, {})} | custom-call | flops 8000000000 | bytes 20000000 | tf_op jit(solution)/shard_map/attend_back/pallas_call | solution.py:1412
  160.3 1.1 collective-permute-start.19
  161.8 0.7 collective-permute-start.21
  162.9 27.4 %collective-permute-done.21.refs_7_ = bf16[192,384]{1,0:T(8,128)(2,1)S(1)} collective-permute-done((bf16[192,384]{1,0:T(8,128)(2,1)S(1)}, bf16[192,384]{1,0:T(8,128)(2,1)S(1)}, u32[]{:S(2)}, u32[]{:S(2)}) %collective-permute-start.21) | collective-permute-done | bytes 147488 | tf_op jit(solution)/shard_map/ppermute | solution.py:34
  190.6 0.8 collective-permute-done.18.refs_1_
  191.4 2.3 add_rows.7
  194.2 1.0 collective-permute-start.24
  195.1 0.5 collective-permute-start.25
  195.6 1.9 add_rows.6
  197.5 12.4 %collective-permute-done.25.refs_7_ = bf16[192,384]{1,0:T(8,128)(2,1)S(1)} collective-permute-done((bf16[192,384]{1,0:T(8,128)(2,1)S(1)}, bf16[192,384]{1,0:T(8,128)(2,1)S(1)}, u32[]{:S(2)}, u32[]{:S(2)}) %collective-permute-start.25) | collective-permute-done | bytes 147488 | tf_op jit(solution)/shard_map/ppermute | solution.py:34
  210.0 1.5 add_rows.9
  211.5 1.5 collective-permute-start.26
  213.1 1.1 collective-permute-start.28
  214.6 1.1 add_rows.8
  215.6 5.6 %collective-permute-done.29.refs_7_ = bf16[192,384]{1,0:T(8,128)(2,1)S(1)} collective-permute-done((bf16[192,384]{1,0:T(8,128)(2,1)S(1)}, bf16[192,384]{1,0:T(8,128)(2,1)S(1)}, u32[]{:S(2)}, u32[]{:S(2)}) %collective-permute-start.29) | collective-permute-done | bytes 147488 | tf_op jit(solution)/shard_map/ppermute | solution.py:34
  221.3 2.9 %add_rows.10 = (bf16[1840,128]{1,0:T(8,128)(2,1)S(1)}, bf16[192,384]{1,0:T(8,128)(2,1)S(1)}, bf16[192,768]{1,0:T(8,128)(2,1)S(1)}, bf16[192,768]{1,0:T(8,128)(2,1)S(1)}) custom-call(bf16[1280,128]{1,0:T(8,128)(2,1)S(1)} %get-tuple-element.133.refs_0_, bf16[1280,128]{1,0:T(8,128)(2,1)S(1)} %collective-permute-done.26.refs_1_, ...), custom_call_target="tpu_custom_call" | custom-call | bytes 3624960 | tf_op jit(solution)/shard_map/add_rows/pallas_call | solution.py:119
  224.2 1.8 collective-permute-start.33
  226.0 3.4 %collective-permute-start.30 = (bf16[192,768]{1,0:T(8,128)(2,1)S(1)}, bf16[192,768]{1,0:T(8,128)(2,1)S(1)}, u32[]{:S(2)}, u32[]{:S(2)}) collective-permute-start(bf16[192,768]{1,0:T(8,128)(2,1)S(1)} %get-tuple-element.141), channel_id=1, source_target_pairs={{2,0},{4,2},{6,4},{8,6},{10,8},{12,10},{14,12},{16,14},{18,16},{20... | collective-permute-start | bytes 884744 | tf_op jit(solution)/shard_map/ppermute | solution.py:1458
  229.4 1.9 collective-permute-start.31
  231.3 0.9 collective-permute-start.35
  232.2 20.0 %collective-permute-done.30.next_ref = bf16[192,768]{1,0:T(8,128)(2,1)S(1)} collective-permute-done((bf16[192,768]{1,0:T(8,128)(2,1)S(1)}, bf16[192,768]{1,0:T(8,128)(2,1)S(1)}, u32[]{:S(2)}, u32[]{:S(2)}) %collective-permute-start.30) | collective-permute-done | bytes 294944 | tf_op jit(solution)/shard_map/ppermute | solution.py:1458
  252.2 1.9 collective-permute-done.31.last_ref
  254.1 2.7 dx_long.1
  256.8 1.7 collective-permute-start.32
  258.5 1.6 add_rows.11.kept_ref
  260.2 0.9 dx_glob.1
  263.0 23.1 %soap.1 = (f32[14,128,128]{2,1,0:T(8,128)}, f32[14,128,128]{2,1,0:T(8,128)}, f32[14,128,128]{2,1,0:T(8,128)}, f32[14,128,128]{2,1,0:T(8,128)}, f32[14,128,128]{2...) custom-call(bf16[1840,128]{1,0:T(8,128)(2,1)S(1)} %add_rows.11.kept_, ...), custom_call_target="tpu_custom_call" | custom-call | flops 1174405120 | bytes 13762560 | tf_op jit(solution)/shard_map/soap/pallas_call | solution.py:447
  286.1 0.6 convert_add_fusion.1
  286.7 1.0 convert_add_fusion
  (125 shorter events, 7.7 us)
Async XLA Ops:
  0.7 2.2 copy-start.24
  0.7 2.1 copy-start.22
  0.7 2.2 copy-start.25
  0.7 2.2 copy-start.23
  0.7 10.5 %collective-permute-start.4 = (bf16[2,2,768]{2,1,0:T(2,128)(2,1)}, bf16[2,2,768]{2,1,0:T(2,128)(2,1)S(1)}, u32[]{:S(2)}, u32[]{:S(2)}) collective-permute-start(bf16[2,2,768]{2,1,0:T(2,128)(2,1)} %param.20), channel_id=1, source_target_pairs={{0,1},{1,0},{2,3},{3,2},{4,5},{5,4},{6,7},{7,6},{8,9},{9,8},{10,11... | collective-permute-start | bytes 18440 | tf_op jit(solution)/shard_map/ppermute | solution.py:1120
  2.7 20.5 %collective-permute-start.3 = (bf16[1792,128]{1,0:T(8,128)(2,1)S(1)}, bf16[1792,128]{1,0:T(8,128)(2,1)S(1)}, u32[]{:S(2)}, u32[]{:S(2)}) collective-permute-start(bf16[1792,128]{1,0:T(8,128)(2,1)S(1)} %bitcast.19), channel_id=1, source_target_pairs={{0,16},{2,18},{4,20},{6,22},{8,24},{10,26},{12,28},{14,30},{16,0},... | collective-permute-start | bytes 1376264 | tf_op jit(solution)/shard_map/ppermute | solution.py:34
  2.9 8.1 %copy-start.26 = (s32[224]{0:T(256)S(1)}, s32[224]{0:T(256)}, u32[]{:S(2)}) copy-start(s32[224]{0:T(256)} %param.24) | copy-start | bytes 2692
  3.2 31.3 %copy-start.27 = (s32[2,1,256]{2,1,0:T(1,128)S(1)}, s32[2,1,256]{2,1,0:T(1,128)}, u32[]{:S(2)}) copy-start(s32[2,1,256]{2,1,0:T(1,128)} %param.21) | copy-start | bytes 6148
  3.2 31.3 %copy-start.2 = (f32[169,384]{1,0:T(8,128)S(1)}, f32[169,384]{1,0:T(8,128)}, u32[]{:S(2)}) copy-start(f32[169,384]{1,0:T(8,128)} %refs_7_.1) | copy-start | bytes 778756
  4.0 38.5 %collective-permute-start.1 = (bf16[192,768]{1,0:T(8,128)(2,1)S(1)}, bf16[192,768]{1,0:T(8,128)(2,1)}, u32[]{:S(2)}, u32[]{:S(2)}) collective-permute-start(bf16[192,768]{1,0:T(8,128)(2,1)S(1)} %get-tuple-element.91), channel_id=1, source_target_pairs={{1,3},{3,5},{5,7},{7,9},{9,11},{11,13},{13,15},{15,17},{17,19},{19... | collective-permute-start | bytes 884744 | tf_op jit(solution)/shard_map/ppermute | solution.py:1265
  7.1 57.1 %collective-permute-start = (bf16[2,264,768]{2,1,0:T(8,128)(2,1)S(1)}, bf16[2,264,768]{2,1,0:T(8,128)(2,1)}, u32[]{:S(2)}, u32[]{:S(2)}) collective-permute-start(bf16[2,264,768]{2,1,0:T(8,128)(2,1)S(1)} %bitcast.24), channel_id=1, source_target_pairs={{0,1},{1,0},{2,3},{3,2},{4,5},{5,4},{6,7},{7,6},{8,9},{9,8},{10,11... | collective-permute-start | bytes 2433032 | tf_op jit(solution)/shard_map/ppermute | solution.py:1120
  11.3 11.9 %collective-permute-start.5 = (bf16[48,128]{1,0:T(8,128)(2,1)S(1)}, bf16[48,128]{1,0:T(8,128)(2,1)S(1)}, u32[]{:S(2)}, u32[]{:S(2)}) collective-permute-start(bf16[48,128]{1,0:T(8,128)(2,1)S(1)} %reshape.131.refs_2_), channel_id=1, source_target_pairs={{0,16},{2,18},{4,20},{6,22},{8,24},{10,26},{12,28},{14,30},{16,0},... | collective-permute-start | bytes 36872 | tf_op jit(solution)/shard_map/ppermute | solution.py:34
  24.5 10.8 %collective-permute-start.8 = (bf16[1120,128]{1,0:T(8,128)(2,1)S(1)}, bf16[1120,128]{1,0:T(8,128)(2,1)S(1)}, u32[]{:S(2)}, u32[]{:S(2)}) collective-permute-start(bf16[1120,128]{1,0:T(8,128)(2,1)S(1)} %get-tuple-element.94.refs_4_), channel_id=1, source_target_pairs={{0,4},{2,6},{4,0},{6,2},{8,12},{10,14},{12,8},{14,10},{16,20},{18,... | collective-permute-start | bytes 860168 | tf_op jit(solution)/shard_map/ppermute | solution.py:34
  25.6 12.1 %collective-permute-start.6 = (bf16[1280,128]{1,0:T(8,128)(2,1)S(1)}, bf16[1280,128]{1,0:T(8,128)(2,1)S(1)}, u32[]{:S(2)}, u32[]{:S(2)}) collective-permute-start(bf16[1280,128]{1,0:T(8,128)(2,1)S(1)} %get-tuple-element.92.refs_0_), channel_id=1, source_target_pairs={{0,8},{2,10},{4,12},{6,14},{8,0},{10,2},{12,4},{14,6},{16,24},{18,... | collective-permute-start | bytes 983048 | tf_op jit(solution)/shard_map/ppermute | solution.py:34
  30.3 10.9 %collective-permute-start.7 = (bf16[1280,128]{1,0:T(8,128)(2,1)S(1)}, bf16[1280,128]{1,0:T(8,128)(2,1)S(1)}, u32[]{:S(2)}, u32[]{:S(2)}) collective-permute-start(bf16[1280,128]{1,0:T(8,128)(2,1)S(1)} %get-tuple-element.93.refs_2_), channel_id=1, source_target_pairs={{0,2},{2,0},{4,6},{6,4},{8,10},{10,8},{12,14},{14,12},{16,18},{18,... | collective-permute-start | bytes 983048 | tf_op jit(solution)/shard_map/ppermute | solution.py:34
  41.8 16.7 %collective-permute-start.9 = (bf16[2560,128]{1,0:T(8,128)(2,1)S(1)}, bf16[2560,128]{1,0:T(8,128)(2,1)S(1)}, u32[]{:S(2)}, u32[]{:S(2)}) collective-permute-start(bf16[2560,128]{1,0:T(8,128)(2,1)S(1)} %get-tuple-element.95.refs_0_), channel_id=1, source_target_pairs={{0,4},{2,6},{4,0},{6,2},{8,12},{10,14},{12,8},{14,10},{16,20},{18,... | collective-permute-start | bytes 1966088 | tf_op jit(solution)/shard_map/ppermute | solution.py:34
  42.1 16.5 %collective-permute-start.10 = (bf16[2560,128]{1,0:T(8,128)(2,1)S(1)}, bf16[2560,128]{1,0:T(8,128)(2,1)S(1)}, u32[]{:S(2)}, u32[]{:S(2)}) collective-permute-start(bf16[2560,128]{1,0:T(8,128)(2,1)S(1)} %get-tuple-element.96.refs_2_), channel_id=1, source_target_pairs={{0,8},{2,10},{4,12},{6,14},{8,0},{10,2},{12,4},{14,6},{16,24},{18,... | collective-permute-start | bytes 1966088 | tf_op jit(solution)/shard_map/ppermute | solution.py:34
  42.5 1.9 collective-permute-start.2
  43.0 14.6 %collective-permute-start.11 = (bf16[2240,128]{1,0:T(8,128)(2,1)S(1)}, bf16[2240,128]{1,0:T(8,128)(2,1)S(1)}, u32[]{:S(2)}, u32[]{:S(2)}) collective-permute-start(bf16[2240,128]{1,0:T(8,128)(2,1)S(1)} %get-tuple-element.97.refs_4_), channel_id=1, source_target_pairs={{0,2},{2,0},{4,6},{6,4},{8,10},{10,8},{12,14},{14,12},{16,18},{18,... | collective-permute-start | bytes 1720328 | tf_op jit(solution)/shard_map/ppermute | solution.py:34
  61.5 31.3 %collective-permute-start.12 = (bf16[5120,128]{1,0:T(8,128)(2,1)}, bf16[5120,128]{1,0:T(8,128)(2,1)}, u32[]{:S(2)}, u32[]{:S(2)}) collective-permute-start(bf16[5120,128]{1,0:T(8,128)(2,1)} %get-tuple-element.98), channel_id=1, source_target_pairs={{0,2},{2,0},{4,6},{6,4},{8,10},{10,8},{12,14},{14,12},{16,18},{18,... | collective-permute-start | bytes 3932168 | tf_op jit(solution)/shard_map/ppermute | solution.py:34
  62.9 29.9 %collective-permute-start.13 = (bf16[5120,128]{1,0:T(8,128)(2,1)}, bf16[5120,128]{1,0:T(8,128)(2,1)}, u32[]{:S(2)}, u32[]{:S(2)}) collective-permute-start(bf16[5120,128]{1,0:T(8,128)(2,1)} %get-tuple-element.99), channel_id=1, source_target_pairs={{0,4},{2,6},{4,0},{6,2},{8,12},{10,14},{12,8},{14,10},{16,20},{18,... | collective-permute-start | bytes 3932168 | tf_op jit(solution)/shard_map/ppermute | solution.py:34
  66.7 26.1 %collective-permute-start.14 = (bf16[4480,128]{1,0:T(8,128)(2,1)}, bf16[4480,128]{1,0:T(8,128)(2,1)}, u32[]{:S(2)}, u32[]{:S(2)}) collective-permute-start(bf16[4480,128]{1,0:T(8,128)(2,1)} %get-tuple-element.100), channel_id=1, source_target_pairs={{0,8},{2,10},{4,12},{6,14},{8,0},{10,2},{12,4},{14,6},{16,24},{18,... | collective-permute-start | bytes 3440648 | tf_op jit(solution)/shard_map/ppermute | solution.py:34
  92.8 18.2 %copy-start.11 = (f32[4,768]{1,0:T(4,128)S(1)}, f32[4,768]{1,0:T(4,128)}, u32[]{:S(2)}) copy-start(f32[4,768]{1,0:T(4,128)} %refs_10_.1) | copy-start | bytes 36868
  107.1 9.2 %copy-start.18 = (bf16[1024,768]{1,0:T(8,128)(2,1)}, bf16[1024,768]{1,0:T(8,128)(2,1)S(1)}, u32[]{:S(2)}) copy-start(bf16[1024,768]{1,0:T(8,128)(2,1)S(1)} %get-tuple-element.115.xe_ref) | copy-start | bytes 4718596
  107.1 9.2 %copy-start.20 = (bf16[1024,384]{1,0:T(8,128)(2,1)}, bf16[1024,384]{1,0:T(8,128)(2,1)S(1)}, u32[]{:S(2)}) copy-start(bf16[1024,384]{1,0:T(8,128)(2,1)S(1)} %get-tuple-element.114.v_ref) | copy-start | bytes 2359300
  107.1 11.6 %copy-start = (bf16[4992,768]{1,0:T(8,128)(2,1)}, bf16[4992,768]{1,0:T(8,128)(2,1)S(1)}, u32[]{:S(2)}) copy-start(bf16[4992,768]{1,0:T(8,128)(2,1)S(1)} %get-tuple-element.102.wu_ref.wd_ref.wo_ref.wall_ref) | copy-start | bytes 23003140
  107.1 3.9 %collective-permute-start.15 = (bf16[528,768]{1,0:T(8,128)(2,1)S(1)}, bf16[528,768]{1,0:T(8,128)(2,1)S(1)}, u32[]{:S(2)}, u32[]{:S(2)}) collective-permute-start(bf16[528,768]{1,0:T(8,128)(2,1)S(1)} %get-tuple-element.101.part_ref), channel_id=1, source_target_pairs={{0,1},{1,0},{2,3},{3,2},{4,5},{5,4},{6,7},{7,6},{8,9},{9,8},{10,11... | collective-permute-start | bytes 2433032 | tf_op jit(solution)/shard_map/ppermute | solution.py:1120
  116.4 2.4 collective-permute-start.16
  127.2 7.9 %copy-start.16 = (bf16[528,768]{1,0:T(8,128)(2,1)}, bf16[528,768]{1,0:T(8,128)(2,1)S(1)}, u32[]{:S(2)}) copy-start(bf16[528,768]{1,0:T(8,128)(2,1)S(1)} %get-tuple-element.109.dh_ref) | copy-start | bytes 2433028
  127.2 7.9 %collective-permute-start.17 = (bf16[528,768]{1,0:T(8,128)(2,1)S(1)}, bf16[528,768]{1,0:T(8,128)(2,1)S(1)}, u32[]{:S(2)}, u32[]{:S(2)}) collective-permute-start(bf16[528,768]{1,0:T(8,128)(2,1)S(1)} %get-tuple-element.109.dh_ref), channel_id=1, source_target_pairs={{0,1},{1,0},{2,3},{3,2},{4,5},{5,4},{6,7},{7,6},{8,9},{9,8},{10,11... | collective-permute-start | bytes 2433032 | tf_op jit(solution)/shard_map/ppermute | solution.py:1120
  127.6 7.6 %copy-start.15 = (f32[528,768]{1,0:T(8,128)S(1)}, f32[528,768]{1,0:T(8,128)}, u32[]{:S(2)}) copy-start(f32[528,768]{1,0:T(8,128)} %copy-done.14) | copy-start | bytes 4866052
  127.6 7.6 %copy-start.19 = (bf16[1024,768]{1,0:T(8,128)(2,1)S(1)}, bf16[1024,768]{1,0:T(8,128)(2,1)}, u32[]{:S(2)}) copy-start(bf16[1024,768]{1,0:T(8,128)(2,1)} %copy-done.18) | copy-start | bytes 4718596
  127.6 7.6 %copy-start.21 = (bf16[1024,384]{1,0:T(8,128)(2,1)S(1)}, bf16[1024,384]{1,0:T(8,128)(2,1)}, u32[]{:S(2)}) copy-start(bf16[1024,384]{1,0:T(8,128)(2,1)} %copy-done.20) | copy-start | bytes 2359300
  160.3 30.3 %collective-permute-start.19 = (bf16[5120,128]{1,0:T(8,128)(2,1)S(1)}, bf16[5120,128]{1,0:T(8,128)(2,1)S(1)}, u32[]{:S(2)}, u32[]{:S(2)}) collective-permute-start(bf16[5120,128]{1,0:T(8,128)(2,1)S(1)} %get-tuple-element.165), channel_id=1, source_target_pairs={{0,4},{2,6},{4,0},{6,2},{8,12},{10,14},{12,8},{14,10},{16,20},{18,... | collective-permute-start | bytes 3932168 | tf_op jit(solution)/shard_map/ppermute | solution.py:34
  161.5 29.9 %collective-permute-start.18 = (bf16[5120,128]{1,0:T(8,128)(2,1)S(1)}, bf16[5120,128]{1,0:T(8,128)(2,1)S(1)}, u32[]{:S(2)}, u32[]{:S(2)}) collective-permute-start(bf16[5120,128]{1,0:T(8,128)(2,1)S(1)} %get-tuple-element.166), channel_id=1, source_target_pairs={{0,2},{2,0},{4,6},{6,4},{8,10},{10,8},{12,14},{14,12},{16,18},{18,... | collective-permute-start | bytes 3932168 | tf_op jit(solution)/shard_map/ppermute | solution.py:34
  161.6 28.7 %collective-permute-start.20 = (bf16[4480,128]{1,0:T(8,128)(2,1)S(1)}, bf16[4480,128]{1,0:T(8,128)(2,1)S(1)}, u32[]{:S(2)}, u32[]{:S(2)}) collective-permute-start(bf16[4480,128]{1,0:T(8,128)(2,1)S(1)} %slice.51), channel_id=1, source_target_pairs={{0,8},{2,10},{4,12},{6,14},{8,0},{10,2},{12,4},{14,6},{16,24},{18,... | collective-permute-start | bytes 3440648 | tf_op jit(solution)/shard_map/ppermute | solution.py:34
  161.8 28.5 %collective-permute-start.21 = (bf16[192,384]{1,0:T(8,128)(2,1)S(1)}, bf16[192,384]{1,0:T(8,128)(2,1)S(1)}, u32[]{:S(2)}, u32[]{:S(2)}) collective-permute-start(bf16[192,384]{1,0:T(8,128)(2,1)S(1)} %get-tuple-element.127.refs_6_), channel_id=1, source_target_pairs={{0,16},{2,18},{4,20},{6,22},{8,24},{10,26},{12,28},{14,30},{16,0},... | collective-permute-start | bytes 442376 | tf_op jit(solution)/shard_map/ppermute | solution.py:34
  193.7 16.2 %collective-permute-start.22 = (bf16[2560,128]{1,0:T(8,128)(2,1)S(1)}, bf16[2560,128]{1,0:T(8,128)(2,1)S(1)}, u32[]{:S(2)}, u32[]{:S(2)}) collective-permute-start(bf16[2560,128]{1,0:T(8,128)(2,1)S(1)} %get-tuple-element.128), channel_id=1, source_target_pairs={{0,4},{2,6},{4,0},{6,2},{8,12},{10,14},{12,8},{14,10},{16,20},{18,... | collective-permute-start | bytes 1966088 | tf_op jit(solution)/shard_map/ppermute | solution.py:34
  194.2 15.8 %collective-permute-start.23 = (bf16[2560,128]{1,0:T(8,128)(2,1)S(1)}, bf16[2560,128]{1,0:T(8,128)(2,1)S(1)}, u32[]{:S(2)}, u32[]{:S(2)}) collective-permute-start(bf16[2560,128]{1,0:T(8,128)(2,1)S(1)} %get-tuple-element.130), channel_id=1, source_target_pairs={{0,8},{2,10},{4,12},{6,14},{8,0},{10,2},{12,4},{14,6},{16,24},{18,... | collective-permute-start | bytes 1966088 | tf_op jit(solution)/shard_map/ppermute | solution.py:34
  194.2 15.8 %collective-permute-start.24 = (bf16[2240,128]{1,0:T(8,128)(2,1)S(1)}, bf16[2240,128]{1,0:T(8,128)(2,1)S(1)}, u32[]{:S(2)}, u32[]{:S(2)}) collective-permute-start(bf16[2240,128]{1,0:T(8,128)(2,1)S(1)} %get-tuple-element.132), channel_id=1, source_target_pairs={{0,2},{2,0},{4,6},{6,4},{8,10},{10,8},{12,14},{14,12},{16,18},{18,... | collective-permute-start | bytes 1720328 | tf_op jit(solution)/shard_map/ppermute | solution.py:34
  195.1 14.8 %collective-permute-start.25 = (bf16[192,384]{1,0:T(8,128)(2,1)S(1)}, bf16[192,384]{1,0:T(8,128)(2,1)S(1)}, u32[]{:S(2)}, u32[]{:S(2)}) collective-permute-start(bf16[192,384]{1,0:T(8,128)(2,1)S(1)} %get-tuple-element.134.refs_6_), channel_id=1, source_target_pairs={{0,2},{2,0},{4,6},{6,4},{8,10},{10,8},{12,14},{14,12},{16,18},{18,... | collective-permute-start | bytes 442376 | tf_op jit(solution)/shard_map/ppermute | solution.py:34
  195.6 58.5 %slice-start = ((s8[7667712]{0:T(1024)(128)(4,1)}), s8[4194304]{0:T(1024)(128)(4,1)S(1)}, s32[]{:S(2)}) async-start(s8[7667712]{0:T(1024)(128)(4,1)} %bitcast.17), calls=%async_computation | async-start | bytes 8388608
  210.0 44.1 %slice-start.1 = ((s8[7667712]{0:T(1024)(128)(4,1)}), s8[3473408]{0:T(1024)(128)(4,1)S(1)}, s32[]{:S(2)}) async-start(s8[7667712]{0:T(1024)(128)(4,1)} %bitcast.17), calls=%async_computation.1 | async-start | bytes 6946816
  211.5 9.8 %collective-permute-start.26 = (bf16[1280,128]{1,0:T(8,128)(2,1)S(1)}, bf16[1280,128]{1,0:T(8,128)(2,1)S(1)}, u32[]{:S(2)}, u32[]{:S(2)}) collective-permute-start(bf16[1280,128]{1,0:T(8,128)(2,1)S(1)} %get-tuple-element.135), channel_id=1, source_target_pairs={{0,8},{2,10},{4,12},{6,14},{8,0},{10,2},{12,4},{14,6},{16,24},{18,... | collective-permute-start | bytes 983048 | tf_op jit(solution)/shard_map/ppermute | solution.py:34
  213.0 8.3 %collective-permute-start.27 = (bf16[1280,128]{1,0:T(8,128)(2,1)S(1)}, bf16[1280,128]{1,0:T(8,128)(2,1)S(1)}, u32[]{:S(2)}, u32[]{:S(2)}) collective-permute-start(bf16[1280,128]{1,0:T(8,128)(2,1)S(1)} %get-tuple-element.137), channel_id=1, source_target_pairs={{0,2},{2,0},{4,6},{6,4},{8,10},{10,8},{12,14},{14,12},{16,18},{18,... | collective-permute-start | bytes 983048 | tf_op jit(solution)/shard_map/ppermute | solution.py:34
  213.1 8.2 %collective-permute-start.28 = (bf16[1120,128]{1,0:T(8,128)(2,1)S(1)}, bf16[1120,128]{1,0:T(8,128)(2,1)S(1)}, u32[]{:S(2)}, u32[]{:S(2)}) collective-permute-start(bf16[1120,128]{1,0:T(8,128)(2,1)S(1)} %get-tuple-element.139), channel_id=1, source_target_pairs={{0,4},{2,6},{4,0},{6,2},{8,12},{10,14},{12,8},{14,10},{16,20},{18,... | collective-permute-start | bytes 860168 | tf_op jit(solution)/shard_map/ppermute | solution.py:34
  214.2 7.1 %collective-permute-start.29 = (bf16[192,384]{1,0:T(8,128)(2,1)S(1)}, bf16[192,384]{1,0:T(8,128)(2,1)S(1)}, u32[]{:S(2)}, u32[]{:S(2)}) collective-permute-start(bf16[192,384]{1,0:T(8,128)(2,1)S(1)} %get-tuple-element.140.refs_6_), channel_id=1, source_target_pairs={{0,4},{2,6},{4,0},{6,2},{8,12},{10,14},{12,8},{14,10},{16,20},{18,... | collective-permute-start | bytes 442376 | tf_op jit(solution)/shard_map/ppermute | solution.py:34
  224.2 36.0 %collective-permute-start.33 = (bf16[1840,128]{1,0:T(8,128)(2,1)S(1)}, bf16[1840,128]{1,0:T(8,128)(2,1)S(1)}, u32[]{:S(2)}, u32[]{:S(2)}) collective-permute-start(bf16[1840,128]{1,0:T(8,128)(2,1)S(1)} %get-tuple-element.146), channel_id=1, source_target_pairs={{0,16},{2,18},{4,20},{6,22},{8,24},{10,26},{12,28},{14,30},{16,0},... | collective-permute-start | bytes 1413128 | tf_op jit(solution)/shard_map/ppermute | solution.py:34
  226.0 26.3 %collective-permute-start.30 = (bf16[192,768]{1,0:T(8,128)(2,1)S(1)}, bf16[192,768]{1,0:T(8,128)(2,1)S(1)}, u32[]{:S(2)}, u32[]{:S(2)}) collective-permute-start(bf16[192,768]{1,0:T(8,128)(2,1)S(1)} %get-tuple-element.141), channel_id=1, source_target_pairs={{2,0},{4,2},{6,4},{8,6},{10,8},{12,10},{14,12},{16,14},{18,16},{20... | collective-permute-start | bytes 884744 | tf_op jit(solution)/shard_map/ppermute | solution.py:1458
  229.4 24.7 %collective-permute-start.31 = (bf16[192,768]{1,0:T(8,128)(2,1)S(1)}, bf16[192,768]{1,0:T(8,128)(2,1)S(1)}, u32[]{:S(2)}, u32[]{:S(2)}) collective-permute-start(bf16[192,768]{1,0:T(8,128)(2,1)S(1)} %get-tuple-element.142), channel_id=1, source_target_pairs={{0,2},{2,4},{4,6},{6,8},{8,10},{10,12},{12,14},{14,16},{16,18},{18... | collective-permute-start | bytes 884744 | tf_op jit(solution)/shard_map/ppermute | solution.py:1459
  231.3 29.9 %collective-permute-start.35 = (bf16[192,384]{1,0:T(8,128)(2,1)S(1)}, bf16[192,384]{1,0:T(8,128)(2,1)S(1)}, u32[]{:S(2)}, u32[]{:S(2)}) collective-permute-start(bf16[192,384]{1,0:T(8,128)(2,1)S(1)} %get-tuple-element.149.small_ref), channel_id=1, source_target_pairs={{0,8},{2,10},{4,12},{6,14},{8,0},{10,2},{12,4},{14,6},{16,24},{18,... | collective-permute-start | bytes 442376 | tf_op jit(solution)/shard_map/ppermute | solution.py:34
  256.8 29.9 %collective-permute-start.32 = (bf16[2,128,768]{2,1,0:T(8,128)(2,1)S(1)}, bf16[2,128,768]{2,1,0:T(8,128)(2,1)S(1)}, u32[]{:S(2)}, u32[]{:S(2)}) collective-permute-start(bf16[2,128,768]{2,1,0:T(8,128)(2,1)S(1)} %get-tuple-element.145), channel_id=1, source_target_pairs={{0,1},{1,0},{2,3},{3,2},{4,5},{5,4},{6,7},{7,6},{8,9},{9,8},{10,11... | collective-permute-start | bytes 1179656 | tf_op jit(solution)/shard_map/ppermute | solution.py:1120
  260.1 1.2 copy-start.1
  260.1 1.4 copy-start.3
  260.1 1.7 copy-start.4
  260.1 2.0 copy-start.5
  260.1 2.2 copy-start.6
  260.1 2.5 copy-start.7
  260.1 2.8 copy-start.8
  260.1 2.8 copy-start.9
  260.2 2.9 copy-start.10
  260.2 2.9 copy-start.12
  260.2 2.8 copy-start.13
  261.1 25.0 %collective-permute-start.34 = (bf16[2,2,768]{2,1,0:T(2,128)(2,1)S(1)}, bf16[2,2,768]{2,1,0:T(2,128)(2,1)S(1)}, u32[]{:S(2)}, u32[]{:S(2)}) collective-permute-start(bf16[2,2,768]{2,1,0:T(2,128)(2,1)S(1)} %get-tuple-element.148), channel_id=1, source_target_pairs={{0,1},{1,0},{2,3},{3,2},{4,5},{5,4},{6,7},{7,6},{8,9},{9,8},{10,11... | collective-permute-start | bytes 18440 | tf_op jit(solution)/shard_map/ppermute | solution.py:1120
  (2 other events, 2.3 us)

commit v2 on v1

--- a/solution.py
+++ b/solution.py
@@ -87,7 +87,7 @@
     for waits, (one, two), out, base, rows in sums:
         for wait in waits:
             wait.wait()
-        step = next(s for s in (128, 64, 48, 32, 16) if rows % s == 0)
+        step = next(s for s in (128, 112, 64, 48, 32, 16) if rows % s == 0)
 
         def add(i, carry):
             at = pl.multiple_of(i * step, 16)
@@ -361,6 +361,23 @@
         mats = [dot_six(x, y, 1, 0) for x, y in zip(new_l + new_r, lefts + rights)]
         thirds = [split_three(x) for x in mats]
         grams = [dot_on(left_six(p, 0), right_six(p, 0), 0, 0) for p in thirds]
+        for k, i in enumerate(slots):
+            given[5, i] = new_l[k]
+            given[6, i] = new_r[k]
+            for kind in range(2):
+                mat_ref[2 * i + kind] = mats[kind * many + k]
+                rows = pl.ds(pl.multiple_of((2 * i + kind) * side, side), side)
+                a_ref[rows, :] = grams[kind * many + k]
+                y_ref[rows, :] = eye
+        return carry
+
+    def rotate(slots):
+        def old(kind):
+            return [state[kind][i] for i in slots]
+
+        lefts, rights = old(3), old(4)
+        tiles = [slice(i * side, (i + 1) * side) for i in slots]
+        grads = [kept_ref[rows, :].astype(F32) + got_ref[rows, :].astype(F32) for rows in tiles]
         turned = [dot_one(x, y, 0, 0) for x, y in zip(lefts, grads)]
         rotated = [dot_one(x, y, 1, 0) for x, y in zip(turned, rights)]
         moms = [BETA_ONE * old_m + (1.0 - BETA_ONE) * x for old_m, x in zip(old(1), rotated)]
@@ -371,19 +388,10 @@
         ]
         turned = [dot_one(x, y, 1, 0) for x, y in zip(lefts, steps)]
         backs = [dot_one(x, y, 1, 1) for x, y in zip(turned, rights)]
-        weights = old(0)
-        for k, i in enumerate(slots):
-            given[0, i] = weights[k] - LEARN_RATE * (backs[k] + WEIGHT_DECAY * weights[k])
+        for k, (i, weight) in enumerate(zip(slots, old(0))):
+            given[0, i] = weight - LEARN_RATE * (backs[k] + WEIGHT_DECAY * weight)
             given[1, i] = moms[k]
             given[2, i] = secs[k]
-            given[5, i] = new_l[k]
-            given[6, i] = new_r[k]
-            for kind in range(2):
-                mat_ref[2 * i + kind] = mats[kind * many + k]
-                rows = pl.ds(pl.multiple_of((2 * i + kind) * side, side), side)
-                a_ref[rows, :] = grams[kind * many + k]
-                y_ref[rows, :] = eye
-        return carry
 
     def send(kinds):
         copies = [pltpu.make_async_copy(given.at[k], done[k], out_sems.at[k]) for k in kinds]
@@ -392,10 +400,12 @@
         return copies
 
     lax.fori_loop(0, n // many, first, 0)
-    copies = send((0, 1, 2, 5, 6))
+    copies = send((5, 6))
     if npad > 2 * n:
         a_ref[2 * n * side :, :] = jnp.concatenate([eye] * (npad - 2 * n), axis=0)
     for at in range(0, side, PANEL):
+        beside = range(at * n // side, (at + PANEL) * n // side)
+        rotate(list(beside))
         panel_inverse(a_ref, t_ref, npad, side, at)
 
         def update(i, carry):
@@ -425,18 +435,26 @@
 
         lax.fori_loop(0, 2 * n // batch, update, 0)
 
-    def last(i, carry):
-        mats = [mat_ref[2 * i], mat_ref[2 * i + 1]]
-        rows = [pl.ds(pl.multiple_of((2 * i + k) * side, side), side) for k in range(2)]
-        turns = [y_ref[r, :] for r in rows]
-        left, right = [dot_three(x, y, 1, 1) for x, y in zip(mats, turns)]
-        given[3, i] = left
-        given[4, i] = right
+    copies += send((0, 1, 2))
+
+    def last(at, carry):
+        slots = [at * many + k for k in range(many)]
+        both = [2 * i + k for i in slots for k in range(2)]
+        mats = [mat_ref[j] for j in both]
+        turns = [y_ref[pl.ds(pl.multiple_of(j * side, side), side), :] for j in both]
+        bases = [dot_three(x, y, 1, 1) for x, y in zip(mats, turns)]
+        for k, i in enumerate(slots):
+            for kind in range(2):
+                given[3 + kind, i] = bases[2 * k + kind]
+                target = done[3 + kind].at[i]
+                pltpu.make_async_copy(given.at[3 + kind, i], target, out_sems.at[3 + kind]).start()
         return carry
 
-    lax.fori_loop(0, n, last, 0)
-    for copy in copies + send((3, 4)):
+    lax.fori_loop(0, n // many, last, 0)
+    for copy in copies:
         copy.wait()
+    for kind in (3, 4):
+        pltpu.make_async_copy(given.at[kind], done[kind], out_sems.at[kind]).wait()
 
 
 def soap_update(grads, small, state, others):
@@ -575,11 +593,12 @@
         shift = (at % rows) % lanes
         part = grid[at : at + 8]
         parts.append(part if shift == 0 else pltpu.roll(part, lanes - shift, 1))
-    moved = jnp.concatenate(parts, axis=0)
+    moved = jnp.concatenate([part[:, :width] for part in parts], axis=0)
+    lanes = width
     index = lax.broadcasted_iota(jnp.int32, moved.shape, 0)
     for bit in (1, 2, 4):
         moved = jnp.where((index & bit) != 0, pltpu.roll(moved, lanes - bit, 1), moved)
-    return moved[:, :width]
+    return moved
 
 
 def softmax_rows(scores):

time: 288 us -> 285 us (0.990)
  Pallas kernels: 102 us -> 98.3 us
  transfers between devices with their start and end apart: 36 -> 36, of which waited for: 17 -> 17; matrix products, arithmetic and copies ran while one was open for 3% -> 3% of each run, Pallas kernels for 16% -> 15%
where the time goes in v2:
time: 285 us; the launch traced here: 284 us
  waiting for transfers between devices  128 us (45%)
  Pallas kernels  98.3 us (34%)
  starting transfers between devices  41.9 us (15%)
  other arithmetic  7.27 us (3%)
  local copies, waits for them, and re-layouts  7.26 us (3%)
    ppermute x25, waiting for transfers between devices, swap_with(): return lax.ppermute(values, 'seq', [(i, i ^ bit) for i in range(count)])  101 us
    ppermute x25, starting transfers between devices, swap_with(): return lax.ppermute(values, 'seq', [(i, i ^ bit) for i in range(count)])  23.8 us
    pallas_call x1, Pallas kernels, on_device(): kernel_call(functools.partial(attend_back_kernel, dims, seq_count, attn_t...  23.1 us
    pallas_call x1, Pallas kernels, soap_update(): pl.pallas_call(functools.partial(soap_kernel, npad), grid=(1,), out_shape...  20.7 us
    ppermute x1, waiting for transfers between devices, on_device(): lax.ppermute(to_last, 'seq', [(i + 1, i) for i in range(seq_count - 1)])  20 us
    pallas_call x11, Pallas kernels, move_rows(): pl.pallas_call(functools.partial(move_kernel, plan, len(arrays)), grid=(1...  16.5 us
    pallas_call x1, Pallas kernels, on_device(): kernel_call(functools.partial(attend_kernel, dims, wall_at, seq_count), '...  14.3 us
    ppermute x8, starting transfers between devices, swap_cores(): return lax.ppermute(values, 'ffn', [(i, i ^ 1) for i in range(count)])  9.65 us
  transfers between devices with their start and end apart: 36, of which 17 were waited for; matrix products, arithmetic and copies ran while one was open for 3% of the time, Pallas kernels for 15%

profile of v2, /device:TPU:17, one launch (start us, length us, event | category | flops | bytes accessed | tf_op | source)
XLA Modules:
  0.0 284.1 jit_solution(4553437069006556583)
XLA Ops:
  0.7 0.7 collective-permute-start.4
  1.4 1.3 convert_element_type.14
  3.2 0.8 join_rows.5
  4.0 3.1 %collective-permute-start.1 = (bf16[192,768]{1,0:T(8,128)(2,1)S(1)}, bf16[192,768]{1,0:T(8,128)(2,1)}, u32[]{:S(2)}, u32[]{:S(2)}) collective-permute-start(bf16[192,768]{1,0:T(8,128)(2,1)S(1)} %get-tuple-element.91), channel_id=1, source_target_pairs={{1,3},{3,5},{5,7},{7,9},{9,11},{11,13},{13,15},{15,17},{17,19},{19... | collective-permute-start | bytes 884744 | tf_op jit(solution)/shard_map/ppermute | solution.py:1284
  7.1 3.9 %collective-permute-start = (bf16[2,264,768]{2,1,0:T(8,128)(2,1)S(1)}, bf16[2,264,768]{2,1,0:T(8,128)(2,1)}, u32[]{:S(2)}, u32[]{:S(2)}) collective-permute-start(bf16[2,264,768]{2,1,0:T(8,128)(2,1)S(1)} %bitcast.24), channel_id=1, source_target_pairs={{0,1},{1,0},{2,3},{3,2},{4,5},{5,4},{6,7},{7,6},{8,9},{9,8},{10,11... | collective-permute-start | bytes 2433032 | tf_op jit(solution)/shard_map/ppermute | solution.py:1139
  11.4 11.8 %collective-permute-done.5.refs_3_ = bf16[48,128]{1,0:T(8,128)(2,1)S(1)} collective-permute-done((bf16[48,128]{1,0:T(8,128)(2,1)S(1)}, bf16[48,128]{1,0:T(8,128)(2,1)S(1)}, u32[]{:S(2)}, u32[]{:S(2)}) %collective-permute-start.5) | collective-permute-done | bytes 12320 | tf_op jit(solution)/shard_map/ppermute | solution.py:34
  23.2 1.3 join_rows.6
  24.5 1.1 collective-permute-start.8
  25.6 4.7 %collective-permute-start.6 = (bf16[1280,128]{1,0:T(8,128)(2,1)S(1)}, bf16[1280,128]{1,0:T(8,128)(2,1)S(1)}, u32[]{:S(2)}, u32[]{:S(2)}) collective-permute-start(bf16[1280,128]{1,0:T(8,128)(2,1)S(1)} %get-tuple-element.92.refs_0_), channel_id=1, source_target_pairs={{0,8},{2,10},{4,12},{6,14},{8,0},{10,2},{12,4},{14,6},{16,24},{18,... | collective-permute-start | bytes 983048 | tf_op jit(solution)/shard_map/ppermute | solution.py:34
  30.3 4.1 %collective-permute-start.7 = (bf16[1280,128]{1,0:T(8,128)(2,1)S(1)}, bf16[1280,128]{1,0:T(8,128)(2,1)S(1)}, u32[]{:S(2)}, u32[]{:S(2)}) collective-permute-start(bf16[1280,128]{1,0:T(8,128)(2,1)S(1)} %get-tuple-element.93.refs_2_), channel_id=1, source_target_pairs={{0,2},{2,0},{4,6},{6,4},{8,10},{10,8},{12,14},{14,12},{16,18},{18,... | collective-permute-start | bytes 983048 | tf_op jit(solution)/shard_map/ppermute | solution.py:34
  34.7 0.5 collective-permute-done.8.refs_5_
  35.3 2.4 collective-permute-done.6.refs_1_
  37.6 3.5 %collective-permute-done.7.refs_3_ = bf16[1280,128]{1,0:T(8,128)(2,1)S(1)} collective-permute-done((bf16[1280,128]{1,0:T(8,128)(2,1)S(1)}, bf16[1280,128]{1,0:T(8,128)(2,1)S(1)}, u32[]{:S(2)}, u32[]{:S(2)}) %collective-permute-start.7) | collective-permute-done | bytes 327712 | tf_op jit(solution)/shard_map/ppermute | solution.py:34
  41.2 0.6 join_rows.7
  42.5 0.5 collective-permute-start.2
  43.6 0.9 collective-permute-done.2
  44.4 1.0 broadcast_select_fusion.2
  45.5 12.1 %collective-permute-done.11.refs_5_ = bf16[2240,128]{1,0:T(8,128)(2,1)S(1)} collective-permute-done((bf16[2240,128]{1,0:T(8,128)(2,1)S(1)}, bf16[2240,128]{1,0:T(8,128)(2,1)S(1)}, u32[]{:S(2)}, u32[]{:S(2)}) %collective-permute-start.11) | collective-permute-done | bytes 573472 | tf_op jit(solution)/shard_map/ppermute | solution.py:34
  57.6 0.9 collective-permute-done.9.refs_1_
  58.5 2.9 %join_rows.8 = (bf16[5120,128]{1,0:T(8,128)(2,1)}, bf16[5120,128]{1,0:T(8,128)(2,1)}, bf16[4480,128]{1,0:T(8,128)(2,1)}) custom-call(bf16[2560,128]{1,0:T(8,128)(2,1)S(1)} %get-tuple-element.95.refs_0_, bf16[2560,128]{1,0:T(8,128)(2,1)S(1)} %collective-permute-done.9.refs_1_, bf16[2560,128]{1,0:T(8,128)(2,1)S(1)} %get-tuple-element.96.refs_2_, ...), custom_call_target="tpu_custom_call" | custom-call | bytes 11304960 | tf_op jit(solution)/shard_map/join_rows/pallas_call | solution.py:119
  61.5 1.5 collective-permute-start.12
  62.9 1.3 collective-permute-start.13
  64.3 2.4 broadcast_select_fusion.1
  66.7 0.8 fusion.16
  67.6 1.5 fusion.14
  69.5 23.3 %collective-permute-done.14 = bf16[4480,128]{1,0:T(8,128)(2,1)} collective-permute-done((bf16[4480,128]{1,0:T(8,128)(2,1)}, bf16[4480,128]{1,0:T(8,128)(2,1)}, u32[]{:S(2)}, u32[]{:S(2)}) %collective-permute-start.14) | collective-permute-done | bytes 1146912 | tf_op jit(solution)/shard_map/ppermute | solution.py:34
  92.8 14.3 %attend.1 = (bf16[528,384]{1,0:T(8,128)(2,1)S(1)}, bf16[1024,384]{1,0:T(8,128)(2,1)S(1)}, bf16[1024,384]{1,0:T(8,128)(2,1)S(1)}, bf16[528,384]{1,0:T(8,128)(2,1)...) custom-call(s32[224]{0:T(256)S(1)} %get-tuple-element.185.row_ref, ...), custom_call_target="tpu_custom_call" | custom-call | flops 4000000000 | bytes 10000000 | tf_op jit(solution)/shard_map/attend/pallas_call | solution.py:1335
  107.1 1.9 collective-permute-start.15
  109.1 1.9 collective-permute-done.15.got_ref
  111.0 5.3 %feed.1 = (f32[528,768]{1,0:T(8,128)S(1)}, bf16[528,768]{1,0:T(8,128)(2,1)S(1)}, f32[528,1536]{1,0:T(8,128)S(1)}, bf16[528,1536]{1,0:T(8,128)(2,1)S(1)}, bf16[528,768]{1,0:T(8,128)(2,1)S(1)}) custom-call(bf16[528,768]{1,0:T(8,128)(2,1)S(1)} %get-tuple-element.182.xr_ref, bf16[528,768]{1,0:T(8,128)(2,1)S(1)} %get-tuple-element.101.part_ref, ...), custom_call_target="tpu_custom_call" | custom-call | flops 3000000000 | bytes 10000000 | tf_op jit(solution)/shard_map/feed/pallas_call | solution.py:1359
  116.8 1.9 collective-permute-done.16.got_ref
  118.8 7.3 %feed_back.1 = (bf16[2,128,768]{2,1,0:T(8,128)(2,1)}, bf16[2,2,768]{2,1,0:T(2,128)(2,1)}, f32[528,768]{1,0:T(8,128)S(1)}, bf16[528,768]{1,0:T(8,128)(2,1)S(1)}, ...) custom-call(s32[1]{0:T(128)} %bitcast.half_ref, ...), custom_call_target="tpu_custom_call" | custom-call | flops 3000000000 | bytes 10000000 | tf_op jit(solution)/shard_map/feed_back/pallas_call | solution.py:1381
  126.0 1.2 copy-done.14
  127.6 7.5 %feed_grads.1.grads_in = bf16[29440,128]{1,0:T(8,128)(2,1)S(1)} custom-call(s32[224]{0:T(256)S(1)} %get-tuple-element.163.place_ref, bf16[528,1536]{1,0:T(8,128)(2,1)S(1)} %get-tuple-element.116.a_ref, bf16[528,768]{1,0:T(8,128)(2,1)S(1)} %get-tuple-element.117.dxb_ref, bf16[528,768]{1,0:T(8,128)(2,1)S(1)} %get-tuple-element.118.hb_ref, ...), custom_call_target="tpu_custom_call" | custom-call | flops 3000000000 | bytes 10000000 | tf_op jit(solution)/shard_map/feed_grads/pallas_call | solution.py:1396
  135.2 1.1 copy-done.17
  136.3 23.1 %attend_back.1 = (bf16[29440,128]{1,0:T(8,128)(2,1)S(1)}, bf16[528,384]{1,0:T(8,128)(2,1)S(1)}, bf16[1024,768]{1,0:T(8,128)(2,1)S(1)}, f32[528,768]{1,0:T(8,128)S(1)}, bf16[192,384]{1,0:T(8,128)(2,1)S(1)}) custom-call(s32[1]{0:T(128)} %bitcast.6.block_ref, s32[224]{0:T(256)S(1)} %get-tuple-element.163.place_ref, ...), custom_call_target="tpu_custom_call", output_to_operand_aliasing={{0}: (18, {})} | custom-call | flops 8000000000 | bytes 20000000 | tf_op jit(solution)/shard_map/attend_back/pallas_call | solution.py:1431
  159.6 1.1 collective-permute-start.19
  161.1 0.7 collective-permute-start.21
  162.2 27.4 %collective-permute-done.21.refs_7_ = bf16[192,384]{1,0:T(8,128)(2,1)S(1)} collective-permute-done((bf16[192,384]{1,0:T(8,128)(2,1)S(1)}, bf16[192,384]{1,0:T(8,128)(2,1)S(1)}, u32[]{:S(2)}, u32[]{:S(2)}) %collective-permute-start.21) | collective-permute-done | bytes 147488 | tf_op jit(solution)/shard_map/ppermute | solution.py:34
  189.9 0.8 collective-permute-done.18.refs_1_
  190.7 2.3 add_rows.7
  193.4 1.0 collective-permute-start.24
  194.4 0.5 collective-permute-start.25
  194.9 1.8 add_rows.6
  196.7 12.5 %collective-permute-done.25.refs_7_ = bf16[192,384]{1,0:T(8,128)(2,1)S(1)} collective-permute-done((bf16[192,384]{1,0:T(8,128)(2,1)S(1)}, bf16[192,384]{1,0:T(8,128)(2,1)S(1)}, u32[]{:S(2)}, u32[]{:S(2)}) %collective-permute-start.25) | collective-permute-done | bytes 147488 | tf_op jit(solution)/shard_map/ppermute | solution.py:34
  209.2 1.4 add_rows.9
  210.6 1.5 collective-permute-start.26
  212.2 1.1 collective-permute-start.28
  213.7 0.9 add_rows.8
  214.7 5.8 %collective-permute-done.29.refs_7_ = bf16[192,384]{1,0:T(8,128)(2,1)S(1)} collective-permute-done((bf16[192,384]{1,0:T(8,128)(2,1)S(1)}, bf16[192,384]{1,0:T(8,128)(2,1)S(1)}, u32[]{:S(2)}, u32[]{:S(2)}) %collective-permute-start.29) | collective-permute-done | bytes 147488 | tf_op jit(solution)/shard_map/ppermute | solution.py:34
  220.4 2.7 add_rows.10
  223.2 1.8 collective-permute-start.33
  224.9 3.4 %collective-permute-start.30 = (bf16[192,768]{1,0:T(8,128)(2,1)S(1)}, bf16[192,768]{1,0:T(8,128)(2,1)S(1)}, u32[]{:S(2)}, u32[]{:S(2)}) collective-permute-start(bf16[192,768]{1,0:T(8,128)(2,1)S(1)} %get-tuple-element.141), channel_id=1, source_target_pairs={{2,0},{4,2},{6,4},{8,6},{10,8},{12,10},{14,12},{16,14},{18,16},{20... | collective-permute-start | bytes 884744 | tf_op jit(solution)/shard_map/ppermute | solution.py:1477
  228.3 1.9 collective-permute-start.31
  230.3 0.9 collective-permute-start.35
  231.2 20.0 %collective-permute-done.30.next_ref = bf16[192,768]{1,0:T(8,128)(2,1)S(1)} collective-permute-done((bf16[192,768]{1,0:T(8,128)(2,1)S(1)}, bf16[192,768]{1,0:T(8,128)(2,1)S(1)}, u32[]{:S(2)}, u32[]{:S(2)}) %collective-permute-start.30) | collective-permute-done | bytes 294944 | tf_op jit(solution)/shard_map/ppermute | solution.py:1477
  251.2 1.8 collective-permute-done.31.last_ref
  253.0 2.7 dx_long.1
  255.7 1.7 collective-permute-start.32
  257.4 1.4 add_rows.11.kept_ref
  259.0 0.9 dx_glob.1
  261.8 20.7 %soap.1 = (f32[14,128,128]{2,1,0:T(8,128)}, f32[14,128,128]{2,1,0:T(8,128)}, f32[14,128,128]{2,1,0:T(8,128)}, f32[14,128,128]{2,1,0:T(8,128)}, f32[14,128,128]{2...) custom-call(bf16[1840,128]{1,0:T(8,128)(2,1)S(1)} %add_rows.11.kept_, ...), custom_call_target="tpu_custom_call" | custom-call | flops 1174405120 | bytes 13762560 | tf_op jit(solution)/shard_map/soap/pallas_call | solution.py:465
  282.5 0.6 convert_add_fusion.1
  283.1 1.0 convert_add_fusion
  (125 shorter events, 7.8 us)
Async XLA Ops:
  0.7 2.2 copy-start.24
  0.7 2.1 copy-start.22
  0.7 2.2 copy-start.25
  0.7 2.2 copy-start.23
  0.7 10.5 %collective-permute-start.4 = (bf16[2,2,768]{2,1,0:T(2,128)(2,1)}, bf16[2,2,768]{2,1,0:T(2,128)(2,1)S(1)}, u32[]{:S(2)}, u32[]{:S(2)}) collective-permute-start(bf16[2,2,768]{2,1,0:T(2,128)(2,1)} %param.20), channel_id=1, source_target_pairs={{0,1},{1,0},{2,3},{3,2},{4,5},{5,4},{6,7},{7,6},{8,9},{9,8},{10,11... | collective-permute-start | bytes 18440 | tf_op jit(solution)/shard_map/ppermute | solution.py:1139
  2.7 20.5 %collective-permute-start.3 = (bf16[1792,128]{1,0:T(8,128)(2,1)S(1)}, bf16[1792,128]{1,0:T(8,128)(2,1)S(1)}, u32[]{:S(2)}, u32[]{:S(2)}) collective-permute-start(bf16[1792,128]{1,0:T(8,128)(2,1)S(1)} %bitcast.19), channel_id=1, source_target_pairs={{0,16},{2,18},{4,20},{6,22},{8,24},{10,26},{12,28},{14,30},{16,0},... | collective-permute-start | bytes 1376264 | tf_op jit(solution)/shard_map/ppermute | solution.py:34
  2.9 8.1 %copy-start.26 = (s32[224]{0:T(256)S(1)}, s32[224]{0:T(256)}, u32[]{:S(2)}) copy-start(s32[224]{0:T(256)} %param.24) | copy-start | bytes 2692
  3.2 31.3 %copy-start.27 = (s32[2,1,256]{2,1,0:T(1,128)S(1)}, s32[2,1,256]{2,1,0:T(1,128)}, u32[]{:S(2)}) copy-start(s32[2,1,256]{2,1,0:T(1,128)} %param.21) | copy-start | bytes 6148
  3.2 31.3 %copy-start.2 = (f32[169,384]{1,0:T(8,128)S(1)}, f32[169,384]{1,0:T(8,128)}, u32[]{:S(2)}) copy-start(f32[169,384]{1,0:T(8,128)} %refs_7_.1) | copy-start | bytes 778756
  4.0 38.5 %collective-permute-start.1 = (bf16[192,768]{1,0:T(8,128)(2,1)S(1)}, bf16[192,768]{1,0:T(8,128)(2,1)}, u32[]{:S(2)}, u32[]{:S(2)}) collective-permute-start(bf16[192,768]{1,0:T(8,128)(2,1)S(1)} %get-tuple-element.91), channel_id=1, source_target_pairs={{1,3},{3,5},{5,7},{7,9},{9,11},{11,13},{13,15},{15,17},{17,19},{19... | collective-permute-start | bytes 884744 | tf_op jit(solution)/shard_map/ppermute | solution.py:1284
  7.1 57.1 %collective-permute-start = (bf16[2,264,768]{2,1,0:T(8,128)(2,1)S(1)}, bf16[2,264,768]{2,1,0:T(8,128)(2,1)}, u32[]{:S(2)}, u32[]{:S(2)}) collective-permute-start(bf16[2,264,768]{2,1,0:T(8,128)(2,1)S(1)} %bitcast.24), channel_id=1, source_target_pairs={{0,1},{1,0},{2,3},{3,2},{4,5},{5,4},{6,7},{7,6},{8,9},{9,8},{10,11... | collective-permute-start | bytes 2433032 | tf_op jit(solution)/shard_map/ppermute | solution.py:1139
  11.3 11.9 %collective-permute-start.5 = (bf16[48,128]{1,0:T(8,128)(2,1)S(1)}, bf16[48,128]{1,0:T(8,128)(2,1)S(1)}, u32[]{:S(2)}, u32[]{:S(2)}) collective-permute-start(bf16[48,128]{1,0:T(8,128)(2,1)S(1)} %reshape.131.refs_2_), channel_id=1, source_target_pairs={{0,16},{2,18},{4,20},{6,22},{8,24},{10,26},{12,28},{14,30},{16,0},... | collective-permute-start | bytes 36872 | tf_op jit(solution)/shard_map/ppermute | solution.py:34
  24.5 10.8 %collective-permute-start.8 = (bf16[1120,128]{1,0:T(8,128)(2,1)S(1)}, bf16[1120,128]{1,0:T(8,128)(2,1)S(1)}, u32[]{:S(2)}, u32[]{:S(2)}) collective-permute-start(bf16[1120,128]{1,0:T(8,128)(2,1)S(1)} %get-tuple-element.94.refs_4_), channel_id=1, source_target_pairs={{0,4},{2,6},{4,0},{6,2},{8,12},{10,14},{12,8},{14,10},{16,20},{18,... | collective-permute-start | bytes 860168 | tf_op jit(solution)/shard_map/ppermute | solution.py:34
  25.6 12.1 %collective-permute-start.6 = (bf16[1280,128]{1,0:T(8,128)(2,1)S(1)}, bf16[1280,128]{1,0:T(8,128)(2,1)S(1)}, u32[]{:S(2)}, u32[]{:S(2)}) collective-permute-start(bf16[1280,128]{1,0:T(8,128)(2,1)S(1)} %get-tuple-element.92.refs_0_), channel_id=1, source_target_pairs={{0,8},{2,10},{4,12},{6,14},{8,0},{10,2},{12,4},{14,6},{16,24},{18,... | collective-permute-start | bytes 983048 | tf_op jit(solution)/shard_map/ppermute | solution.py:34
  30.3 10.9 %collective-permute-start.7 = (bf16[1280,128]{1,0:T(8,128)(2,1)S(1)}, bf16[1280,128]{1,0:T(8,128)(2,1)S(1)}, u32[]{:S(2)}, u32[]{:S(2)}) collective-permute-start(bf16[1280,128]{1,0:T(8,128)(2,1)S(1)} %get-tuple-element.93.refs_2_), channel_id=1, source_target_pairs={{0,2},{2,0},{4,6},{6,4},{8,10},{10,8},{12,14},{14,12},{16,18},{18,... | collective-permute-start | bytes 983048 | tf_op jit(solution)/shard_map/ppermute | solution.py:34
  41.8 16.7 %collective-permute-start.9 = (bf16[2560,128]{1,0:T(8,128)(2,1)S(1)}, bf16[2560,128]{1,0:T(8,128)(2,1)S(1)}, u32[]{:S(2)}, u32[]{:S(2)}) collective-permute-start(bf16[2560,128]{1,0:T(8,128)(2,1)S(1)} %get-tuple-element.95.refs_0_), channel_id=1, source_target_pairs={{0,4},{2,6},{4,0},{6,2},{8,12},{10,14},{12,8},{14,10},{16,20},{18,... | collective-permute-start | bytes 1966088 | tf_op jit(solution)/shard_map/ppermute | solution.py:34
  42.1 16.5 %collective-permute-start.10 = (bf16[2560,128]{1,0:T(8,128)(2,1)S(1)}, bf16[2560,128]{1,0:T(8,128)(2,1)S(1)}, u32[]{:S(2)}, u32[]{:S(2)}) collective-permute-start(bf16[2560,128]{1,0:T(8,128)(2,1)S(1)} %get-tuple-element.96.refs_2_), channel_id=1, source_target_pairs={{0,8},{2,10},{4,12},{6,14},{8,0},{10,2},{12,4},{14,6},{16,24},{18,... | collective-permute-start | bytes 1966088 | tf_op jit(solution)/shard_map/ppermute | solution.py:34
  42.5 1.9 collective-permute-start.2
  43.0 14.6 %collective-permute-start.11 = (bf16[2240,128]{1,0:T(8,128)(2,1)S(1)}, bf16[2240,128]{1,0:T(8,128)(2,1)S(1)}, u32[]{:S(2)}, u32[]{:S(2)}) collective-permute-start(bf16[2240,128]{1,0:T(8,128)(2,1)S(1)} %get-tuple-element.97.refs_4_), channel_id=1, source_target_pairs={{0,2},{2,0},{4,6},{6,4},{8,10},{10,8},{12,14},{14,12},{16,18},{18,... | collective-permute-start | bytes 1720328 | tf_op jit(solution)/shard_map/ppermute | solution.py:34
  61.5 31.3 %collective-permute-start.12 = (bf16[5120,128]{1,0:T(8,128)(2,1)}, bf16[5120,128]{1,0:T(8,128)(2,1)}, u32[]{:S(2)}, u32[]{:S(2)}) collective-permute-start(bf16[5120,128]{1,0:T(8,128)(2,1)} %get-tuple-element.98), channel_id=1, source_target_pairs={{0,2},{2,0},{4,6},{6,4},{8,10},{10,8},{12,14},{14,12},{16,18},{18,... | collective-permute-start | bytes 3932168 | tf_op jit(solution)/shard_map/ppermute | solution.py:34
  62.9 29.9 %collective-permute-start.13 = (bf16[5120,128]{1,0:T(8,128)(2,1)}, bf16[5120,128]{1,0:T(8,128)(2,1)}, u32[]{:S(2)}, u32[]{:S(2)}) collective-permute-start(bf16[5120,128]{1,0:T(8,128)(2,1)} %get-tuple-element.99), channel_id=1, source_target_pairs={{0,4},{2,6},{4,0},{6,2},{8,12},{10,14},{12,8},{14,10},{16,20},{18,... | collective-permute-start | bytes 3932168 | tf_op jit(solution)/shard_map/ppermute | solution.py:34
  66.7 26.1 %collective-permute-start.14 = (bf16[4480,128]{1,0:T(8,128)(2,1)}, bf16[4480,128]{1,0:T(8,128)(2,1)}, u32[]{:S(2)}, u32[]{:S(2)}) collective-permute-start(bf16[4480,128]{1,0:T(8,128)(2,1)} %get-tuple-element.100), channel_id=1, source_target_pairs={{0,8},{2,10},{4,12},{6,14},{8,0},{10,2},{12,4},{14,6},{16,24},{18,... | collective-permute-start | bytes 3440648 | tf_op jit(solution)/shard_map/ppermute | solution.py:34
  92.8 18.2 %copy-start.11 = (f32[4,768]{1,0:T(4,128)S(1)}, f32[4,768]{1,0:T(4,128)}, u32[]{:S(2)}) copy-start(f32[4,768]{1,0:T(4,128)} %refs_10_.1) | copy-start | bytes 36868
  107.1 9.2 %copy-start.18 = (bf16[1024,768]{1,0:T(8,128)(2,1)}, bf16[1024,768]{1,0:T(8,128)(2,1)S(1)}, u32[]{:S(2)}) copy-start(bf16[1024,768]{1,0:T(8,128)(2,1)S(1)} %get-tuple-element.115.xe_ref) | copy-start | bytes 4718596
  107.1 9.2 %copy-start.20 = (bf16[1024,384]{1,0:T(8,128)(2,1)}, bf16[1024,384]{1,0:T(8,128)(2,1)S(1)}, u32[]{:S(2)}) copy-start(bf16[1024,384]{1,0:T(8,128)(2,1)S(1)} %get-tuple-element.114.v_ref) | copy-start | bytes 2359300
  107.1 11.6 %copy-start = (bf16[4992,768]{1,0:T(8,128)(2,1)}, bf16[4992,768]{1,0:T(8,128)(2,1)S(1)}, u32[]{:S(2)}) copy-start(bf16[4992,768]{1,0:T(8,128)(2,1)S(1)} %get-tuple-element.102.wu_ref.wd_ref.wo_ref.wall_ref) | copy-start | bytes 23003140
  107.1 3.9 %collective-permute-start.15 = (bf16[528,768]{1,0:T(8,128)(2,1)S(1)}, bf16[528,768]{1,0:T(8,128)(2,1)S(1)}, u32[]{:S(2)}, u32[]{:S(2)}) collective-permute-start(bf16[528,768]{1,0:T(8,128)(2,1)S(1)} %get-tuple-element.101.part_ref), channel_id=1, source_target_pairs={{0,1},{1,0},{2,3},{3,2},{4,5},{5,4},{6,7},{7,6},{8,9},{9,8},{10,11... | collective-permute-start | bytes 2433032 | tf_op jit(solution)/shard_map/ppermute | solution.py:1139
  116.4 2.4 collective-permute-start.16
  127.2 7.9 %copy-start.16 = (bf16[528,768]{1,0:T(8,128)(2,1)}, bf16[528,768]{1,0:T(8,128)(2,1)S(1)}, u32[]{:S(2)}) copy-start(bf16[528,768]{1,0:T(8,128)(2,1)S(1)} %get-tuple-element.109.dh_ref) | copy-start | bytes 2433028
  127.2 7.9 %collective-permute-start.17 = (bf16[528,768]{1,0:T(8,128)(2,1)S(1)}, bf16[528,768]{1,0:T(8,128)(2,1)S(1)}, u32[]{:S(2)}, u32[]{:S(2)}) collective-permute-start(bf16[528,768]{1,0:T(8,128)(2,1)S(1)} %get-tuple-element.109.dh_ref), channel_id=1, source_target_pairs={{0,1},{1,0},{2,3},{3,2},{4,5},{5,4},{6,7},{7,6},{8,9},{9,8},{10,11... | collective-permute-start | bytes 2433032 | tf_op jit(solution)/shard_map/ppermute | solution.py:1139
  127.6 7.6 %copy-start.15 = (f32[528,768]{1,0:T(8,128)S(1)}, f32[528,768]{1,0:T(8,128)}, u32[]{:S(2)}) copy-start(f32[528,768]{1,0:T(8,128)} %copy-done.14) | copy-start | bytes 4866052
  127.6 7.6 %copy-start.19 = (bf16[1024,768]{1,0:T(8,128)(2,1)S(1)}, bf16[1024,768]{1,0:T(8,128)(2,1)}, u32[]{:S(2)}) copy-start(bf16[1024,768]{1,0:T(8,128)(2,1)} %copy-done.18) | copy-start | bytes 4718596
  127.6 7.6 %copy-start.21 = (bf16[1024,384]{1,0:T(8,128)(2,1)S(1)}, bf16[1024,384]{1,0:T(8,128)(2,1)}, u32[]{:S(2)}) copy-start(bf16[1024,384]{1,0:T(8,128)(2,1)} %copy-done.20) | copy-start | bytes 2359300
  159.6 30.3 %collective-permute-start.19 = (bf16[5120,128]{1,0:T(8,128)(2,1)S(1)}, bf16[5120,128]{1,0:T(8,128)(2,1)S(1)}, u32[]{:S(2)}, u32[]{:S(2)}) collective-permute-start(bf16[5120,128]{1,0:T(8,128)(2,1)S(1)} %get-tuple-element.165), channel_id=1, source_target_pairs={{0,4},{2,6},{4,0},{6,2},{8,12},{10,14},{12,8},{14,10},{16,20},{18,... | collective-permute-start | bytes 3932168 | tf_op jit(solution)/shard_map/ppermute | solution.py:34
  160.8 29.9 %collective-permute-start.18 = (bf16[5120,128]{1,0:T(8,128)(2,1)S(1)}, bf16[5120,128]{1,0:T(8,128)(2,1)S(1)}, u32[]{:S(2)}, u32[]{:S(2)}) collective-permute-start(bf16[5120,128]{1,0:T(8,128)(2,1)S(1)} %get-tuple-element.166), channel_id=1, source_target_pairs={{0,2},{2,0},{4,6},{6,4},{8,10},{10,8},{12,14},{14,12},{16,18},{18,... | collective-permute-start | bytes 3932168 | tf_op jit(solution)/shard_map/ppermute | solution.py:34
  160.9 28.7 %collective-permute-start.20 = (bf16[4480,128]{1,0:T(8,128)(2,1)S(1)}, bf16[4480,128]{1,0:T(8,128)(2,1)S(1)}, u32[]{:S(2)}, u32[]{:S(2)}) collective-permute-start(bf16[4480,128]{1,0:T(8,128)(2,1)S(1)} %slice.51), channel_id=1, source_target_pairs={{0,8},{2,10},{4,12},{6,14},{8,0},{10,2},{12,4},{14,6},{16,24},{18,... | collective-permute-start | bytes 3440648 | tf_op jit(solution)/shard_map/ppermute | solution.py:34
  161.1 28.5 %collective-permute-start.21 = (bf16[192,384]{1,0:T(8,128)(2,1)S(1)}, bf16[192,384]{1,0:T(8,128)(2,1)S(1)}, u32[]{:S(2)}, u32[]{:S(2)}) collective-permute-start(bf16[192,384]{1,0:T(8,128)(2,1)S(1)} %get-tuple-element.127.refs_6_), channel_id=1, source_target_pairs={{0,16},{2,18},{4,20},{6,22},{8,24},{10,26},{12,28},{14,30},{16,0},... | collective-permute-start | bytes 442376 | tf_op jit(solution)/shard_map/ppermute | solution.py:34
  193.0 16.3 %collective-permute-start.22 = (bf16[2560,128]{1,0:T(8,128)(2,1)S(1)}, bf16[2560,128]{1,0:T(8,128)(2,1)S(1)}, u32[]{:S(2)}, u32[]{:S(2)}) collective-permute-start(bf16[2560,128]{1,0:T(8,128)(2,1)S(1)} %get-tuple-element.128), channel_id=1, source_target_pairs={{0,4},{2,6},{4,0},{6,2},{8,12},{10,14},{12,8},{14,10},{16,20},{18,... | collective-permute-start | bytes 1966088 | tf_op jit(solution)/shard_map/ppermute | solution.py:34
  193.4 15.8 %collective-permute-start.23 = (bf16[2560,128]{1,0:T(8,128)(2,1)S(1)}, bf16[2560,128]{1,0:T(8,128)(2,1)S(1)}, u32[]{:S(2)}, u32[]{:S(2)}) collective-permute-start(bf16[2560,128]{1,0:T(8,128)(2,1)S(1)} %get-tuple-element.130), channel_id=1, source_target_pairs={{0,8},{2,10},{4,12},{6,14},{8,0},{10,2},{12,4},{14,6},{16,24},{18,... | collective-permute-start | bytes 1966088 | tf_op jit(solution)/shard_map/ppermute | solution.py:34
  193.4 15.8 %collective-permute-start.24 = (bf16[2240,128]{1,0:T(8,128)(2,1)S(1)}, bf16[2240,128]{1,0:T(8,128)(2,1)S(1)}, u32[]{:S(2)}, u32[]{:S(2)}) collective-permute-start(bf16[2240,128]{1,0:T(8,128)(2,1)S(1)} %get-tuple-element.132), channel_id=1, source_target_pairs={{0,2},{2,0},{4,6},{6,4},{8,10},{10,8},{12,14},{14,12},{16,18},{18,... | collective-permute-start | bytes 1720328 | tf_op jit(solution)/shard_map/ppermute | solution.py:34
  194.4 14.8 %collective-permute-start.25 = (bf16[192,384]{1,0:T(8,128)(2,1)S(1)}, bf16[192,384]{1,0:T(8,128)(2,1)S(1)}, u32[]{:S(2)}, u32[]{:S(2)}) collective-permute-start(bf16[192,384]{1,0:T(8,128)(2,1)S(1)} %get-tuple-element.134.refs_6_), channel_id=1, source_target_pairs={{0,2},{2,0},{4,6},{6,4},{8,10},{10,8},{12,14},{14,12},{16,18},{18,... | collective-permute-start | bytes 442376 | tf_op jit(solution)/shard_map/ppermute | solution.py:34
  194.9 58.2 %slice-start = ((s8[7667712]{0:T(1024)(128)(4,1)}), s8[4194304]{0:T(1024)(128)(4,1)S(1)}, s32[]{:S(2)}) async-start(s8[7667712]{0:T(1024)(128)(4,1)} %bitcast.17), calls=%async_computation | async-start | bytes 8388608
  209.2 43.8 %slice-start.1 = ((s8[7667712]{0:T(1024)(128)(4,1)}), s8[3473408]{0:T(1024)(128)(4,1)S(1)}, s32[]{:S(2)}) async-start(s8[7667712]{0:T(1024)(128)(4,1)} %bitcast.17), calls=%async_computation.1 | async-start | bytes 6946816
  210.6 9.8 %collective-permute-start.26 = (bf16[1280,128]{1,0:T(8,128)(2,1)S(1)}, bf16[1280,128]{1,0:T(8,128)(2,1)S(1)}, u32[]{:S(2)}, u32[]{:S(2)}) collective-permute-start(bf16[1280,128]{1,0:T(8,128)(2,1)S(1)} %get-tuple-element.135), channel_id=1, source_target_pairs={{0,8},{2,10},{4,12},{6,14},{8,0},{10,2},{12,4},{14,6},{16,24},{18,... | collective-permute-start | bytes 983048 | tf_op jit(solution)/shard_map/ppermute | solution.py:34
  212.2 8.3 %collective-permute-start.27 = (bf16[1280,128]{1,0:T(8,128)(2,1)S(1)}, bf16[1280,128]{1,0:T(8,128)(2,1)S(1)}, u32[]{:S(2)}, u32[]{:S(2)}) collective-permute-start(bf16[1280,128]{1,0:T(8,128)(2,1)S(1)} %get-tuple-element.137), channel_id=1, source_target_pairs={{0,2},{2,0},{4,6},{6,4},{8,10},{10,8},{12,14},{14,12},{16,18},{18,... | collective-permute-start | bytes 983048 | tf_op jit(solution)/shard_map/ppermute | solution.py:34
  212.2 8.2 %collective-permute-start.28 = (bf16[1120,128]{1,0:T(8,128)(2,1)S(1)}, bf16[1120,128]{1,0:T(8,128)(2,1)S(1)}, u32[]{:S(2)}, u32[]{:S(2)}) collective-permute-start(bf16[1120,128]{1,0:T(8,128)(2,1)S(1)} %get-tuple-element.139), channel_id=1, source_target_pairs={{0,4},{2,6},{4,0},{6,2},{8,12},{10,14},{12,8},{14,10},{16,20},{18,... | collective-permute-start | bytes 860168 | tf_op jit(solution)/shard_map/ppermute | solution.py:34
  213.3 7.1 %collective-permute-start.29 = (bf16[192,384]{1,0:T(8,128)(2,1)S(1)}, bf16[192,384]{1,0:T(8,128)(2,1)S(1)}, u32[]{:S(2)}, u32[]{:S(2)}) collective-permute-start(bf16[192,384]{1,0:T(8,128)(2,1)S(1)} %get-tuple-element.140.refs_6_), channel_id=1, source_target_pairs={{0,4},{2,6},{4,0},{6,2},{8,12},{10,14},{12,8},{14,10},{16,20},{18,... | collective-permute-start | bytes 442376 | tf_op jit(solution)/shard_map/ppermute | solution.py:34
  223.2 35.8 %collective-permute-start.33 = (bf16[1840,128]{1,0:T(8,128)(2,1)S(1)}, bf16[1840,128]{1,0:T(8,128)(2,1)S(1)}, u32[]{:S(2)}, u32[]{:S(2)}) collective-permute-start(bf16[1840,128]{1,0:T(8,128)(2,1)S(1)} %get-tuple-element.146), channel_id=1, source_target_pairs={{0,16},{2,18},{4,20},{6,22},{8,24},{10,26},{12,28},{14,30},{16,0},... | collective-permute-start | bytes 1413128 | tf_op jit(solution)/shard_map/ppermute | solution.py:34
  224.9 26.3 %collective-permute-start.30 = (bf16[192,768]{1,0:T(8,128)(2,1)S(1)}, bf16[192,768]{1,0:T(8,128)(2,1)S(1)}, u32[]{:S(2)}, u32[]{:S(2)}) collective-permute-start(bf16[192,768]{1,0:T(8,128)(2,1)S(1)} %get-tuple-element.141), channel_id=1, source_target_pairs={{2,0},{4,2},{6,4},{8,6},{10,8},{12,10},{14,12},{16,14},{18,16},{20... | collective-permute-start | bytes 884744 | tf_op jit(solution)/shard_map/ppermute | solution.py:1477
  228.3 24.7 %collective-permute-start.31 = (bf16[192,768]{1,0:T(8,128)(2,1)S(1)}, bf16[192,768]{1,0:T(8,128)(2,1)S(1)}, u32[]{:S(2)}, u32[]{:S(2)}) collective-permute-start(bf16[192,768]{1,0:T(8,128)(2,1)S(1)} %get-tuple-element.142), channel_id=1, source_target_pairs={{0,2},{2,4},{4,6},{6,8},{8,10},{10,12},{12,14},{14,16},{16,18},{18... | collective-permute-start | bytes 884744 | tf_op jit(solution)/shard_map/ppermute | solution.py:1478
  230.3 29.8 %collective-permute-start.35 = (bf16[192,384]{1,0:T(8,128)(2,1)S(1)}, bf16[192,384]{1,0:T(8,128)(2,1)S(1)}, u32[]{:S(2)}, u32[]{:S(2)}) collective-permute-start(bf16[192,384]{1,0:T(8,128)(2,1)S(1)} %get-tuple-element.149.small_ref), channel_id=1, source_target_pairs={{0,8},{2,10},{4,12},{6,14},{8,0},{10,2},{12,4},{14,6},{16,24},{18,... | collective-permute-start | bytes 442376 | tf_op jit(solution)/shard_map/ppermute | solution.py:34
  255.7 27.4 %collective-permute-start.32 = (bf16[2,128,768]{2,1,0:T(8,128)(2,1)S(1)}, bf16[2,128,768]{2,1,0:T(8,128)(2,1)S(1)}, u32[]{:S(2)}, u32[]{:S(2)}) collective-permute-start(bf16[2,128,768]{2,1,0:T(8,128)(2,1)S(1)} %get-tuple-element.145), channel_id=1, source_target_pairs={{0,1},{1,0},{2,3},{3,2},{4,5},{5,4},{6,7},{7,6},{8,9},{9,8},{10,11... | collective-permute-start | bytes 1179656 | tf_op jit(solution)/shard_map/ppermute | solution.py:1139
  258.8 1.2 copy-start.1
  258.8 1.4 copy-start.3
  258.8 1.7 copy-start.4
  258.9 2.0 copy-start.5
  258.9 2.2 copy-start.6
  258.9 2.5 copy-start.7
  258.9 2.8 copy-start.8
  258.9 2.8 copy-start.9
  258.9 2.9 %copy-start.10 = (f32[169,384]{1,0:T(8,128)S(1)}, f32[169,384]{1,0:T(8,128)}, u32[]{:S(2)}) copy-start(f32[169,384]{1,0:T(8,128)} %refs_9_.1) | copy-start | bytes 778756
  258.9 2.9 %copy-start.12 = (f32[4,768]{1,0:T(4,128)S(1)}, f32[4,768]{1,0:T(4,128)}, u32[]{:S(2)}) copy-start(f32[4,768]{1,0:T(4,128)} %refs_11_.1) | copy-start | bytes 36868
  258.9 2.8 %copy-start.13 = (f32[4,768]{1,0:T(4,128)S(1)}, f32[4,768]{1,0:T(4,128)}, u32[]{:S(2)}) copy-start(f32[4,768]{1,0:T(4,128)} %refs_12_.1) | copy-start | bytes 36868
  259.9 22.6 %collective-permute-start.34 = (bf16[2,2,768]{2,1,0:T(2,128)(2,1)S(1)}, bf16[2,2,768]{2,1,0:T(2,128)(2,1)S(1)}, u32[]{:S(2)}, u32[]{:S(2)}) collective-permute-start(bf16[2,2,768]{2,1,0:T(2,128)(2,1)S(1)} %get-tuple-element.148), channel_id=1, source_target_pairs={{0,1},{1,0},{2,3},{3,2},{4,5},{5,4},{6,7},{7,6},{8,9},{9,8},{10,11... | collective-permute-start | bytes 18440 | tf_op jit(solution)/shard_map/ppermute | solution.py:1139
  (2 other events, 2.3 us)
